TPU v7x, 128 devices: a whole 4x4x4 slice. The times are simulated.
128 devices in a mesh: dp: 8 (over z, core), mp: 16 (over x, y).
Axes of the slice: x: 4, y: 4, z: 4, core: 2. Of those that a mesh axis runs over, the one named last changes fastest.
Arguments:
- grad_query: bfloat16 [2, 64, 294912], P(None, None, ('dp', 'mp')), may hold values from -100 to 100
- grad_key: bfloat16 [2, 64, 65536], P(None, None, ('dp', 'mp')), may hold values from -100 to 100
- weight_query: bfloat16 [2, 64, 294912], P(None, None, ('dp', 'mp')), may hold values from -6 to 6
- weight_key: bfloat16 [2, 64, 65536], P(None, None, ('dp', 'mp')), may hold values from -6 to 6
- moment_query: float32 [256, 294912], P(('dp', 'mp')), may hold values from -6 to 6
- moment_key: float32 [256, 65536], P(('dp', 'mp')), may hold values from -6 to 6
- logit_peak: bfloat16 [8, 2, 64], P('dp'), may hold values from 5 to 400
- owner_table: int32 [64, 2, 1], replicated, may hold values from 0 to 7; in each aligned block of 8 rows (0 to 7, 8 to 15, ..., all dimensions but the last counted through in order) at most 2 rows name the same one
- head_order: int32 [64], replicated, may hold values from 0 to 63, each once
Outputs:
- query_rollout: bfloat16 [2, 64, 294912], P(None, 'mp', 'dp')
- key_rollout: bfloat16 [2, 64, 65536], P(None, 'mp', 'dp')
- query_moment_out: float32 [256, 294912], P(('dp', 'mp'))
- key_moment_out: float32 [256, 65536], P(('dp', 'mp'))
Inputs may be any that keep to these rules, and one draw needn't show every extreme that they name: `owner_table`: among the 8 rows of one rollout rank (positions r * 4 to (r + 1) * 4 - 1, all layers), no dp index is named by more than 2 rows. `head_order`: A permutation of the heads.
All inputs are finite; a program needn't handle non-finite values.
Results may differ from a plain program's by a relative error of at most 0.0045.
Values may be sent and summed in bfloat16 or wider, within the bound.
No kernel may reach another device: no remote copies, remote signals or barrier semaphores. Data moves between devices by JAX's collectives and lax.ppermute only.
A program may use at most 64 MiB of HBM per device.

v0:
```python
import math

import jax
import jax.numpy as jnp
from jax import lax
from jax.sharding import PartitionSpec as P

DN = 128
RQ = 1536
RK = 512
ITERS = 5
DQ = 192


quintic_one = 3.4445
quintic_two = -4.775
quintic_three = 2.0315
momentum_decay = 0.95
step_size = 0.5
logit_cap = 100.0


def owner_slots(owners, rank_count, capacity, owner_count):
    head_count, layer_count = owners.shape
    per_rank = head_count // rank_count
    blocks = owners.reshape(rank_count, per_rank * layer_count)
    matches = (
        blocks[:, :, None] == jnp.arange(owner_count, dtype=jnp.int32)[None, None, :]
    ).astype(jnp.int32)
    earlier = jnp.cumsum(matches, axis=1) - matches
    slot_number = jnp.sum(earlier * matches, axis=2)
    rank_number = jnp.arange(rank_count, dtype=jnp.int32)[:, None]
    device_number = blocks * rank_count + rank_number
    return (device_number * capacity + slot_number).reshape(head_count, layer_count)


def gather_rows(table, index):
    return jnp.take(table, index, axis=0, mode="fill", fill_value=0)


def orthogonal_batch(moment):
    norms = jnp.sqrt(jnp.sum(moment * moment, axis=(1, 2), keepdims=True))
    scaled = (moment / (norms + 1e-07)).astype(jnp.bfloat16)
    for sweep_index in range(ITERS):
        gram_matrix = jnp.einsum(
            "bij,bkj->bik", scaled, scaled, preferred_element_type=jnp.float32
        ).astype(jnp.bfloat16)
        square = jnp.einsum(
            "bij,bjk->bik", gram_matrix, gram_matrix, preferred_element_type=jnp.float32
        )
        mixing = (quintic_two * gram_matrix.astype(jnp.float32) + quintic_three * square).astype(
            jnp.bfloat16
        )
        scaled = (
            quintic_one * scaled.astype(jnp.float32)
            + jnp.einsum("bij,bjk->bik", mixing, scaled, preferred_element_type=jnp.float32)
        ).astype(jnp.bfloat16)
    return scaled


def finish_block(weight_whole, polar_factor, factor, row_count, column_count, nope_rows):
    stepped = weight_whole.astype(jnp.float32).reshape(
        -1, row_count, column_count
    ) - step_size * 0.2 * math.sqrt(max(row_count, column_count)) * polar_factor.astype(jnp.float32)
    row_index = jnp.arange(row_count, dtype=jnp.int32)[None, :, None]
    row_factor = jnp.where(
        row_index < nope_rows, jnp.sqrt(factor)[:, None, None], factor[:, None, None]
    )
    return (
        (stepped * row_factor)
        .astype(jnp.bfloat16)
        .reshape(stepped.shape[0], row_count * column_count)
    )


def body(
    grad_query,
    grad_key,
    weight_query,
    weight_key,
    moment_query,
    moment_key,
    logit_peak,
    owner_table,
    head_order,
):
    owner_count = lax.axis_size("dp")
    rank_count = lax.axis_size("mp")
    device_count = owner_count * rank_count
    layer_count, head_count, piece_query = grad_query.shape
    piece_key = grad_key.shape[2]
    capacity = moment_query.shape[0]
    per_rank = head_count // rank_count
    unit_total = layer_count * head_count
    here_owner = lax.axis_index("dp")
    here_rank = lax.axis_index("mp")
    here_device = here_owner * rank_count + here_rank
    target = owner_slots(owner_table[:, :, 0], rank_count, capacity, owner_count)
    unit_rows = jnp.arange(layer_count, dtype=jnp.int32)[None, :] * head_count + head_order[:, None]
    query_grads = grad_query.reshape(unit_total, piece_query)
    key_grads = grad_key.reshape(unit_total, piece_key)
    peak_table = lax.pmax(logit_peak[0], "dp").astype(jnp.float32).reshape(-1)
    query_pack = jnp.concatenate(
        (query_grads, weight_query.reshape(unit_total, piece_query)), axis=1
    )
    key_pack = jnp.concatenate((key_grads, weight_key.reshape(unit_total, piece_key)), axis=1)
    source_index = (
        jnp.full((device_count * capacity,), unit_total, jnp.int32)
        .at[target.reshape(-1)]
        .set(unit_rows.reshape(-1))
    )
    owned_query, owned_key = (
        lax.all_to_all(
            gather_rows(query_pack, source_index),
            ("dp", "mp"),
            split_axis=0,
            concat_axis=1,
            tiled=True,
        ),
        lax.all_to_all(
            gather_rows(key_pack, source_index),
            ("dp", "mp"),
            split_axis=0,
            concat_axis=1,
            tiled=True,
        ),
    )
    owned_query = owned_query.reshape(capacity, device_count, -1)
    owned_key = owned_key.reshape(capacity, device_count, -1)
    owned_query_grad = owned_query[:, :, :piece_query].reshape(capacity, -1)
    owned_key_grad = owned_key[:, :, :piece_key].reshape(capacity, -1)
    slot_unit = (
        jnp.full((device_count * capacity,), -1, jnp.int32)
        .at[target.reshape(-1)]
        .set(unit_rows.reshape(-1))
    )
    owned_units = lax.dynamic_slice_in_dim(slot_unit, here_device * capacity, capacity)
    filled = owned_units >= 0
    query_next = momentum_decay * moment_query + owned_query_grad.astype(jnp.float32)
    key_next = momentum_decay * moment_key + owned_key_grad.astype(jnp.float32)
    polar_query = orthogonal_batch(query_next.reshape(capacity, DQ, RQ))
    polar_key = orthogonal_batch(key_next.reshape(capacity, DN, RK))
    owned_query_weight = owned_query[:, :, piece_query:].reshape(capacity, -1)
    owned_key_weight = owned_key[:, :, piece_key:].reshape(capacity, -1)
    peak_owned = jnp.sum(
        jnp.where(
            owned_units[:, None] == jnp.arange(unit_total, dtype=jnp.int32)[None, :],
            peak_table[None, :],
            0.0,
        ),
        axis=1,
    )
    factor = jnp.minimum(1.0, logit_cap / jnp.where(filled, peak_owned, logit_cap))
    send_query = finish_block(owned_query_weight, polar_query, factor, DQ, RQ, DN)
    send_key = finish_block(owned_key_weight, polar_key, factor, DN, RK, DN)
    back_query, back_key = (
        lax.all_to_all(send_query, "dp", split_axis=1, concat_axis=0, tiled=True),
        lax.all_to_all(send_key, "dp", split_axis=1, concat_axis=0, tiled=True),
    )
    rank_target = lax.dynamic_slice_in_dim(target, here_rank * per_rank, per_rank, 0).T.reshape(-1)
    local_index = rank_target // capacity // rank_count * capacity + rank_target % capacity
    query_rollout = jnp.take(back_query, local_index, axis=0).reshape(
        layer_count, per_rank, back_query.shape[1]
    )
    key_rollout = jnp.take(back_key, local_index, axis=0).reshape(
        layer_count, per_rank, back_key.shape[1]
    )
    query_moment_out = jnp.where(filled[:, None], query_next, moment_query)
    key_moment_out = jnp.where(filled[:, None], key_next, moment_key)
    return (query_rollout, key_rollout, query_moment_out, key_moment_out)


def solution(mesh):
    placed = (
        P(None, None, ("dp", "mp")),
        P(None, None, ("dp", "mp")),
        P(None, None, ("dp", "mp")),
        P(None, None, ("dp", "mp")),
        P(("dp", "mp"), None),
        P(("dp", "mp"), None),
        P("dp", None, None),
        P(),
        P(),
    )
    return jax.shard_map(
        body,
        mesh=mesh,
        in_specs=placed,
        out_specs=(
            P(None, "mp", "dp"),
            P(None, "mp", "dp"),
            P(("dp", "mp"), None),
            P(("dp", "mp"), None),
        ),
        check_vma=False,
    )
```

profile of v0, /device:TPU:1, one launch (start us, length us, event | category | flops | bytes accessed | tf_op | source)
XLA Modules:
  0.0 154.8 jit_solution(6182314452963181012)
XLA Ops:
  5.8 1.2 gather_fusion.2
  7.2 1.4 broadcast_select_fusion.2
  8.6 11.5 %all-to-all-start.2 = ((bf16[128,2,1024]{2,1,0:T(2,128)(2,1)}), bf16[128,2,1024]{2,1,0:T(2,128)(2,1)S(1)}, u32[]{:S(2)}, u32[]{:S(2)}) async-start(bf16[128,2,1024]{2,1,0:T(2,128)(2,1)} %broadcast_select_fusion.2), calls=%async_computation.2 | async-start | bytes 1048576 | tf_op jit(solution)/shard_map/all_to_all | solution.py:120
  20.2 3.4 %gather_fusion = bf16[256,4608]{1,0:T(8,128)(2,1)} fusion(bf16[128,4608]{1,0:T(8,128)(2,1)S(1)} %pad_maximum_fusion, s32[1024]{0:T(1024)S(1)} %pad_clamp_fusion.1), kind=kCustom, calls=%fused_computation | custom fusion | bytes 4719616 | tf_op jit(solution)/shard_map/jit(_take)/gather | solution.py:38
  23.6 2.9 %gather.25 = bf16[128,2,4608]{2,1,0:T(2,128)(2,1)S(1)} reshape(bf16[256,4608]{1,0:T(8,128)(2,1)} %gather_fusion) | data formatting | bytes 4718592 | tf_op jit(solution)/shard_map/jit(_take)/gather | solution.py:38
  27.6 12.8 %pmax.7 = bf16[128]{0:T(256)(128)(2,1)S(1)} all-reduce(bf16[128]{0:T(256)(128)(2,1)S(1)} %broadcast_in_dim.159), channel_id=1, replica_groups=mesh['dp'=8,'mp'=16] {'dp'}, use_global_device_ids=true, to_apply=%region_5.6 | all-reduce | flops 128 | bytes 512 | tf_op jit(solution)/shard_map/pmax | solution.py:102
  41.4 2.3 %broadcast_select_fusion.4 = (f32[2,65536]{1,0:T(2,128)}, f32[2,65536]{1,0:T(2,128)S(1)}) fusion(f32[2,65536]{1,0:T(2,128)} %param.14, pred[2]{0:T(512)(128)(4,1)S(1)} %get-tuple-element.8, f32[2,65536]{1,0:T(2,128)S(1)} %bitcast.95), kind=kLoop, calls=%fused_computation.96 | loop fusion | flops 393216 | bytes 2097154 | tf_op jit(solution)/shard_map/jit(_where)/select_n | solution.py:169
  48.6 6.5 %all-to-all-start.3 = ((bf16[2,8,8192]{2,0,1:T(2,128)(2,1)}), bf16[2,8,8192]{2,0,1:T(2,128)(2,1)S(1)}, u32[]{:S(2)}, u32[]{:S(2)}) async-start(bf16[2,8,8192]{2,0,1:T(2,128)(2,1)} %copy.54), calls=%async_computation.3 | async-start | bytes 524288 | tf_op jit(solution)/shard_map/all_to_all | solution.py:158
  55.1 3.5 %broadcast_select_fusion = bf16[128,2,4608]{2,1,0:T(2,128)(2,1)} fusion(bf16[128,2,4608]{2,1,0:T(2,128)(2,1)S(1)} %gather.25, pred[128,2]{1,0:T(8,128)(4,1)S(1)} %broadcast_in_dim.153), kind=kLoop, calls=%fused_computation.6 | loop fusion | flops 1179648 | bytes 4718848 | tf_op jit(solution)/shard_map/jit(_take)/select_n | solution.py:38
  58.6 3.0 %all-to-all-done.3 = bf16[2,8,8192]{2,0,1:T(2,128)(2,1)S(1)} async-done(((bf16[2,8,8192]{2,0,1:T(2,128)(2,1)}), bf16[2,8,8192]{2,0,1:T(2,128)(2,1)S(1)}, u32[]{:S(2)}, u32[]{:S(2)}) %all-to-all-start.3) | async-done | bytes 262176 | tf_op jit(solution)/shard_map/all_to_all | solution.py:158
  61.6 8.0 %all-to-all-start = ((bf16[128,2,4608]{2,1,0:T(2,128)(2,1)}), bf16[128,2,4608]{2,1,0:T(2,128)(2,1)S(1)}, u32[]{:S(2)}, u32[]{:S(2)}) async-start(bf16[128,2,4608]{2,1,0:T(2,128)(2,1)} %broadcast_select_fusion), calls=%async_computation | async-start | bytes 4718592 | tf_op jit(solution)/shard_map/all_to_all | solution.py:113
  71.7 30.6 %all-to-all-done = bf16[128,2,4608]{2,1,0:T(2,128)(2,1)S(1)} async-done(((bf16[128,2,4608]{2,1,0:T(2,128)(2,1)}), bf16[128,2,4608]{2,1,0:T(2,128)(2,1)S(1)}, u32[]{:S(2)}, u32[]{:S(2)}) %all-to-all-start) | async-done | bytes 2359328 | tf_op jit(solution)/shard_map/all_to_all | solution.py:113
  102.5 1.8 %convert_bitcast_fusion = (f32[1,2,128,2304]{3,2,1,0:T(8,128)S(1)}, f32[2,128,2304]{2,1,0:T(8,128)}) fusion(bf16[2,128,4608]{2,1,0:T(8,128)(2,1)S(1)} %bitcast.91), kind=kLoop, calls=%fused_computation.25 | loop fusion | flops 1179648 | bytes 7077888
  104.3 3.0 %reshape.447 = f32[2,192,1536]{2,1,0:T(8,128)} reshape(f32[2,128,2304]{2,1,0:T(8,128)} %get-tuple-element.15) | data formatting | bytes 4718592 | tf_op jit(solution)/shard_map/convert_element_type | solution.py:62
  107.3 1.8 %copy.55 = f32[1,2,128,2304]{3,1,2,0:T(2,128)S(1)} copy(f32[1,2,128,2304]{3,2,1,0:T(8,128)S(1)} %get-tuple-element.14) | data formatting | bytes 4718592
  109.2 3.2 %broadcast_select_fusion.1 = (f32[2,294912]{1,0:T(2,128)}, f32[2,294912]{1,0:T(2,128)S(1)}) fusion(f32[2,294912]{1,0:T(2,128)S(1)} %copy-done.1, pred[2]{0:T(512)(128)(4,1)S(1)} %get-tuple-element.8, f32[2,294912]{1,0:T(2,128)S(1)} %bitcast.92), kind=kLoop, calls=%fused_computation.28 | loop fusion | flops 1769472 | bytes 9437186 | tf_op jit(solution)/shard_map/jit(_where)/select_n | solution.py:168
  112.4 2.6 %multiply_reduce_fusion = f32[2]{0:T(128)S(1)} fusion(f32[2,294912]{1,0:T(2,128)S(1)} %get-tuple-element.7), kind=kLoop, calls=%fused_computation.26 | loop fusion | flops 1179646 | bytes 2359304 | tf_op jit(solution)/shard_map/reduce_sum | solution.py:42
  118.7 1.2 convolution_convert_fusion.1
  119.9 2.9 %fusion.3 = bf16[2,192,1536]{2,1,0:T(8,128)(2,1)} fusion(bf16[2,192,1536]{2,1,0:T(8,128)(2,1)S(1)} %fusion.2, bf16[2,192,192]{2,1,0:T(8,128)(2,1)} %convolution_convert_fusion.1), kind=kOutput, calls=%fused_computation.15 | convolution fusion | flops 257531904 | bytes 2506752 | tf_op jit(solution)/shard_map/bij,bjk->bik/dot_general | solution.py:56
  122.8 2.8 %convolution_convert_fusion = bf16[2,192,192]{2,1,0:T(8,128)(2,1)} fusion(bf16[2,192,1536]{2,1,0:T(8,128)(2,1)} %fusion.3), kind=kOutput, calls=%fused_computation.61 | convolution fusion | flops 226566144 | bytes 1327104 | tf_op jit(solution)/shard_map/bij,bkj->bik/dot_general | solution.py:45
  125.6 2.6 %fusion.9 = bf16[2,192,1536]{2,1,0:T(8,128)(2,1)S(1)} fusion(f32[2,192,1536]{2,1,0:T(8,128)S(1)} %copy-done, bf16[2,192,1536]{2,1,0:T(8,128)(2,1)} %fusion.3, f32[2,192]{1,0:T(2,128)S(1)} %broadcast_select_fusion.6, bf16[2,192,192]{2,1,0:T(8,128)(2,1)} %convolution_convert_fusion), kind=kOutput, calls=%fused_computation.21 | convolution fusion | flops 260481024 | bytes 4867584 | tf_op jit(solution)/shard_map/bij,bjk->bik/dot_general | solution.py:56
  128.8 2.2 %copy.52 = bf16[2,8,36864]{2,0,1:T(2,128)(2,1)} copy(bf16[2,8,36864]{2,1,0:T(8,128)(2,1)S(1)} %all_to_all.50) | data formatting | bytes 2359296 | tf_op jit(solution)/shard_map/all_to_all | solution.py:157
  131.1 4.4 %all-to-all-start.1 = ((bf16[2,8,36864]{2,0,1:T(2,128)(2,1)}), bf16[2,8,36864]{2,0,1:T(2,128)(2,1)S(1)}, u32[]{:S(2)}, u32[]{:S(2)}) async-start(bf16[2,8,36864]{2,0,1:T(2,128)(2,1)} %copy.52), calls=%async_computation.1 | async-start | bytes 2359296 | tf_op jit(solution)/shard_map/all_to_all | solution.py:157
  136.3 15.7 %all-to-all-done.1 = bf16[2,8,36864]{2,0,1:T(2,128)(2,1)S(1)} async-done(((bf16[2,8,36864]{2,0,1:T(2,128)(2,1)}), bf16[2,8,36864]{2,0,1:T(2,128)(2,1)S(1)}, u32[]{:S(2)}, u32[]{:S(2)}) %all-to-all-start.1) | async-done | bytes 1179680 | tf_op jit(solution)/shard_map/all_to_all | solution.py:157
  (91 shorter events, 22.3 us)
Async XLA Ops:
  7.0 13.1 %copy-start.2 = (bf16[2,64,2304]{2,1,0:T(8,128)(2,1)S(1)}, bf16[2,64,2304]{2,1,0:T(8,128)(2,1)}, u32[]{:S(2)}) copy-start(bf16[2,64,2304]{2,1,0:T(8,128)(2,1)} %param.11) | copy-start | bytes 1769476
  7.0 13.1 %copy-start.3 = (bf16[2,64,2304]{2,1,0:T(8,128)(2,1)S(1)}, bf16[2,64,2304]{2,1,0:T(8,128)(2,1)}, u32[]{:S(2)}) copy-start(bf16[2,64,2304]{2,1,0:T(8,128)(2,1)} %param.9) | copy-start | bytes 1769476
  8.6 32.2 %all-to-all-start.2 = ((bf16[128,2,1024]{2,1,0:T(2,128)(2,1)}), bf16[128,2,1024]{2,1,0:T(2,128)(2,1)S(1)}, u32[]{:S(2)}, u32[]{:S(2)}) async-start(bf16[128,2,1024]{2,1,0:T(2,128)(2,1)} %broadcast_select_fusion.2), calls=%async_computation.2 | async-start | bytes 1048576 | tf_op jit(solution)/shard_map/all_to_all | solution.py:120
  23.6 3.9 %copy-start.5 = (bf16[1,2,64]{2,1,0:T(2,128)(2,1)S(1)}, bf16[1,2,64]{2,1,0:T(2,128)(2,1)}, u32[]{:S(2)}) copy-start(bf16[1,2,64]{2,1,0:T(2,128)(2,1)} %param.15) | copy-start | bytes 772
  48.6 13.0 %all-to-all-start.3 = ((bf16[2,8,8192]{2,0,1:T(2,128)(2,1)}), bf16[2,8,8192]{2,0,1:T(2,128)(2,1)S(1)}, u32[]{:S(2)}, u32[]{:S(2)}) async-start(bf16[2,8,8192]{2,0,1:T(2,128)(2,1)} %copy.54), calls=%async_computation.3 | async-start | bytes 524288 | tf_op jit(solution)/shard_map/all_to_all | solution.py:158
  61.6 40.6 %all-to-all-start = ((bf16[128,2,4608]{2,1,0:T(2,128)(2,1)}), bf16[128,2,4608]{2,1,0:T(2,128)(2,1)S(1)}, u32[]{:S(2)}, u32[]{:S(2)}) async-start(bf16[128,2,4608]{2,1,0:T(2,128)(2,1)} %broadcast_select_fusion), calls=%async_computation | async-start | bytes 4718592 | tf_op jit(solution)/shard_map/all_to_all | solution.py:113
  107.3 1.8 %copy-start.1 = (f32[2,294912]{1,0:T(2,128)S(1)}, f32[2,294912]{1,0:T(2,128)}, u32[]{:S(2)}) copy-start(f32[2,294912]{1,0:T(2,128)} %param.13) | copy-start | bytes 7077892
  119.9 5.7 %copy-start = (f32[2,192,1536]{2,1,0:T(8,128)S(1)}, f32[2,192,1536]{2,1,0:T(8,128)}, u32[]{:S(2)}) copy-start(f32[2,192,1536]{2,1,0:T(8,128)} %reshape.447) | copy-start | bytes 7077892
  128.8 6.7 %copy-start.4 = (bf16[2,4,8192]{2,1,0:T(4,128)(2,1)S(1)}, bf16[2,4,8192]{2,1,0:T(4,128)(2,1)}, u32[]{:S(2)}) copy-start(bf16[2,4,8192]{2,1,0:T(4,128)(2,1)} %gather.31) | copy-start | bytes 393220
  131.1 21.0 %all-to-all-start.1 = ((bf16[2,8,36864]{2,0,1:T(2,128)(2,1)}), bf16[2,8,36864]{2,0,1:T(2,128)(2,1)S(1)}, u32[]{:S(2)}, u32[]{:S(2)}) async-start(bf16[2,8,36864]{2,0,1:T(2,128)(2,1)} %copy.52), calls=%async_computation.1 | async-start | bytes 2359296 | tf_op jit(solution)/shard_map/all_to_all | solution.py:157
where the time goes:
time: 156 us; the launch traced here: 155 us
  waiting for transfers between devices  49.3 us (32%)
  starting transfers between devices  30.5 us (20%)
  local copies, waits for them, and re-layouts  24.3 us (16%)
  other arithmetic  21.2 us (14%)
  matrix products  15.6 us (10%)
  blocking collectives  12.8 us (8%)
    all_to_all x1, waiting for transfers between devices, body(): lax.all_to_all(gather_rows(query_pack, source_index), ('dp', 'mp'), split...  30.6 us
    all_to_all x1, waiting for transfers between devices, body(): lax.all_to_all(send_query, 'dp', split_axis=1, concat_axis=0, tiled=True)  15.7 us
    pmax x1, blocking collectives, body(): peak_table = lax.pmax(logit_peak[0], 'dp').astype(jnp.float32).reshape(-1)  12.8 us
    all_to_all x1, starting transfers between devices, body(): lax.all_to_all(gather_rows(key_pack, source_index), ('dp', 'mp'), split_a...  11.5 us
    dot_general x10, matrix products, orthogonal_batch(): jnp.einsum('bij,bjk->bik', mixing, scaled, preferred_element_type=jnp.flo...  9.06 us
    all_to_all x1, starting transfers between devices, body(): lax.all_to_all(gather_rows(query_pack, source_index), ('dp', 'mp'), split...  8.04 us
    gather x4, local copies, waits for them, and re-layouts, gather_rows(): return jnp.take(table, index, axis=0, mode='fill', fill_value=0)  7.63 us
    all_to_all x1, starting transfers between devices, body(): lax.all_to_all(send_key, 'dp', split_axis=1, concat_axis=0, tiled=True)  6.52 us
  transfers between devices with their start and end apart: 4, of which 3 were waited for; matrix products, arithmetic and copies ran while one was open for 9% of the time, Pallas kernels for 0%

commit v1 on v0

v1 whole, which is shorter than its diff:
```python
import functools
import math

import jax
import jax.numpy as jnp
from jax import lax
from jax.experimental import pallas as pl
from jax.experimental.pallas import tpu as pltpu
from jax.sharding import PartitionSpec as P

DN = 128
RQ = 1536
RK = 512
ITERS = 5
DQ = 192
LANE = 128

quintic_one = 3.4445
quintic_two = -4.775
quintic_three = 2.0315
momentum_decay = 0.95
step_size = 0.5
logit_cap = 100.0

f32 = jnp.float32
bf16 = jnp.bfloat16
VMEM = pl.BlockSpec(memory_space=pltpu.VMEM)
SMEM = pl.BlockSpec(memory_space=pltpu.SMEM)


def iota(shape, dim):
    return lax.broadcasted_iota(jnp.int32, shape, dim)


def dot(a, b, dims=((1,), (0,))):
    return lax.dot_general(a, b, (dims, ((), ())), preferred_element_type=f32)


def head_matrix(head_ref, heads):
    return (iota((heads, heads), 0) == head_ref[...]).astype(bf16)


def pack_grads_kernel(owner_ref, head_ref, gq_ref, gk_ref, out_ref, stage, *, ranks, owners, slots):
    heads, layers = owner_ref.shape
    devices = ranks * owners
    per_rank = heads // ranks
    tq = gq_ref.shape[1] // LANE
    tk = gk_ref.shape[1] // LANE
    rows = (tq + tk) * slots
    by_row = owner_ref[...].astype(f32)
    eye = (iota((heads, heads), 0) == iota((heads, heads), 1)).astype(f32)
    by_lane = dot(by_row, eye, ((0,), (0,)))
    other, mine = iota((heads, heads), 0), iota((heads, heads), 1)
    same_rank = (other // per_rank) == (mine // per_rank)
    heads_of = head_matrix(head_ref, heads)
    lane_rank = iota((1, heads), 1) // per_rank
    picks = [[None] * layers for _ in range(slots)]
    for layer in range(layers):
        owner = by_lane[layer : layer + 1, :]
        earlier = jnp.zeros((1, heads), f32)
        for before in range(layers):
            ahead = (other <= mine) if before < layer else (other < mine)
            hit = same_rank & ahead & (by_row[:, before : before + 1] == owner)
            earlier += jnp.sum(hit.astype(f32), axis=0, keepdims=True)
        target = (owner.astype(jnp.int32) * ranks + lane_rank) * slots + earlier.astype(jnp.int32)
        for slot in range(slots):
            chosen = (iota((devices, heads), 0) * slots + slot == target).astype(bf16)
            picks[slot][layer] = dot(chosen, heads_of, ((1,), (1,))).astype(bf16)
    for slot in range(slots):
        pick = jnp.concatenate(picks[slot], axis=1)
        for ref, tiles, base in ((gq_ref, tq, 0), (gk_ref, tk, tq)):
            value = dot(pick, ref[...])
            for tile in range(tiles):
                stage[pl.ds((base + tile) * slots + slot, devices, stride=rows), :] = value[
                    :, tile * LANE : (tile + 1) * LANE
                ]
    out_ref[...] = stage[...].astype(bf16)


def pack_weights_kernel(head_ref, wq_ref, wk_ref, out_ref, stage, *, ranks):
    layers, heads, _ = wq_ref.shape
    per_rank = heads // ranks
    tq = wq_ref.shape[2] // LANE
    tk = wk_ref.shape[2] // LANE
    rows = layers * (tq + tk) * per_rank
    heads_of = head_matrix(head_ref, heads)
    place, position = iota((heads, heads), 0), iota((heads, heads), 1)
    order = (position == (place % ranks) * per_rank + place // ranks).astype(bf16)
    pick = dot(order, heads_of, ((1,), (1,))).astype(bf16)
    for layer in range(layers):
        for ref, tiles, base in ((wq_ref, tq, 0), (wk_ref, tk, tq)):
            value = dot(pick, ref[layer])
            for tile in range(tiles):
                first = (layer * (tq + tk) + base + tile) * per_rank
                for place_in in range(per_rank):
                    stage[pl.ds(first + place_in, ranks, stride=rows), :] = value[
                        place_in * ranks : (place_in + 1) * ranks, tile * LANE : (tile + 1) * LANE
                    ]
    out_ref[...] = stage[...].astype(bf16)


def polar_kernel(
    owner_ref, recv_ref, mq_ref, mk_ref, peak_ref, out_ref, mq_out, mk_out, flat_q, flat_k, *, ranks, owners, slots
):
    here_owner = lax.axis_index("dp")
    here_rank = lax.axis_index("mp")
    devices = ranks * owners
    unit_rows = owner_ref.shape[0] // ranks
    held = jnp.int32(0)
    for unit in range(unit_rows):
        held += (owner_ref[here_rank * unit_rows + unit] == here_owner).astype(jnp.int32)
    sub = iota((8, LANE), 0)
    filled = (sub % slots) < held
    low = sub < 4
    tq = DQ * RQ // LANE // devices * slots
    tk = DN * RK // LANE // devices * slots
    rows = tq + tk

    def tile_of(value, index):
        return value[index * 8 : (index + 1) * 8, :]

    def step(quad, carry):
        block = recv_ref[pl.ds(pl.multiple_of(quad * 4 * rows, 16), 4 * rows), :].astype(f32)
        for pair in range(2):
            g = [tile_of(block, pair * 11 + j) for j in range(11)]
            query = g[0:4] + [jnp.where(low, g[4], g[5])] + g[6:10]
            key = [pltpu.roll(jnp.where(low, g[5], g[4]), 4, 0), g[10]]
            for grads, ref, out, count in ((query, mq_ref, mq_out, 9), (key, mk_ref, mk_out, 2)):
                base = pl.multiple_of((quad * 2 + pair) * count * 8, 8)
                for j in range(count):
                    at = pl.ds(pl.multiple_of(base + j * 8, 8), 8)
                    old = ref[at, :]
                    out[at, :] = jnp.where(filled, momentum_decay * old + grads[j], old)
        return carry

    lax.fori_loop(0, devices // 4, step, 0)

    chains = []
    for slot in range(slots):
        for ref, height, width in ((mq_out, DQ, RQ), (mk_out, DN, RK)):
            tiles = width // LANE
            parts = [ref[pl.ds(tile * slots + slot, height, stride=tiles * slots), :] for tile in range(tiles)]
            total = jnp.zeros((height, LANE), f32)
            for part in parts:
                total += part * part
            norm = jnp.sqrt(jnp.sum(total, keepdims=True))
            scale = 1.0 / (norm + 1e-07)
            chains.append(jnp.concatenate([(part * scale).astype(bf16) for part in parts], axis=1))
    for _ in range(ITERS):
        grams = [dot(x, x, ((1,), (1,))).astype(bf16) for x in chains]
        squares = [dot(a, a) for a in grams]
        mixings = [
            (quintic_two * a.astype(f32) + quintic_three * s).astype(bf16) for a, s in zip(grams, squares)
        ]
        products = [dot(b, x) for b, x in zip(mixings, chains)]
        chains = [(quintic_one * x.astype(f32) + y).astype(bf16) for x, y in zip(chains, products)]
    fq = DQ * RQ // LANE // owners
    fk = DN * RK // LANE // owners
    for slot in range(slots):
        for x, flat, height, width in (
            (chains[slot * 2], flat_q, DQ, RQ),
            (chains[slot * 2 + 1], flat_k, DN, RK),
        ):
            tiles = width // LANE
            for tile in range(tiles):
                flat[pl.ds(tile, height, stride=tiles), :] = x[:, tile * LANE : (tile + 1) * LANE].astype(f32)
        for owner in range(owners):
            at = slot * (fq + fk)
            out_ref[owner, at : at + fq, :] = flat_q[owner * fq : (owner + 1) * fq, :].astype(bf16)
            out_ref[owner, at + fq : at + fq + fk, :] = flat_k[owner * fk : (owner + 1) * fk, :].astype(bf16)
    peaks = jnp.concatenate([peak_ref[...].astype(f32), jnp.zeros((14, 64), f32)], axis=0)
    peaks = jnp.concatenate([peaks, jnp.zeros((16, 64), f32)], axis=1).astype(bf16)
    for owner in range(owners):
        out_ref[owner, slots * (fq + fk) :, :] = peaks


def finish_kernel(owner_ref, head_ref, polar_ref, weight_ref, q_out, k_out, spread_q, spread_k, *, ranks, owners, slots):
    here_owner = lax.axis_index("dp")
    here_rank = lax.axis_index("mp")
    heads = head_ref.shape[0]
    unit_rows = owner_ref.shape[0] // ranks
    per_rank = heads // ranks
    layers = unit_rows // per_rank
    fq = DQ * RQ // LANE // owners
    fk = DN * RK // LANE // owners
    peaks = polar_ref[0, slots * (fq + fk) :, :].astype(f32)
    for owner in range(1, owners):
        peaks = jnp.maximum(peaks, polar_ref[owner, slots * (fq + fk) :, :].astype(f32))
    names = [owner_ref[here_rank * unit_rows + unit] for unit in range(unit_rows)]
    sub, lane = iota((8, LANE), 0), iota((8, LANE), 1)
    head_of = jnp.zeros((8, LANE), jnp.int32)
    for place in range(per_rank):
        head_of = jnp.where(sub % per_rank == place, head_ref[here_rank * per_rank + place], head_of)
    row_height = RQ // LANE
    for layer in range(layers):
        peak = jnp.sum(
            jnp.where(head_of == lane, jnp.broadcast_to(peaks[layer : layer + 1, :], (8, LANE)), 0.0),
            axis=1,
            keepdims=True,
        )
        factor = jnp.broadcast_to(jnp.minimum(1.0, logit_cap / peak), (8, LANE))
        root = jnp.sqrt(factor)
        for place in range(per_rank):
            unit = place * layers + layer
            earlier = jnp.int32(0)
            for before in range(unit):
                earlier += (names[before] == names[unit]).astype(jnp.int32)
            start = pl.multiple_of(earlier * (fq + fk), 16)
            block = polar_ref[names[unit], pl.ds(start, fq + fk), :].astype(f32)
            spread_q[pl.ds(layer * fq * per_rank + place, fq, stride=per_rank), :] = block[:fq]
            spread_k[pl.ds(layer * fk * per_rank + place, fk, stride=per_rank), :] = block[fq:]
        sq = fq // ranks * per_rank
        sk = fk // ranks * per_rank
        cq = step_size * 0.2 * math.sqrt(max(DQ, RQ))
        ck = step_size * 0.2 * math.sqrt(max(DN, RK))
        span = sq + sk
        for pair in range(ranks // 2):
            held = [
                weight_ref[2 * pair + j].astype(f32)[layer * span : (layer + 1) * span] for j in range(2)
            ]
            wq = jnp.concatenate([x[:sq] for x in held], axis=0)
            wk = jnp.concatenate([x[sq:] for x in held], axis=0)
            at = layer * fq * per_rank + pair * 2 * sq
            stepped = wq - cq * spread_q[at : at + 2 * sq, :]
            tiles = []
            for tile in range(2 * sq // 8):
                row = here_owner * (DQ // owners) + (pair * 2 * sq + tile * 8) // per_rank // row_height
                tiles.append(stepped[tile * 8 : tile * 8 + 8] * jnp.where(row < DN, root, factor))
            q_out[at : at + 2 * sq, :] = jnp.concatenate(tiles, axis=0).astype(bf16)
            at = layer * fk * per_rank + pair * 2 * sk
            stepped = wk - ck * spread_k[at : at + 2 * sk, :]
            tiles = [stepped[tile * 8 : tile * 8 + 8] * root for tile in range(2 * sk // 8)]
            k_out[at : at + 2 * sk, :] = jnp.concatenate(tiles, axis=0).astype(bf16)


def call(kernel, name, out_shape, in_specs, scratch, flops, moved):
    return pl.pallas_call(
        kernel,
        name=name,
        out_shape=out_shape,
        in_specs=in_specs,
        out_specs=jax.tree.map(lambda _: VMEM, out_shape),
        scratch_shapes=scratch,
        compiler_params=pltpu.CompilerParams(vmem_limit_bytes=40 * 2**20),
        cost_estimate=pl.CostEstimate(flops=flops, bytes_accessed=moved, transcendentals=0),
    )


def to_rows(array):
    slots, width = array.shape
    return array.reshape(slots, width // LANE, LANE).transpose(1, 0, 2).reshape(-1, LANE)


def from_rows(rows, slots):
    return rows.reshape(-1, slots, LANE).transpose(1, 0, 2).reshape(slots, -1)


def body(
    grad_query,
    grad_key,
    weight_query,
    weight_key,
    moment_query,
    moment_key,
    logit_peak,
    owner_table,
    head_order,
):
    owners = lax.axis_size("dp")
    ranks = lax.axis_size("mp")
    devices = owners * ranks
    layers, heads, piece_q = grad_query.shape
    piece_k = grad_key.shape[2]
    slots = moment_query.shape[0]
    per_rank = heads // ranks
    tiles = (piece_q + piece_k) // LANE
    kw = dict(ranks=ranks, owners=owners, slots=slots)
    shape = jax.ShapeDtypeStruct
    owner_2d = owner_table[:, :, 0]
    owner_1d = owner_2d.reshape(-1)
    head_row = head_order.reshape(1, heads)

    packed = call(
        functools.partial(pack_grads_kernel, **kw),
        "pack_grads",
        shape((devices * tiles * slots, LANE), bf16),
        [VMEM] * 4,
        [pltpu.VMEM((devices * tiles * slots, LANE), f32)],
        2 * 256 * 128 * 2816,
        3 * 2**20,
    )(
        owner_2d,
        head_row,
        grad_query.reshape(layers * heads, piece_q),
        grad_key.reshape(layers * heads, piece_k),
    )
    packed = packed.reshape(devices, tiles, slots, LANE).transpose(0, 2, 1, 3).reshape(devices, slots, -1)
    owned = lax.all_to_all(packed, ("dp", "mp"), split_axis=0, concat_axis=0, tiled=True)
    owned = owned.reshape(devices, slots, tiles, LANE).transpose(0, 2, 1, 3).reshape(-1, LANE)

    wrows = layers * tiles * per_rank
    packed_w = call(
        functools.partial(pack_weights_kernel, ranks=ranks),
        "pack_weights",
        shape((ranks * wrows, LANE), bf16),
        [VMEM] * 3,
        [pltpu.VMEM((ranks * wrows, LANE), f32)],
        2 * 128 * 64 * 2816,
        3 * 2**20,
    )(head_row, weight_query, weight_key)
    weights = lax.all_to_all(
        packed_w.reshape(ranks, wrows, LANE), "mp", split_axis=0, concat_axis=0, tiled=True
    )

    fq = DQ * RQ // LANE
    fk = DN * RK // LANE
    send_rows = slots * (fq + fk) // owners + 16
    polar, next_q, next_k = call(
        functools.partial(polar_kernel, **kw),
        "polar",
        (
            shape((owners, send_rows, LANE), bf16),
            shape((fq * slots, LANE), f32),
            shape((fk * slots, LANE), f32),
        ),
        [SMEM, VMEM, VMEM, VMEM, VMEM],
        [pltpu.VMEM((fq, LANE), f32), pltpu.VMEM((fk, LANE), f32)],
        4 * 10**9,
        8 * 2**20,
    )(owner_1d, owned, to_rows(moment_query), to_rows(moment_key), logit_peak[0])
    back = lax.all_to_all(polar, "dp", split_axis=0, concat_axis=0, tiled=True)

    oq = layers * per_rank * fq // owners
    ok = layers * per_rank * fk // owners
    new_q, new_k = call(
        functools.partial(finish_kernel, **kw),
        "finish",
        (shape((oq, LANE), bf16), shape((ok, LANE), bf16)),
        [SMEM, SMEM, VMEM, VMEM],
        [pltpu.VMEM((oq, LANE), f32), pltpu.VMEM((ok, LANE), f32)],
        10**7,
        4 * 2**20,
    )(owner_1d, head_order, back, weights)

    def rollout(rows):
        rows = rows.reshape(layers, -1, per_rank, LANE).transpose(0, 2, 1, 3)
        return rows.reshape(layers, per_rank, -1)

    return rollout(new_q), rollout(new_k), from_rows(next_q, slots), from_rows(next_k, slots)


def solution(mesh):
    placed = (
        P(None, None, ("dp", "mp")),
        P(None, None, ("dp", "mp")),
        P(None, None, ("dp", "mp")),
        P(None, None, ("dp", "mp")),
        P(("dp", "mp"), None),
        P(("dp", "mp"), None),
        P("dp", None, None),
        P(),
        P(),
    )
    return jax.shard_map(
        body,
        mesh=mesh,
        in_specs=placed,
        out_specs=(
            P(None, "mp", "dp"),
            P(None, "mp", "dp"),
            P(("dp", "mp"), None),
            P(("dp", "mp"), None),
        ),
        check_vma=False,
    )
```

time: 156 us -> 83 us (0.53)
  waiting for transfers between devices: 49.3 us -> 23 us
  other arithmetic: 21.2 us -> 0 us
  local copies, waits for them, and re-layouts: 24.3 us -> 6.68 us
  matrix products: 15.6 us -> 0 us
  starting transfers between devices: 30.5 us -> 15.1 us
  Pallas kernels: 0 us -> 12.6 us
  blocking collectives: 12.8 us -> 24.5 us
    all_to_all x4 -> x2, waiting for transfers between devices: 49.3 us -> 23 us  [the longest x1 21 us: body(): lax.all_to_all(packed, ('dp', 'mp'), split_axis=0, concat_axis=0, tiled=T...]
    all_to_all x0 -> x1, blocking collectives: none -> 24.5 us  [body(): back = lax.all_to_all(polar, 'dp', split_axis=0, concat_axis=0, tiled=True)]
    dot_general x20 -> x0, matrix products: 15.6 us -> none  [the longest x10 9.06 us: orthogonal_batch(): jnp.einsum('bij,bjk->bik', mixing, scaled, preferred_element_type=jnp.flo...]
    all_to_all x4 -> x2, starting transfers between devices: 30.5 us -> 15.1 us  [the longest x1 11.5 us: body(): lax.all_to_all(packed, ('dp', 'mp'), split_axis=0, concat_axis=0, tiled=T...]
    pmax x1 -> x0, blocking collectives: 12.8 us -> none  [body(): peak_table = lax.pmax(logit_peak[0], 'dp').astype(jnp.float32).reshape(-1)]
    pallas_call x0 -> x4, Pallas kernels: none -> 12.6 us  [the longest x1 6.96 us: body(): call(functools.partial(polar_kernel, **kw), 'polar', (shape((owners, send...]
    select_n x11 -> x0, other arithmetic: 12.5 us -> none  [the longest x3 4.89 us: gather_rows(): return jnp.take(table, index, axis=0, mode='fill', fill_value=0)]
    gather x8 -> x0, local copies, waits for them, and re-layouts: 10.1 us -> none  [the longest x4 7.63 us: gather_rows(): return jnp.take(table, index, axis=0, mode='fill', fill_value=0)]
  transfers between devices with their start and end apart: 4 -> 2, of which waited for: 3 -> 2; matrix products, arithmetic and copies ran while one was open for 9% -> 0% of each run, Pallas kernels for 0% -> 10%
where the time goes in v1:
time: 83 us; the launch traced here: 82.6 us
  blocking collectives  24.5 us (30%)
  waiting for transfers between devices  23 us (28%)
  starting transfers between devices  15.1 us (18%)
  Pallas kernels  12.6 us (15%)
  local copies, waits for them, and re-layouts  6.68 us (8%)
    all_to_all x1, blocking collectives, body(): back = lax.all_to_all(polar, 'dp', split_axis=0, concat_axis=0, tiled=True)  24.5 us
    all_to_all x1, waiting for transfers between devices, body(): lax.all_to_all(packed, ('dp', 'mp'), split_axis=0, concat_axis=0, tiled=T...  21 us
    all_to_all x1, starting transfers between devices, body(): lax.all_to_all(packed, ('dp', 'mp'), split_axis=0, concat_axis=0, tiled=T...  11.5 us
    pallas_call x1, Pallas kernels, body(): call(functools.partial(polar_kernel, **kw), 'polar', (shape((owners, send...  6.96 us
    unnamed x25, local copies, waits for them, and re-layouts  5.77 us
    all_to_all x1, starting transfers between devices, body(): lax.all_to_all(packed_w.reshape(ranks, wrows, LANE), 'mp', split_axis=0,...  3.6 us
    pallas_call x1, Pallas kernels, body(): call(functools.partial(pack_grads_kernel, **kw), 'pack_grads', shape((dev...  2.13 us
    all_to_all x1, waiting for transfers between devices, body(): lax.all_to_all(packed_w.reshape(ranks, wrows, LANE), 'mp', split_axis=0,...  1.97 us
  transfers between devices with their start and end apart: 2, of which 2 were waited for; matrix products, arithmetic and copies ran while one was open for 0% of the time, Pallas kernels for 10%

profile of v1, /device:TPU:1, one launch (start us, length us, event | category | flops | bytes accessed | tf_op | source)
XLA Modules:
  0.0 82.6 jit_solution(15421680201327251557)
XLA Ops:
  0.6 0.8 copy.22.owner_ref
  1.4 1.1 %copy-done.2 = bf16[2,64,2304]{2,1,0:T(8,128)(2,1)S(1)} copy-done((bf16[2,64,2304]{2,1,0:T(8,128)(2,1)S(1)}, bf16[2,64,2304]{2,1,0:T(8,128)(2,1)}, u32[]{:S(2)}) %copy-start.2) | copy-done | bytes 589848
  2.5 0.9 %copy-done.4 = bf16[2,64,512]{2,1,0:T(8,128)(2,1)S(1)} copy-done((bf16[2,64,512]{2,1,0:T(8,128)(2,1)S(1)}, bf16[2,64,512]{2,1,0:T(8,128)(2,1)}, u32[]{:S(2)}) %copy-start.4) | copy-done | bytes 131096
  3.4 0.7 copy-done.6
  4.0 2.1 %pack_grads.1 = bf16[5632,128]{1,0:T(8,128)(2,1)} custom-call(s32[64,2]{1,0:T(8,128)S(1)} %copy.22.owner_ref, s32[1,64]{1,0:T(1,128)S(1)} %bitcast.51, bf16[128,2304]{1,0:T(8,128)(2,1)S(1)} %bitcast.49, bf16[128,512]{1,0:T(8,128)(2,1)S(1)} %bitcast.50), custom_call_target="tpu_custom_call" | custom-call | flops 184549376 | bytes 3145728 | tf_op jit(solution)/shard_map/pack_grads/pallas_call | solution.py:283
  6.2 11.5 %all-to-all-start = ((bf16[128,2,2816]{2,1,0:T(2,128)(2,1)}), bf16[128,2,2816]{2,1,0:T(2,128)(2,1)S(1)}, u32[]{:S(2)}, u32[]{:S(2)}) async-start(bf16[128,2,2816]{2,1,0:T(2,128)(2,1)} %bitcast.6), calls=%async_computation | async-start | bytes 2883584 | tf_op jit(solution)/shard_map/all_to_all | solution.py:298
  17.7 0.0 copy-done.3
  17.7 0.0 copy-done.5
  17.7 0.0 copy-done.7
  17.7 0.0 copy-start.11
  17.7 0.0 copy-start.9
  17.7 0.0 copy-start.10
  17.7 1.6 %pack_weights.1 = bf16[2816,128]{1,0:T(8,128)(2,1)} custom-call(s32[1,64]{1,0:T(1,128)S(1)} %bitcast.52, bf16[2,64,2304]{2,1,0:T(8,128)(2,1)S(1)} %copy-done.3, bf16[2,64,512]{2,1,0:T(8,128)(2,1)S(1)} %copy-done.5), custom_call_target="tpu_custom_call" | custom-call | flops 46137344 | bytes 3145728 | tf_op jit(solution)/shard_map/pack_weights/pallas_call | solution.py:302
  19.4 21.0 %all-to-all-done = bf16[128,2,2816]{2,1,0:T(2,128)(2,1)S(1)} async-done(((bf16[128,2,2816]{2,1,0:T(2,128)(2,1)}), bf16[128,2,2816]{2,1,0:T(2,128)(2,1)S(1)}, u32[]{:S(2)}, u32[]{:S(2)}) %all-to-all-start) | async-done | bytes 1441824 | tf_op jit(solution)/shard_map/all_to_all | solution.py:298
  40.4 3.6 %all-to-all-start.2 = ((bf16[16,176,128]{2,1,0:T(8,128)(2,1)}), bf16[16,176,128]{2,1,0:T(8,128)(2,1)S(1)}, u32[]{:S(2)}, u32[]{:S(2)}) async-start(bf16[16,176,128]{2,1,0:T(8,128)(2,1)} %bitcast.17), calls=%async_computation.2 | async-start | bytes 1441792 | tf_op jit(solution)/shard_map/all_to_all | solution.py:311
  44.0 0.1 copy.21
  44.1 0.1 reshape_squeeze.3.owner_ref
  44.3 0.0 copy-start.1
  44.3 1.4 %copy-done.1 = bf16[128,2,2816]{2,1,0:T(2,128)(2,1)S(1)} copy-done((bf16[128,2,2816]{2,1,0:T(2,128)(2,1)S(1)}, bf16[128,2,2816]{2,1,0:T(2,128)(2,1)}, u32[]{:S(2)}) %copy-start.1) | copy-done | bytes 1441816
  45.7 1.7 %copy-done.8 = f32[2,294912]{1,0:T(2,128)S(1)} copy-done((f32[2,294912]{1,0:T(2,128)S(1)}, f32[2,294912]{1,0:T(2,128)}, u32[]{:S(2)}) %copy-start.8) | copy-done | bytes 2359320
  47.3 7.0 %polar.1 = (bf16[8,720,128]{2,1,0:T(8,128)(2,1)S(1)}, f32[4608,128]{1,0:T(8,128)}, f32[1024,128]{1,0:T(8,128)}) custom-call(s32[128]{0:T(128)S(1)} %reshape_squeeze.3.owner_ref, bf16[5632,128]{1,0:T(8,128)(2,1)S(1)} %bitcast.48, f32[4608,128]{1,0:T(8,128)S(1)} %bitcast.53, f32[1024,128]{1,0:T(8,128)S(1)} %bitcast.54, bf16[2,64]{1,0:T(2,128)(2,1)S(1)} %bitcast.55), custom_call_target="tpu_custom_call" | custom-call | flops 4000000000 | bytes 8388608 | tf_op jit(solution)/shard_map/polar/pallas_call | solution.py:318
  54.3 2.0 %all-to-all-done.2.weight_ref = bf16[16,176,128]{2,1,0:T(8,128)(2,1)S(1)} async-done(((bf16[16,176,128]{2,1,0:T(8,128)(2,1)}), bf16[16,176,128]{2,1,0:T(8,128)(2,1)S(1)}, u32[]{:S(2)}, u32[]{:S(2)}) %all-to-all-start.2) | async-done | bytes 720928 | tf_op jit(solution)/shard_map/all_to_all | solution.py:311
  56.3 24.5 %all_to_all.15.polar_ref = bf16[8,720,128]{2,1,0:T(8,128)(2,1)S(1)} all-to-all(bf16[8,720,128]{2,1,0:T(8,128)(2,1)S(1)} %get-tuple-element.9), channel_id=1, replica_groups=mesh['dp'=8,'mp'=16] {'dp'}, dimensions={0} | all-to-all | bytes 2949120 | tf_op jit(solution)/shard_map/all_to_all | solution.py:331
  80.8 1.8 %finish.1 = (bf16[2304,128]{1,0:T(8,128)(2,1)}, bf16[512,128]{1,0:T(8,128)(2,1)}) custom-call(s32[128]{0:T(128)S(1)} %reshape_squeeze.3.owner_ref, s32[64]{0:T(128)S(1)} %copy-done.7, bf16[8,720,128]{2,1,0:T(8,128)(2,1)S(1)} %all_to_all.15.polar_ref, bf16[16,176,128]{2,1,0:T(8,128)(2,1)S(1)} %all-to-all-done.2.weight_ref), custom_call_target="tpu_custom_call" | custom-call | flops 10000000 | bytes 4194304 | tf_op jit(solution)/shard_map/finish/pallas_call | solution.py:335
  (12 shorter events, 0.0 us)
Async XLA Ops:
  1.4 1.1 %copy-start.2 = (bf16[2,64,2304]{2,1,0:T(8,128)(2,1)S(1)}, bf16[2,64,2304]{2,1,0:T(8,128)(2,1)}, u32[]{:S(2)}) copy-start(bf16[2,64,2304]{2,1,0:T(8,128)(2,1)} %param.9) | copy-start | bytes 1769476
  2.5 0.9 %copy-start.4 = (bf16[2,64,512]{2,1,0:T(8,128)(2,1)S(1)}, bf16[2,64,512]{2,1,0:T(8,128)(2,1)}, u32[]{:S(2)}) copy-start(bf16[2,64,512]{2,1,0:T(8,128)(2,1)} %param.10) | copy-start | bytes 393220
  3.4 0.7 copy-start.6
  6.2 11.5 %copy-start.3 = (bf16[2,64,2304]{2,1,0:T(8,128)(2,1)S(1)}, bf16[2,64,2304]{2,1,0:T(8,128)(2,1)}, u32[]{:S(2)}) copy-start(bf16[2,64,2304]{2,1,0:T(8,128)(2,1)} %wq_ref.1) | copy-start | bytes 1769476
  6.2 11.5 %copy-start.5 = (bf16[2,64,512]{2,1,0:T(8,128)(2,1)S(1)}, bf16[2,64,512]{2,1,0:T(8,128)(2,1)}, u32[]{:S(2)}) copy-start(bf16[2,64,512]{2,1,0:T(8,128)(2,1)} %wk_ref.1) | copy-start | bytes 393220
  6.2 11.5 %copy-start.7 = (s32[64]{0:T(128)S(1)}, s32[64]{0:T(128)}, u32[]{:S(2)}) copy-start(s32[64]{0:T(128)} %head_ref.1) | copy-start | bytes 772
  6.2 34.2 %all-to-all-start = ((bf16[128,2,2816]{2,1,0:T(2,128)(2,1)}), bf16[128,2,2816]{2,1,0:T(2,128)(2,1)S(1)}, u32[]{:S(2)}, u32[]{:S(2)}) async-start(bf16[128,2,2816]{2,1,0:T(2,128)(2,1)} %bitcast.6), calls=%async_computation | async-start | bytes 2883584 | tf_op jit(solution)/shard_map/all_to_all | solution.py:298
  17.7 26.3 %copy-start.11 = (s32[64,2,1]{0,2,1:T(1,128)S(1)}, s32[64,2,1]{0,2,1:T(1,128)}, u32[]{:S(2)}) copy-start(s32[64,2,1]{0,2,1:T(1,128)} %param.16) | copy-start | bytes 1540
  17.7 26.6 %copy-start.9 = (f32[2,65536]{1,0:T(2,128)S(1)}, f32[2,65536]{1,0:T(2,128)}, u32[]{:S(2)}) copy-start(f32[2,65536]{1,0:T(2,128)} %param.14) | copy-start | bytes 1572868
  17.7 26.6 %copy-start.10 = (bf16[1,2,64]{2,1,0:T(2,128)(2,1)S(1)}, bf16[1,2,64]{2,1,0:T(2,128)(2,1)}, u32[]{:S(2)}) copy-start(bf16[1,2,64]{2,1,0:T(2,128)(2,1)} %param.15) | copy-start | bytes 772
  40.4 3.9 %copy-start = (bf16[128,2,2816]{2,1,0:T(2,128)(2,1)}, bf16[128,2,2816]{2,1,0:T(2,128)(2,1)S(1)}, u32[]{:S(2)}) copy-start(bf16[128,2,2816]{2,1,0:T(2,128)(2,1)S(1)} %all-to-all-done) | copy-start | bytes 4325380
  40.4 15.9 %all-to-all-start.2 = ((bf16[16,176,128]{2,1,0:T(8,128)(2,1)}), bf16[16,176,128]{2,1,0:T(8,128)(2,1)S(1)}, u32[]{:S(2)}, u32[]{:S(2)}) async-start(bf16[16,176,128]{2,1,0:T(8,128)(2,1)} %bitcast.17), calls=%async_computation.2 | async-start | bytes 1441792 | tf_op jit(solution)/shard_map/all_to_all | solution.py:311
  44.3 1.4 %copy-start.1 = (bf16[128,2,2816]{2,1,0:T(2,128)(2,1)S(1)}, bf16[128,2,2816]{2,1,0:T(2,128)(2,1)}, u32[]{:S(2)}) copy-start(bf16[128,2,2816]{2,1,0:T(2,128)(2,1)} %copy-done) | copy-start | bytes 4325380
  45.7 1.7 %copy-start.8 = (f32[2,294912]{1,0:T(2,128)S(1)}, f32[2,294912]{1,0:T(2,128)}, u32[]{:S(2)}) copy-start(f32[2,294912]{1,0:T(2,128)} %param.13) | copy-start | bytes 7077892

commit v2 on v1

v2 whole, which is shorter than its diff:
```python
import functools
import math

import jax
import jax.numpy as jnp
from jax import lax
from jax.experimental import pallas as pl
from jax.experimental.pallas import tpu as pltpu
from jax.sharding import PartitionSpec as P

DN = 128
RQ = 1536
RK = 512
ITERS = 5
DQ = 192
LANE = 128

quintic_one = 3.4445
quintic_two = -4.775
quintic_three = 2.0315
momentum_decay = 0.95
step_size = 0.5
logit_cap = 100.0

f32 = jnp.float32
bf16 = jnp.bfloat16
VMEM = pl.BlockSpec(memory_space=pltpu.VMEM)
SMEM = pl.BlockSpec(memory_space=pltpu.SMEM)
HBM = pl.BlockSpec(memory_space=pltpu.HBM)
SIDE = 4


def iota(shape, dim):
    return lax.broadcasted_iota(jnp.int32, shape, dim)


def dot(a, b, dims=((1,), (0,))):
    return lax.dot_general(a, b, (dims, ((), ())), preferred_element_type=f32)


def head_matrix(head_ref, heads):
    return (iota((heads, heads), 0) == head_ref[...]).astype(bf16)


def pack_grads_kernel(
    owner_ref, head_ref, gq_far, gk_far, out_far, gq_ref, gk_ref, stage, out_ref, sems, *, ranks, owners, slots
):
    copies = [
        pltpu.make_async_copy(gq_far, gq_ref, sems.at[0]),
        pltpu.make_async_copy(gk_far, gk_ref, sems.at[1]),
    ]
    for copy in copies:
        copy.start()
    layers, heads = owner_ref.shape
    devices = ranks * owners
    per_rank = heads // ranks
    tq = gq_ref.shape[1] // LANE
    tk = gk_ref.shape[1] // LANE
    rows = (tq + tk) * slots
    by_lane = owner_ref[...].astype(f32)
    eye = (iota((heads, heads), 0) == iota((heads, heads), 1)).astype(f32)
    by_row = dot(eye, by_lane, ((1,), (1,)))
    other, mine = iota((heads, heads), 0), iota((heads, heads), 1)
    same_rank = (other // per_rank) == (mine // per_rank)
    heads_of = head_matrix(head_ref, heads)
    lane_rank = iota((1, heads), 1) // per_rank
    picks = [[None] * layers for _ in range(slots)]
    for layer in range(layers):
        owner = by_lane[layer : layer + 1, :]
        earlier = jnp.zeros((1, heads), f32)
        for before in range(layers):
            ahead = (other <= mine) if before < layer else (other < mine)
            hit = same_rank & ahead & (by_row[:, before : before + 1] == owner)
            earlier += jnp.sum(hit.astype(f32), axis=0, keepdims=True)
        target = (owner.astype(jnp.int32) * ranks + lane_rank) * slots + earlier.astype(jnp.int32)
        for slot in range(slots):
            chosen = (iota((devices, heads), 0) * slots + slot == target).astype(bf16)
            picks[slot][layer] = dot(chosen, heads_of, ((1,), (1,))).astype(bf16)
    for copy in copies:
        copy.wait()
    for slot in range(slots):
        pick = jnp.concatenate(picks[slot], axis=1)
        for ref, tiles, base in ((gq_ref, tq, 0), (gk_ref, tk, tq)):
            value = dot(pick, ref[...])
            for tile in range(tiles):
                stage[pl.ds((base + tile) * slots + slot, devices, stride=rows), :] = value[
                    :, tile * LANE : (tile + 1) * LANE
                ]
    sends = []
    count = out_ref.shape[0] // owners
    for owner in range(owners):
        at = pl.ds(owner * count, count)
        out_ref[at, :] = stage[at, :].astype(bf16)
        sends.append(pltpu.make_async_copy(out_ref.at[at, :], out_far.at[at, :], sems.at[2 + owner]))
        sends[-1].start()
    for copy in sends:
        copy.wait()


def pack_weights_kernel(head_ref, wq_ref, wk_ref, *rest, ranks):
    outs, stage = rest[:-1], rest[-1]
    here_rank = lax.axis_index("mp")
    here_x, here_y = here_rank // SIDE, here_rank % SIDE
    layers, heads, _ = wq_ref.shape
    per_rank = heads // ranks
    tq = wq_ref.shape[2] // LANE
    tk = wk_ref.shape[2] // LANE
    rows = layers * (tq + tk) * per_rank
    heads_of = head_matrix(head_ref, heads)
    place, position = iota((heads, heads), 0), iota((heads, heads), 1)
    to_x = (here_x + place % SIDE) % SIDE
    to_y = (here_y + place % ranks // SIDE) % SIDE
    order = (position == (to_x * SIDE + to_y) * per_rank + place // ranks).astype(bf16)
    pick = dot(order, heads_of, ((1,), (1,))).astype(bf16)
    for layer in range(layers):
        for ref, tiles, base in ((wq_ref, tq, 0), (wk_ref, tk, tq)):
            value = dot(pick, ref[layer])
            for tile in range(tiles):
                first = (layer * (tq + tk) + base + tile) * per_rank
                for place_in in range(per_rank):
                    stage[pl.ds(first + place_in, ranks, stride=rows), :] = value[
                        place_in * ranks : (place_in + 1) * ranks, tile * LANE : (tile + 1) * LANE
                    ]
    for shift, out in enumerate(outs):
        out[...] = stage[shift * SIDE * rows : (shift + 1) * SIDE * rows, :].astype(bf16).reshape(SIDE, rows, LANE)


def polar_kernel(
    owner_ref,
    recv_ref,
    mq_far,
    mk_far,
    out_far,
    mq_next,
    mk_next,
    mq_ref,
    mk_ref,
    out_ref,
    sems_in,
    sems_out,
    sems_send,
    *,
    ranks,
    owners,
    slots,
):
    devices = ranks * owners
    parts = sems_in.shape[0] // 2

    def piece(ref, part):
        count = ref.shape[0] // parts
        return ref.at[pl.ds(part * count, count), :]

    def moves(sems, pairs):
        return [
            [
                pltpu.make_async_copy(piece(src, part), piece(dst, part), sems.at[2 * part + j])
                for j, (src, dst) in enumerate(pairs)
            ]
            for part in range(parts)
        ]

    loads = moves(sems_in, ((mq_far, mq_ref), (mk_far, mk_ref)))
    stores = moves(sems_out, ((mq_ref, mq_next), (mk_ref, mk_next)))
    for pair in loads:
        for copy in pair:
            copy.start()
    here_owner = lax.axis_index("dp")
    here_rank = lax.axis_index("mp")
    layers, heads = owner_ref.shape
    per_rank = heads // ranks
    named = (owner_ref[...] == here_owner) & (iota((layers, heads), 1) // per_rank == here_rank)
    held = jnp.sum(jnp.sum(named.astype(f32), axis=1, keepdims=True), axis=0, keepdims=True)
    held = jnp.broadcast_to(held.astype(jnp.int32), (8, LANE))
    sub = iota((8, LANE), 0)
    decay = jnp.where((sub % slots) < held, momentum_decay, 1.0)
    low = sub < 4
    tq = DQ * RQ // LANE // devices * slots
    tk = DN * RK // LANE // devices * slots
    rows = tq + tk

    def tile_of(value, index):
        return value[index * 8 : (index + 1) * 8, :]

    def step(quad, totals):
        totals = list(totals)
        block = recv_ref[pl.ds(pl.multiple_of(quad * 4 * rows, 16), 4 * rows), :].astype(f32)
        for pair in range(2):
            g = [tile_of(block, pair * 11 + j) for j in range(11)]
            query = g[0:4] + [jnp.where(low, g[4], g[5])] + g[6:10]
            key = [pltpu.roll(jnp.where(low, g[5], g[4]), 4, 0), g[10]]
            for which, (grads, ref, count) in enumerate(((query, mq_ref, 9), (key, mk_ref, 2))):
                base = pl.multiple_of((quad * 2 + pair) * count * 8, 8)
                for j in range(count):
                    at = pl.ds(pl.multiple_of(base + j * 8, 8), 8)
                    new = ref[at, :] * decay + grads[j]
                    ref[at, :] = new
                    totals[which] += new * new
        return tuple(totals)

    totals = (jnp.zeros((8, LANE), f32), jnp.zeros((8, LANE), f32))
    turns = devices // 4 // parts
    for part in range(parts):
        for copy in loads[part]:
            copy.wait()
        totals = lax.fori_loop(part * turns, (part + 1) * turns, step, totals)
        for copy in stores[part]:
            copy.start()

    chains = []
    for slot in range(slots):
        for ref, total, height, width in ((mq_ref, totals[0], DQ, RQ), (mk_ref, totals[1], DN, RK)):
            tiles = width // LANE
            norm = jnp.sqrt(jnp.sum(jnp.where(sub % slots == slot, total, 0.0), keepdims=True))
            scale = 1.0 / (norm + 1e-07)
            chains.append(
                jnp.concatenate(
                    [
                        (ref[pl.ds(tile * slots + slot, height, stride=tiles * slots), :] * scale).astype(bf16)
                        for tile in range(tiles)
                    ],
                    axis=1,
                )
            )
    for turn in range(ITERS):
        grams = [dot(x, x, ((1,), (1,))).astype(bf16) for x in chains]
        squares = [dot(a, a) for a in grams]
        mixings = [
            (quintic_two * a.astype(f32) + quintic_three * s).astype(bf16) for a, s in zip(grams, squares)
        ]
        products = [dot(b, x) for b, x in zip(mixings, chains)]
        chains = [quintic_one * x.astype(f32) + y for x, y in zip(chains, products)]
        if turn < ITERS - 1:
            chains = [x.astype(bf16) for x in chains]
    fq = DQ * RQ // LANE // owners
    fk = DN * RK // LANE // owners
    sends = []
    for owner in range(owners):
        for slot in range(slots):
            for x, height, width, at in (
                (chains[2 * slot], DQ, RQ, slot * (fq + fk)),
                (chains[2 * slot + 1], DN, RK, slot * (fq + fk) + fq),
            ):
                span = height // owners
                mine = x[owner * span : (owner + 1) * span]
                for tile in range(0, width // LANE, 2):
                    both = [mine[:, (tile + j) * LANE : (tile + j + 1) * LANE] for j in range(2)]
                    out_ref[owner, at + tile * span : at + (tile + 2) * span, :] = jnp.concatenate(
                        both, axis=0
                    ).astype(bf16)
        sends.append(pltpu.make_async_copy(out_ref.at[owner], out_far.at[owner], sems_send.at[owner]))
        sends[-1].start()
    for copy in sends:
        copy.wait()
    for pair in stores:
        for copy in pair:
            copy.wait()


def finish_kernel(owner_ref, head_ref, peak_ref, polar_ref, *rest, ranks, owners, slots):
    weight_refs, (q_out, k_out, spread_q, spread_k) = rest[:SIDE], rest[SIDE:]
    here_owner = lax.axis_index("dp")
    here_rank = lax.axis_index("mp")
    heads = head_ref.shape[0]
    layers = owner_ref.shape[0]
    per_rank = heads // ranks
    fq = DQ * RQ // LANE // owners
    fk = DN * RK // LANE // owners
    peaks = jnp.concatenate([peak_ref[...].astype(f32), jnp.zeros((layers, LANE - heads), f32)], axis=1)
    names = [
        owner_ref[layer, here_rank * per_rank + place] for place in range(per_rank) for layer in range(layers)
    ]
    sub, lane = iota((8, LANE), 0), iota((8, LANE), 1)
    head_of = jnp.zeros((8, LANE), jnp.int32)
    for place in range(per_rank):
        head_of = jnp.where(sub % per_rank == place, head_ref[here_rank * per_rank + place], head_of)
    sq = fq // ranks * per_rank
    sk = fk // ranks * per_rank
    span = sq + sk
    cq = step_size * 0.2 * math.sqrt(max(DQ, RQ))
    ck = step_size * 0.2 * math.sqrt(max(DN, RK))
    for layer in range(layers):
        for place in range(per_rank):
            unit = place * layers + layer
            earlier = jnp.int32(0)
            for before in range(unit):
                earlier += (names[before] == names[unit]).astype(jnp.int32)
            start = pl.multiple_of(earlier * (fq + fk), 16)
            block = polar_ref[names[unit], pl.ds(start, fq + fk), :].astype(f32)
            for spread, height, width, base in ((spread_q, DQ, RQ, 0), (spread_k, DN, RK, fq)):
                deep = height // owners
                tiles = width // LANE
                first = layer * deep * tiles * per_rank + place
                for tile in range(tiles):
                    spread[pl.ds(first + tile * per_rank, deep, stride=tiles * per_rank), :] = block[
                        base + tile * deep : base + (tile + 1) * deep
                    ]
    for t in range(SIDE):
        for s in range(SIDE):
            source = (here_rank // SIDE + SIDE - t) % SIDE * SIDE + (here_rank % SIDE + SIDE - s) % SIDE
            held = weight_refs[t][s].astype(f32)
            for layer in range(layers):
                at = pl.ds(pl.multiple_of(layer * fq * per_rank + source * sq, 8), sq)
                spread_q[at, :] = held[layer * span : layer * span + sq] - cq * spread_q[at, :]
                at = pl.ds(pl.multiple_of(layer * fk * per_rank + source * sk, 8), sk)
                spread_k[at, :] = held[layer * span + sq : (layer + 1) * span] - ck * spread_k[at, :]
    for layer in range(layers):
        peak = jnp.sum(
            jnp.where(head_of == lane, jnp.broadcast_to(peaks[layer : layer + 1, :], (8, LANE)), 0.0),
            axis=1,
            keepdims=True,
        )
        factor = jnp.broadcast_to(jnp.minimum(1.0, logit_cap / peak), (8, LANE))
        root = jnp.sqrt(factor)
        height = RQ // LANE * per_rank
        for row in range(DQ // owners):
            at = layer * fq * per_rank + row * height
            scale = jnp.where(here_owner * (DQ // owners) + row < DN, root, factor)
            value = spread_q[at : at + height, :] * jnp.concatenate([scale] * (height // 8), axis=0)
            q_out[at : at + height, :] = value.astype(bf16)
        at = layer * fk * per_rank
        height = fk * per_rank
        value = spread_k[at : at + height, :] * jnp.concatenate([root] * (height // 8), axis=0)
        k_out[at : at + height, :] = value.astype(bf16)


def call(kernel, name, out_shape, in_specs, scratch, flops, moved, out_specs=None, limit=8):
    return pl.pallas_call(
        kernel,
        name=name,
        out_shape=out_shape,
        in_specs=in_specs,
        out_specs=out_specs or jax.tree.map(lambda _: VMEM, out_shape),
        scratch_shapes=scratch,
        compiler_params=pltpu.CompilerParams(vmem_limit_bytes=limit * 2**20),
        cost_estimate=pl.CostEstimate(flops=flops, bytes_accessed=moved, transcendentals=0),
    )


def to_rows(array):
    slots, width = array.shape
    return array.reshape(slots, width // LANE, LANE).transpose(1, 0, 2).reshape(-1, LANE)


def from_rows(rows, slots):
    return rows.reshape(-1, slots, LANE).transpose(1, 0, 2).reshape(slots, -1)


def body(
    grad_query,
    grad_key,
    weight_query,
    weight_key,
    moment_query,
    moment_key,
    logit_peak,
    owner_table,
    head_order,
):
    owners = lax.axis_size("dp")
    ranks = lax.axis_size("mp")
    devices = owners * ranks
    layers, heads, piece_q = grad_query.shape
    piece_k = grad_key.shape[2]
    slots = moment_query.shape[0]
    per_rank = heads // ranks
    tiles = (piece_q + piece_k) // LANE
    kw = dict(ranks=ranks, owners=owners, slots=slots)
    shape = jax.ShapeDtypeStruct
    owner_2d = owner_table[:, :, 0].T
    head_row = head_order.reshape(1, heads)

    packed = call(
        functools.partial(pack_grads_kernel, **kw),
        "pack_grads",
        shape((devices * tiles * slots, LANE), bf16),
        [VMEM, VMEM, HBM, HBM],
        [
            pltpu.VMEM((layers * heads, piece_q), bf16),
            pltpu.VMEM((layers * heads, piece_k), bf16),
            pltpu.VMEM((devices * tiles * slots, LANE), f32),
            pltpu.VMEM((devices * tiles * slots, LANE), bf16),
            pltpu.SemaphoreType.DMA((2 + owners,)),
        ],
        2 * 256 * 128 * 2816,
        3 * 2**20,
        out_specs=HBM,
        limit=58,
    )(
        owner_2d,
        head_row,
        grad_query.reshape(layers * heads, piece_q),
        grad_key.reshape(layers * heads, piece_k),
    )
    packed = packed.reshape(devices, tiles, slots, LANE).transpose(0, 2, 1, 3).reshape(devices, slots, -1)
    owned = lax.all_to_all(packed, ("dp", "mp"), split_axis=0, concat_axis=0, tiled=True)
    owned = owned.reshape(devices, slots, tiles, LANE).transpose(0, 2, 1, 3).reshape(-1, LANE)

    wrows = layers * tiles * per_rank
    by_y = call(
        functools.partial(pack_weights_kernel, ranks=ranks),
        "pack_weights",
        [shape((SIDE, wrows, LANE), bf16)] * SIDE,
        [VMEM] * 3,
        [pltpu.VMEM((ranks * wrows, LANE), f32)],
        2 * 128 * 64 * 2816,
        3 * 2**20,
    )(head_row, weight_query, weight_key)
    along_y = [
        [(i, i // SIDE * SIDE + (i + s) % SIDE) for i in range(ranks)] for s in range(SIDE)
    ]
    along_x = [[(i, (i + t * SIDE) % ranks) for i in range(ranks)] for t in range(SIDE)]
    peaks = logit_peak[0]
    reach = 1
    while reach < owners:
        peaks = jnp.maximum(peaks, lax.ppermute(peaks, "dp", [(i, i ^ reach) for i in range(owners)]))
        reach *= 2
    owned, by_y, peaks = lax.optimization_barrier((owned, by_y, peaks))
    by_y = [by_y[0]] + [lax.ppermute(by_y[s], "mp", along_y[s]) for s in range(1, SIDE)]
    fq = DQ * RQ // LANE
    fk = DN * RK // LANE
    parts = 4
    polar, next_q, next_k = call(
        functools.partial(polar_kernel, **kw),
        "polar",
        (
            shape((owners, slots * (fq + fk) // owners, LANE), bf16),
            shape((fq * slots, LANE), f32),
            shape((fk * slots, LANE), f32),
        ),
        [VMEM, VMEM, HBM, HBM],
        [
            pltpu.VMEM((fq * slots, LANE), f32),
            pltpu.VMEM((fk * slots, LANE), f32),
            pltpu.VMEM((owners, slots * (fq + fk) // owners, LANE), bf16),
            pltpu.SemaphoreType.DMA((2 * parts,)),
            pltpu.SemaphoreType.DMA((2 * parts,)),
            pltpu.SemaphoreType.DMA((owners,)),
        ],
        4 * 10**9,
        8 * 2**20,
        (HBM, HBM, HBM),
        50,
    )(owner_2d, owned, to_rows(moment_query), to_rows(moment_key))
    polar, by_y = lax.optimization_barrier((polar, by_y))
    by_x = [jnp.stack([block[t] for block in by_y], axis=0) for t in range(SIDE)]
    weights = [by_x[0]] + [lax.ppermute(by_x[t], "mp", along_x[t]) for t in range(1, SIDE)]
    back = lax.all_to_all(polar, "dp", split_axis=0, concat_axis=0, tiled=True)

    oq = layers * per_rank * fq // owners
    ok = layers * per_rank * fk // owners
    new_q, new_k = call(
        functools.partial(finish_kernel, **kw),
        "finish",
        (shape((oq, LANE), bf16), shape((ok, LANE), bf16)),
        [SMEM, SMEM, VMEM, VMEM] + [VMEM] * SIDE,
        [
            pltpu.VMEM((oq, LANE), f32),
            pltpu.VMEM((ok, LANE), f32),
        ],
        10**7,
        4 * 2**20,
    )(owner_2d, head_order, peaks, back, *weights)

    def rollout(rows):
        rows = rows.reshape(layers, -1, per_rank, LANE).transpose(0, 2, 1, 3)
        return rows.reshape(layers, per_rank, -1)

    return rollout(new_q), rollout(new_k), from_rows(next_q, slots), from_rows(next_k, slots)


def solution(mesh):
    placed = (
        P(None, None, ("dp", "mp")),
        P(None, None, ("dp", "mp")),
        P(None, None, ("dp", "mp")),
        P(None, None, ("dp", "mp")),
        P(("dp", "mp"), None),
        P(("dp", "mp"), None),
        P("dp", None, None),
        P(),
        P(),
    )
    return jax.shard_map(
        body,
        mesh=mesh,
        in_specs=placed,
        out_specs=(
            P(None, "mp", "dp"),
            P(None, "mp", "dp"),
            P(("dp", "mp"), None),
            P(("dp", "mp"), None),
        ),
        check_vma=False,
    )
```

time: 83 us -> 77.7 us (0.936)
  blocking collectives: 24.5 us -> 0 us
  starting transfers between devices: 15.1 us -> 28.1 us
  waiting for transfers between devices: 23 us -> 32.8 us
  local copies, waits for them, and re-layouts: 6.68 us -> 0.09 us
  Pallas kernels: 12.6 us -> 14.9 us
    all_to_all x1 -> x0, blocking collectives: 24.5 us -> none  [body(): back = lax.all_to_all(polar, 'dp', split_axis=0, concat_axis=0, tiled=True)]
    ppermute x0 -> x9, waiting for transfers between devices: none -> 14.7 us  [the longest x3 8.29 us: body(): lax.ppermute(by_x[t], 'mp', along_x[t])]
    ppermute x0 -> x9, starting transfers between devices: none -> 11.9 us  [the longest x3 5.18 us: body(): lax.ppermute(by_x[t], 'mp', along_x[t])]
    all_to_all x1, waiting for transfers between devices: 21 us -> 12.4 us  [body(): lax.all_to_all(packed, ('dp', 'mp'), split_axis=0, concat_axis=0, tiled=T...]
    unnamed x25 -> x12, local copies, waits for them, and re-layouts: 5.77 us -> 0.04 us
    all_to_all x1, waiting for transfers between devices: 1.97 us -> 5.67 us  [body(): back = lax.all_to_all(polar, 'dp', split_axis=0, concat_axis=0, tiled=True)]
    pallas_call x1, Pallas kernels: 6.96 us -> 8.37 us  [body(): call(functools.partial(polar_kernel, **kw), 'polar', (shape((owners, slot...]
    pallas_call x1, Pallas kernels: 2.13 us -> 3.52 us  [body(): call(functools.partial(pack_grads_kernel, **kw), 'pack_grads', shape((dev...]
  transfers between devices with their start and end apart: 2 -> 11, of which waited for: 2 -> 7; matrix products, arithmetic and copies ran while one was open for 0% -> 0% of each run, Pallas kernels for 10% -> 12%
where the time goes in v2:
time: 77.7 us; the launch traced here: 76.8 us
  waiting for transfers between devices  32.8 us (42%)
  starting transfers between devices  28.1 us (36%)
  Pallas kernels  14.9 us (19%)
  between operations  0.78 us (1%)
    all_to_all x1, waiting for transfers between devices, body(): lax.all_to_all(packed, ('dp', 'mp'), split_axis=0, concat_axis=0, tiled=T...  12.4 us
    all_to_all x1, starting transfers between devices, body(): lax.all_to_all(packed, ('dp', 'mp'), split_axis=0, concat_axis=0, tiled=T...  11.5 us
    pallas_call x1, Pallas kernels, body(): call(functools.partial(polar_kernel, **kw), 'polar', (shape((owners, slot...  8.37 us
    ppermute x3, waiting for transfers between devices, body(): lax.ppermute(by_x[t], 'mp', along_x[t])  8.29 us
    ppermute x3, waiting for transfers between devices, body(): lax.ppermute(peaks, 'dp', [(i, i ^ reach) for i in range(owners)])  6.45 us
    all_to_all x1, waiting for transfers between devices, body(): back = lax.all_to_all(polar, 'dp', split_axis=0, concat_axis=0, tiled=True)  5.67 us
    ppermute x3, starting transfers between devices, body(): lax.ppermute(by_x[t], 'mp', along_x[t])  5.18 us
    all_to_all x1, starting transfers between devices, body(): back = lax.all_to_all(polar, 'dp', split_axis=0, concat_axis=0, tiled=True)  4.73 us
  transfers between devices with their start and end apart: 11, of which 7 were waited for; matrix products, arithmetic and copies ran while one was open for 0% of the time, Pallas kernels for 12%

profile of v2, /device:TPU:1, one launch (start us, length us, event | category | flops | bytes accessed | tf_op | source)
XLA Modules:
  0.0 76.8 jit_solution(16925487633792247971)
XLA Ops:
  0.6 3.5 %pack_grads.1 = bf16[5632,128]{1,0:T(8,128)(2,1)} custom-call(s32[2,64]{1,0:T(2,128)} %bitcast.51, s32[1,64]{1,0:T(1,128)} %bitcast.49, bf16[128,2304]{1,0:T(8,128)(2,1)} %bitcast.56, bf16[128,512]{1,0:T(8,128)(2,1)} %bitcast.57), custom_call_target="tpu_custom_call" | custom-call | flops 184549376 | bytes 3145728 | tf_op jit(solution)/shard_map/pack_grads/pallas_call | solution.py:373
  4.2 0.0 copy-start
  4.2 0.0 copy-start.1
  4.2 11.5 %all-to-all-start = ((bf16[128,2,2816]{2,1,0:T(2,128)(2,1)}), bf16[128,2,2816]{2,1,0:T(2,128)(2,1)S(1)}, u32[]{:S(2)}, u32[]{:S(2)}) async-start(bf16[128,2,2816]{2,1,0:T(2,128)(2,1)} %bitcast.55), calls=%async_computation | async-start | bytes 2883584 | tf_op jit(solution)/shard_map/all_to_all | solution.py:396
  15.8 1.1 %collective-permute-start = (bf16[2,64]{1,0:T(2,128)(2,1)S(1)}, bf16[2,64]{1,0:T(2,128)(2,1)S(1)}, u32[]{:S(2)}, u32[]{:S(2)}) collective-permute-start(bf16[2,64]{1,0:T(2,128)(2,1)S(1)} %bitcast.61), channel_id=1, source_target_pairs={{0,16},{16,0},{32,48},{48,32},{64,80},{80,64},{96,112},{112,96},{1... | collective-permute-start | bytes 776 | tf_op jit(solution)/shard_map/ppermute | solution.py:416
  16.9 0.8 %collective-permute-done = bf16[2,64]{1,0:T(2,128)(2,1)S(1)} collective-permute-done((bf16[2,64]{1,0:T(2,128)(2,1)S(1)}, bf16[2,64]{1,0:T(2,128)(2,1)S(1)}, u32[]{:S(2)}, u32[]{:S(2)}) %collective-permute-start) | collective-permute-done | bytes 288 | tf_op jit(solution)/shard_map/ppermute | solution.py:416
  17.7 0.8 %collective-permute-start.1 = (bf16[2,64]{1,0:T(2,128)(2,1)S(1)}, bf16[2,64]{1,0:T(2,128)(2,1)S(1)}, u32[]{:S(2)}, u32[]{:S(2)}) collective-permute-start(bf16[2,64]{1,0:T(2,128)(2,1)S(1)} %bitcast_maximum_fusion), channel_id=1, source_target_pairs={{0,32},{16,48},{32,0},{48,16},{64,96},{80,112},{96,64},{112,80},{1... | collective-permute-start | bytes 776 | tf_op jit(solution)/shard_map/ppermute | solution.py:416
  18.5 3.3 %collective-permute-done.1 = bf16[2,64]{1,0:T(2,128)(2,1)S(1)} collective-permute-done((bf16[2,64]{1,0:T(2,128)(2,1)S(1)}, bf16[2,64]{1,0:T(2,128)(2,1)S(1)}, u32[]{:S(2)}, u32[]{:S(2)}) %collective-permute-start.1) | collective-permute-done | bytes 288 | tf_op jit(solution)/shard_map/ppermute | solution.py:416
  21.9 1.1 %collective-permute-start.2 = (bf16[2,64]{1,0:T(2,128)(2,1)S(1)}, bf16[2,64]{1,0:T(2,128)(2,1)S(1)}, u32[]{:S(2)}, u32[]{:S(2)}) collective-permute-start(bf16[2,64]{1,0:T(2,128)(2,1)S(1)} %max.10), channel_id=1, source_target_pairs={{0,64},{16,80},{32,96},{48,112},{64,0},{80,16},{96,32},{112,48},{1... | collective-permute-start | bytes 776 | tf_op jit(solution)/shard_map/ppermute | solution.py:416
  23.0 0.8 %pack_weights.1 = (bf16[4,176,128]{2,1,0:T(8,128)(2,1)S(1)}, bf16[4,176,128]{2,1,0:T(8,128)(2,1)S(1)}, bf16[4,176,128]{2,1,0:T(8,128)(2,1)S(1)}, bf16[4,176,128]{2,1,0:T(8,128)(2,1)S(1)}) custom-call(s32[1,64]{1,0:T(1,128)S(1)} %bitcast.50, bf16[2,64,2304]{2,1,0:T(8,128)(2,1)S(1)} %copy-done, bf16[2,64,512]{2,1,0:T(8,128)(2,1)S(1)} %copy-done.1), custom_call_target="tpu_custom_call" | custom-call | flops 46137344 | bytes 3145728 | tf_op jit(solution)/shard_map/pack_weights/pallas_call | solution.py:400
  23.8 2.3 %collective-permute-done.2 = bf16[2,64]{1,0:T(2,128)(2,1)S(1)} collective-permute-done((bf16[2,64]{1,0:T(2,128)(2,1)S(1)}, bf16[2,64]{1,0:T(2,128)(2,1)S(1)}, u32[]{:S(2)}, u32[]{:S(2)}) %collective-permute-start.2) | collective-permute-done | bytes 288 | tf_op jit(solution)/shard_map/ppermute | solution.py:416
  26.1 12.4 %all-to-all-done = bf16[128,2,2816]{2,1,0:T(2,128)(2,1)S(1)} async-done(((bf16[128,2,2816]{2,1,0:T(2,128)(2,1)}), bf16[128,2,2816]{2,1,0:T(2,128)(2,1)S(1)}, u32[]{:S(2)}, u32[]{:S(2)}) %all-to-all-start) | async-done | bytes 1441824 | tf_op jit(solution)/shard_map/all_to_all | solution.py:396
  38.5 0.5 collective-permute-start.3
  39.0 2.6 %collective-permute-start.4 = (bf16[4,176,128]{2,1,0:T(8,128)(2,1)S(1)}, bf16[4,176,128]{2,1,0:T(8,128)(2,1)S(1)}, u32[]{:S(2)}, u32[]{:S(2)}) collective-permute-start(bf16[4,176,128]{2,1,0:T(8,128)(2,1)S(1)} %get-tuple-element.33), channel_id=1, source_target_pairs={{0,2},{1,3},{2,0},{3,1},{4,6},{5,7},{6,4},{7,5},{8,10},{9,11},{10,... | collective-permute-start | bytes 540680 | tf_op jit(solution)/shard_map/ppermute | solution.py:419
  41.6 0.5 collective-permute-start.5
  42.1 8.4 %polar.1 = (bf16[8,704,128]{2,1,0:T(8,128)(2,1)}, f32[4608,128]{1,0:T(8,128)}, f32[1024,128]{1,0:T(8,128)}) custom-call(s32[2,64]{1,0:T(2,128)S(1)} %bitcast.52, bf16[5632,128]{1,0:T(8,128)(2,1)S(1)} %bitcast.48, f32[4608,128]{1,0:T(8,128)} %bitcast.58, f32[1024,128]{1,0:T(8,128)S(1)} %bitcast.54), custom_call_target="tpu_custom_call" | custom-call | flops 4000000000 | bytes 8388608 | tf_op jit(solution)/shard_map/polar/pallas_call | solution.py:423
  50.5 4.7 %all-to-all-start.1 = ((bf16[8,704,128]{2,1,0:T(8,128)(2,1)}), bf16[8,704,128]{2,1,0:T(8,128)(2,1)S(1)}, u32[]{:S(2)}, u32[]{:S(2)}) async-start(bf16[8,704,128]{2,1,0:T(8,128)(2,1)} %get-tuple-element.35), calls=%async_computation.1 | async-start | bytes 2883584 | tf_op jit(solution)/shard_map/all_to_all | solution.py:448
  55.4 0.4 collective-permute-start.6
  55.8 4.7 %collective-permute-start.7 = (bf16[4,176,128]{2,1,0:T(8,128)(2,1)S(1)}, bf16[4,176,128]{2,1,0:T(8,128)(2,1)S(1)}, u32[]{:S(2)}, u32[]{:S(2)}) collective-permute-start(bf16[4,176,128]{2,1,0:T(8,128)(2,1)S(1)} %pad_maximum_fusion.2), channel_id=1, source_target_pairs={{0,8},{1,9},{2,10},{3,11},{4,12},{5,13},{6,14},{7,15},{8,0},{9,1},... | collective-permute-start | bytes 540680 | tf_op jit(solution)/shard_map/ppermute | solution.py:447
  60.5 0.1 collective-permute-start.8
  60.6 3.4 %collective-permute-done.6.rest_1_ = bf16[4,176,128]{2,1,0:T(8,128)(2,1)S(1)} collective-permute-done((bf16[4,176,128]{2,1,0:T(8,128)(2,1)S(1)}, bf16[4,176,128]{2,1,0:T(8,128)(2,1)S(1)}, u32[]{:S(2)}, u32[]{:S(2)}) %collective-permute-start.6) | collective-permute-done | bytes 180256 | tf_op jit(solution)/shard_map/ppermute | solution.py:447
  64.1 4.8 %collective-permute-done.7.rest_2_ = bf16[4,176,128]{2,1,0:T(8,128)(2,1)S(1)} collective-permute-done((bf16[4,176,128]{2,1,0:T(8,128)(2,1)S(1)}, bf16[4,176,128]{2,1,0:T(8,128)(2,1)S(1)}, u32[]{:S(2)}, u32[]{:S(2)}) %collective-permute-start.7) | collective-permute-done | bytes 180256 | tf_op jit(solution)/shard_map/ppermute | solution.py:447
  68.9 5.7 %all-to-all-done.1.polar_ref = bf16[8,704,128]{2,1,0:T(8,128)(2,1)S(1)} async-done(((bf16[8,704,128]{2,1,0:T(8,128)(2,1)}), bf16[8,704,128]{2,1,0:T(8,128)(2,1)S(1)}, u32[]{:S(2)}, u32[]{:S(2)}) %all-to-all-start.1) | async-done | bytes 1441824 | tf_op jit(solution)/shard_map/all_to_all | solution.py:448
  74.6 2.2 %finish.1 = (bf16[2304,128]{1,0:T(8,128)(2,1)}, bf16[512,128]{1,0:T(8,128)(2,1)}) custom-call(s32[2,64]{1,0:T(2,128)S(1)} %bitcast.53, s32[64]{0:T(128)S(1)} %copy-done.2, bf16[2,64]{1,0:T(2,128)(2,1)S(1)} %max.11.peak_ref, bf16[8,704,128]{2,1,0:T(8,128)(2,1)S(1)} %all-to-all-done.1.polar_ref, bf16[4,176,128]{2,1,0:T(8,128)(2,1)S(1)} %pad_maximum_fusion.rest_0_, ...), custom_call_target="tpu_custom_call" | custom-call | flops 10000000 | bytes 4194304 | tf_op jit(solution)/shard_map/finish/pallas_call | solution.py:452
  (23 shorter events, 0.2 us)
Async XLA Ops:
  4.2 11.6 %copy-start.5 = (bf16[1,2,64]{2,1,0:T(2,128)(2,1)S(1)}, bf16[1,2,64]{2,1,0:T(2,128)(2,1)}, u32[]{:S(2)}) copy-start(bf16[1,2,64]{2,1,0:T(2,128)(2,1)} %param.15) | copy-start | bytes 772
  4.2 18.8 %copy-start = (bf16[2,64,2304]{2,1,0:T(8,128)(2,1)S(1)}, bf16[2,64,2304]{2,1,0:T(8,128)(2,1)}, u32[]{:S(2)}) copy-start(bf16[2,64,2304]{2,1,0:T(8,128)(2,1)} %wq_ref.1) | copy-start | bytes 1769476
  4.2 18.8 %copy-start.1 = (bf16[2,64,512]{2,1,0:T(8,128)(2,1)S(1)}, bf16[2,64,512]{2,1,0:T(8,128)(2,1)}, u32[]{:S(2)}) copy-start(bf16[2,64,512]{2,1,0:T(8,128)(2,1)} %wk_ref.1) | copy-start | bytes 393220
  4.2 18.8 %copy-start.2 = (s32[64]{0:T(128)S(1)}, s32[64]{0:T(128)}, u32[]{:S(2)}) copy-start(s32[64]{0:T(128)} %head_ref.1) | copy-start | bytes 772
  4.2 37.9 %copy-start.3 = (s32[64,2,1]{0,2,1:T(1,128)S(1)}, s32[64,2,1]{0,2,1:T(1,128)}, u32[]{:S(2)}) copy-start(s32[64,2,1]{0,2,1:T(1,128)} %param.16) | copy-start | bytes 1540
  4.2 37.9 %copy-start.4 = (f32[2,65536]{1,0:T(2,128)S(1)}, f32[2,65536]{1,0:T(2,128)}, u32[]{:S(2)}) copy-start(f32[2,65536]{1,0:T(2,128)} %param.14) | copy-start | bytes 1572868
  4.2 34.3 %all-to-all-start = ((bf16[128,2,2816]{2,1,0:T(2,128)(2,1)}), bf16[128,2,2816]{2,1,0:T(2,128)(2,1)S(1)}, u32[]{:S(2)}, u32[]{:S(2)}) async-start(bf16[128,2,2816]{2,1,0:T(2,128)(2,1)} %bitcast.55), calls=%async_computation | async-start | bytes 2883584 | tf_op jit(solution)/shard_map/all_to_all | solution.py:396
  15.8 2.0 %collective-permute-start = (bf16[2,64]{1,0:T(2,128)(2,1)S(1)}, bf16[2,64]{1,0:T(2,128)(2,1)S(1)}, u32[]{:S(2)}, u32[]{:S(2)}) collective-permute-start(bf16[2,64]{1,0:T(2,128)(2,1)S(1)} %bitcast.61), channel_id=1, source_target_pairs={{0,16},{16,0},{32,48},{48,32},{64,80},{80,64},{96,112},{112,96},{1... | collective-permute-start | bytes 776 | tf_op jit(solution)/shard_map/ppermute | solution.py:416
  17.7 4.1 %collective-permute-start.1 = (bf16[2,64]{1,0:T(2,128)(2,1)S(1)}, bf16[2,64]{1,0:T(2,128)(2,1)S(1)}, u32[]{:S(2)}, u32[]{:S(2)}) collective-permute-start(bf16[2,64]{1,0:T(2,128)(2,1)S(1)} %bitcast_maximum_fusion), channel_id=1, source_target_pairs={{0,32},{16,48},{32,0},{48,16},{64,96},{80,112},{96,64},{112,80},{1... | collective-permute-start | bytes 776 | tf_op jit(solution)/shard_map/ppermute | solution.py:416
  21.9 4.2 %collective-permute-start.2 = (bf16[2,64]{1,0:T(2,128)(2,1)S(1)}, bf16[2,64]{1,0:T(2,128)(2,1)S(1)}, u32[]{:S(2)}, u32[]{:S(2)}) collective-permute-start(bf16[2,64]{1,0:T(2,128)(2,1)S(1)} %max.10), channel_id=1, source_target_pairs={{0,64},{16,80},{32,96},{48,112},{64,0},{80,16},{96,32},{112,48},{1... | collective-permute-start | bytes 776 | tf_op jit(solution)/shard_map/ppermute | solution.py:416
  38.5 12.0 %collective-permute-start.3 = (bf16[4,176,128]{2,1,0:T(8,128)(2,1)S(1)}, bf16[4,176,128]{2,1,0:T(8,128)(2,1)S(1)}, u32[]{:S(2)}, u32[]{:S(2)}) collective-permute-start(bf16[4,176,128]{2,1,0:T(8,128)(2,1)S(1)} %get-tuple-element.32), channel_id=1, source_target_pairs={{0,1},{1,2},{2,3},{3,0},{4,5},{5,6},{6,7},{7,4},{8,9},{9,10},{10,1... | collective-permute-start | bytes 540680 | tf_op jit(solution)/shard_map/ppermute | solution.py:419
  39.0 11.6 %collective-permute-start.4 = (bf16[4,176,128]{2,1,0:T(8,128)(2,1)S(1)}, bf16[4,176,128]{2,1,0:T(8,128)(2,1)S(1)}, u32[]{:S(2)}, u32[]{:S(2)}) collective-permute-start(bf16[4,176,128]{2,1,0:T(8,128)(2,1)S(1)} %get-tuple-element.33), channel_id=1, source_target_pairs={{0,2},{1,3},{2,0},{3,1},{4,6},{5,7},{6,4},{7,5},{8,10},{9,11},{10,... | collective-permute-start | bytes 540680 | tf_op jit(solution)/shard_map/ppermute | solution.py:419
  41.6 8.9 %collective-permute-start.5 = (bf16[4,176,128]{2,1,0:T(8,128)(2,1)S(1)}, bf16[4,176,128]{2,1,0:T(8,128)(2,1)S(1)}, u32[]{:S(2)}, u32[]{:S(2)}) collective-permute-start(bf16[4,176,128]{2,1,0:T(8,128)(2,1)S(1)} %get-tuple-element.34), channel_id=1, source_target_pairs={{0,3},{1,0},{2,1},{3,2},{4,7},{5,4},{6,5},{7,6},{8,11},{9,8},{10,9... | collective-permute-start | bytes 540680 | tf_op jit(solution)/shard_map/ppermute | solution.py:419
  50.5 24.1 %all-to-all-start.1 = ((bf16[8,704,128]{2,1,0:T(8,128)(2,1)}), bf16[8,704,128]{2,1,0:T(8,128)(2,1)S(1)}, u32[]{:S(2)}, u32[]{:S(2)}) async-start(bf16[8,704,128]{2,1,0:T(8,128)(2,1)} %get-tuple-element.35), calls=%async_computation.1 | async-start | bytes 2883584 | tf_op jit(solution)/shard_map/all_to_all | solution.py:448
  55.4 8.7 %collective-permute-start.6 = (bf16[4,176,128]{2,1,0:T(8,128)(2,1)S(1)}, bf16[4,176,128]{2,1,0:T(8,128)(2,1)S(1)}, u32[]{:S(2)}, u32[]{:S(2)}) collective-permute-start(bf16[4,176,128]{2,1,0:T(8,128)(2,1)S(1)} %pad_maximum_fusion.1), channel_id=1, source_target_pairs={{0,4},{1,5},{2,6},{3,7},{4,8},{5,9},{6,10},{7,11},{8,12},{9,13},{1... | collective-permute-start | bytes 540680 | tf_op jit(solution)/shard_map/ppermute | solution.py:447
  55.8 13.1 %collective-permute-start.7 = (bf16[4,176,128]{2,1,0:T(8,128)(2,1)S(1)}, bf16[4,176,128]{2,1,0:T(8,128)(2,1)S(1)}, u32[]{:S(2)}, u32[]{:S(2)}) collective-permute-start(bf16[4,176,128]{2,1,0:T(8,128)(2,1)S(1)} %pad_maximum_fusion.2), channel_id=1, source_target_pairs={{0,8},{1,9},{2,10},{3,11},{4,12},{5,13},{6,14},{7,15},{8,0},{9,1},... | collective-permute-start | bytes 540680 | tf_op jit(solution)/shard_map/ppermute | solution.py:447
  60.5 8.4 %collective-permute-start.8 = (bf16[4,176,128]{2,1,0:T(8,128)(2,1)S(1)}, bf16[4,176,128]{2,1,0:T(8,128)(2,1)S(1)}, u32[]{:S(2)}, u32[]{:S(2)}) collective-permute-start(bf16[4,176,128]{2,1,0:T(8,128)(2,1)S(1)} %pad_maximum_fusion.3), channel_id=1, source_target_pairs={{0,12},{1,13},{2,14},{3,15},{4,0},{5,1},{6,2},{7,3},{8,4},{9,5},{1... | collective-permute-start | bytes 540680 | tf_op jit(solution)/shard_map/ppermute | solution.py:447

commit v3 on v2

--- a/solution.py
+++ b/solution.py
@@ -414,8 +414,9 @@
     reach = 1
     while reach < owners:
         peaks = jnp.maximum(peaks, lax.ppermute(peaks, "dp", [(i, i ^ reach) for i in range(owners)]))
+        if reach == 2:
+            peaks, by_y = lax.optimization_barrier((peaks, by_y))
         reach *= 2
-    owned, by_y, peaks = lax.optimization_barrier((owned, by_y, peaks))
     by_y = [by_y[0]] + [lax.ppermute(by_y[s], "mp", along_y[s]) for s in range(1, SIDE)]
     fq = DQ * RQ // LANE
     fk = DN * RK // LANE

time: 77.7 us -> 73.8 us (0.950)
  waiting for transfers between devices: 32.8 us -> 24.9 us
  starting transfers between devices: 28.1 us -> 32.7 us
    ppermute x3, waiting for transfers between devices: 6.45 us -> 15.1 us  [body(): lax.ppermute(peaks, 'dp', [(i, i ^ reach) for i in range(owners)])]
    ppermute x3, waiting for transfers between devices: 8.29 us -> 0.01 us  [body(): lax.ppermute(by_x[t], 'mp', along_x[t])]
    all_to_all x1, waiting for transfers between devices: 5.67 us -> 0.01 us  [body(): back = lax.all_to_all(polar, 'dp', split_axis=0, concat_axis=0, tiled=True)]
    ppermute x3, starting transfers between devices: 3.64 us -> 6.84 us  [body(): lax.ppermute(by_y[s], 'mp', along_y[s])]
    all_to_all x1, waiting for transfers between devices: 12.4 us -> 9.76 us  [body(): lax.all_to_all(packed, ('dp', 'mp'), split_axis=0, concat_axis=0, tiled=T...]
    ppermute x3, starting transfers between devices: 3.06 us -> 4.84 us  [body(): lax.ppermute(peaks, 'dp', [(i, i ^ reach) for i in range(owners)])]
  transfers between devices with their start and end apart: 11 -> 11, of which waited for: 7 -> 4; matrix products, arithmetic and copies ran while one was open for 0% -> 0% of each run, Pallas kernels for 12% -> 12%
where the time goes in v3:
time: 73.8 us; the launch traced here: 73.5 us
  starting transfers between devices  32.7 us (44%)
  waiting for transfers between devices  24.9 us (34%)
  Pallas kernels  14.9 us (20%)
  between operations  0.81 us (1%)
    ppermute x3, waiting for transfers between devices, body(): lax.ppermute(peaks, 'dp', [(i, i ^ reach) for i in range(owners)])  15.1 us
    all_to_all x1, starting transfers between devices, body(): lax.all_to_all(packed, ('dp', 'mp'), split_axis=0, concat_axis=0, tiled=T...  11.5 us
    all_to_all x1, waiting for transfers between devices, body(): lax.all_to_all(packed, ('dp', 'mp'), split_axis=0, concat_axis=0, tiled=T...  9.76 us
    pallas_call x1, Pallas kernels, body(): call(functools.partial(polar_kernel, **kw), 'polar', (shape((owners, slot...  8.37 us
    ppermute x3, starting transfers between devices, body(): lax.ppermute(by_y[s], 'mp', along_y[s])  6.84 us
    all_to_all x1, starting transfers between devices, body(): back = lax.all_to_all(polar, 'dp', split_axis=0, concat_axis=0, tiled=True)  4.94 us
    ppermute x3, starting transfers between devices, body(): lax.ppermute(peaks, 'dp', [(i, i ^ reach) for i in range(owners)])  4.84 us
    ppermute x3, starting transfers between devices, body(): lax.ppermute(by_x[t], 'mp', along_x[t])  4.57 us
  transfers between devices with their start and end apart: 11, of which 4 were waited for; matrix products, arithmetic and copies ran while one was open for 0% of the time, Pallas kernels for 12%

profile of v3, /device:TPU:1, one launch (start us, length us, event | category | flops | bytes accessed | tf_op | source)
XLA Modules:
  0.0 73.5 jit_solution(3135173138247013541)
XLA Ops:
  0.6 3.5 %pack_grads.1 = bf16[5632,128]{1,0:T(8,128)(2,1)} custom-call(s32[2,64]{1,0:T(2,128)} %bitcast.51, s32[1,64]{1,0:T(1,128)} %bitcast.49, bf16[128,2304]{1,0:T(8,128)(2,1)} %bitcast.56, bf16[128,512]{1,0:T(8,128)(2,1)} %bitcast.57), custom_call_target="tpu_custom_call" | custom-call | flops 184549376 | bytes 3145728 | tf_op jit(solution)/shard_map/pack_grads/pallas_call | solution.py:373
  4.2 0.0 copy-start.5
  4.2 0.0 copy-start
  4.2 0.0 copy-start.1
  4.2 0.0 copy-start.2
  4.2 0.0 copy-start.3
  4.2 0.0 copy-start.4
  4.2 11.5 %all-to-all-start = ((bf16[128,2,2816]{2,1,0:T(2,128)(2,1)}), bf16[128,2,2816]{2,1,0:T(2,128)(2,1)S(1)}, u32[]{:S(2)}, u32[]{:S(2)}) async-start(bf16[128,2,2816]{2,1,0:T(2,128)(2,1)} %bitcast.55), calls=%async_computation | async-start | bytes 2883584 | tf_op jit(solution)/shard_map/all_to_all | solution.py:396
  15.8 1.1 %collective-permute-start = (bf16[2,64]{1,0:T(2,128)(2,1)S(1)}, bf16[2,64]{1,0:T(2,128)(2,1)S(1)}, u32[]{:S(2)}, u32[]{:S(2)}) collective-permute-start(bf16[2,64]{1,0:T(2,128)(2,1)S(1)} %bitcast.61), channel_id=1, source_target_pairs={{0,16},{16,0},{32,48},{48,32},{64,80},{80,64},{96,112},{112,96},{1... | collective-permute-start | bytes 776 | tf_op jit(solution)/shard_map/ppermute | solution.py:416
  16.9 0.8 %collective-permute-done = bf16[2,64]{1,0:T(2,128)(2,1)S(1)} collective-permute-done((bf16[2,64]{1,0:T(2,128)(2,1)S(1)}, bf16[2,64]{1,0:T(2,128)(2,1)S(1)}, u32[]{:S(2)}, u32[]{:S(2)}) %collective-permute-start) | collective-permute-done | bytes 288 | tf_op jit(solution)/shard_map/ppermute | solution.py:416
  17.7 0.8 %collective-permute-start.1 = (bf16[2,64]{1,0:T(2,128)(2,1)S(1)}, bf16[2,64]{1,0:T(2,128)(2,1)S(1)}, u32[]{:S(2)}, u32[]{:S(2)}) collective-permute-start(bf16[2,64]{1,0:T(2,128)(2,1)S(1)} %bitcast_maximum_fusion), channel_id=1, source_target_pairs={{0,32},{16,48},{32,0},{48,16},{64,96},{80,112},{96,64},{112,80},{1... | collective-permute-start | bytes 776 | tf_op jit(solution)/shard_map/ppermute | solution.py:416
  18.5 0.8 %pack_weights.1 = (bf16[4,176,128]{2,1,0:T(8,128)(2,1)S(1)}, bf16[4,176,128]{2,1,0:T(8,128)(2,1)S(1)}, bf16[4,176,128]{2,1,0:T(8,128)(2,1)S(1)}, bf16[4,176,128]{2,1,0:T(8,128)(2,1)S(1)}) custom-call(s32[1,64]{1,0:T(1,128)S(1)} %bitcast.50, bf16[2,64,2304]{2,1,0:T(8,128)(2,1)S(1)} %copy-done, bf16[2,64,512]{2,1,0:T(8,128)(2,1)S(1)} %copy-done.1), custom_call_target="tpu_custom_call" | custom-call | flops 46137344 | bytes 3145728 | tf_op jit(solution)/shard_map/pack_weights/pallas_call | solution.py:400
  19.3 2.6 %collective-permute-done.1 = bf16[2,64]{1,0:T(2,128)(2,1)S(1)} collective-permute-done((bf16[2,64]{1,0:T(2,128)(2,1)S(1)}, bf16[2,64]{1,0:T(2,128)(2,1)S(1)}, u32[]{:S(2)}, u32[]{:S(2)}) %collective-permute-start.1) | collective-permute-done | bytes 288 | tf_op jit(solution)/shard_map/ppermute | solution.py:416
  21.9 5.2 %collective-permute-start.4 = (bf16[4,176,128]{2,1,0:T(8,128)(2,1)S(1)}, bf16[4,176,128]{2,1,0:T(8,128)(2,1)S(1)}, u32[]{:S(2)}, u32[]{:S(2)}) collective-permute-start(bf16[4,176,128]{2,1,0:T(8,128)(2,1)S(1)} %get-tuple-element.31), channel_id=1, source_target_pairs={{0,2},{1,3},{2,0},{3,1},{4,6},{5,7},{6,4},{7,5},{8,10},{9,11},{10,... | collective-permute-start | bytes 540680 | tf_op jit(solution)/shard_map/ppermute | solution.py:420
  27.1 1.6 %collective-permute-start.5 = (bf16[4,176,128]{2,1,0:T(8,128)(2,1)S(1)}, bf16[4,176,128]{2,1,0:T(8,128)(2,1)S(1)}, u32[]{:S(2)}, u32[]{:S(2)}) collective-permute-start(bf16[4,176,128]{2,1,0:T(8,128)(2,1)S(1)} %get-tuple-element.32), channel_id=1, source_target_pairs={{0,3},{1,0},{2,1},{3,2},{4,7},{5,4},{6,5},{7,6},{8,11},{9,8},{10,9... | collective-permute-start | bytes 540680 | tf_op jit(solution)/shard_map/ppermute | solution.py:420
  28.7 9.8 %all-to-all-done = bf16[128,2,2816]{2,1,0:T(2,128)(2,1)S(1)} async-done(((bf16[128,2,2816]{2,1,0:T(2,128)(2,1)}), bf16[128,2,2816]{2,1,0:T(2,128)(2,1)S(1)}, u32[]{:S(2)}, u32[]{:S(2)}) %all-to-all-start) | async-done | bytes 1441824 | tf_op jit(solution)/shard_map/all_to_all | solution.py:396
  38.5 8.4 %polar.1 = (bf16[8,704,128]{2,1,0:T(8,128)(2,1)}, f32[4608,128]{1,0:T(8,128)}, f32[1024,128]{1,0:T(8,128)}) custom-call(s32[2,64]{1,0:T(2,128)S(1)} %bitcast.52, bf16[5632,128]{1,0:T(8,128)(2,1)S(1)} %bitcast.48, f32[4608,128]{1,0:T(8,128)} %bitcast.58, f32[1024,128]{1,0:T(8,128)S(1)} %bitcast.54), custom_call_target="tpu_custom_call" | custom-call | flops 4000000000 | bytes 8388608 | tf_op jit(solution)/shard_map/polar/pallas_call | solution.py:424
  46.9 4.9 %all-to-all-start.1 = ((bf16[8,704,128]{2,1,0:T(8,128)(2,1)}), bf16[8,704,128]{2,1,0:T(8,128)(2,1)S(1)}, u32[]{:S(2)}, u32[]{:S(2)}) async-start(bf16[8,704,128]{2,1,0:T(8,128)(2,1)} %get-tuple-element.33), calls=%async_computation.1 | async-start | bytes 2883584 | tf_op jit(solution)/shard_map/all_to_all | solution.py:449
  51.9 0.4 collective-permute-start.6
  52.4 3.0 %collective-permute-start.7 = (bf16[4,176,128]{2,1,0:T(8,128)(2,1)S(1)}, bf16[4,176,128]{2,1,0:T(8,128)(2,1)S(1)}, u32[]{:S(2)}, u32[]{:S(2)}) collective-permute-start(bf16[4,176,128]{2,1,0:T(8,128)(2,1)S(1)} %pad_maximum_fusion.2), channel_id=1, source_target_pairs={{0,8},{1,9},{2,10},{3,11},{4,12},{5,13},{6,14},{7,15},{8,0},{9,1},... | collective-permute-start | bytes 540680 | tf_op jit(solution)/shard_map/ppermute | solution.py:448
  55.4 1.2 %collective-permute-start.8 = (bf16[4,176,128]{2,1,0:T(8,128)(2,1)S(1)}, bf16[4,176,128]{2,1,0:T(8,128)(2,1)S(1)}, u32[]{:S(2)}, u32[]{:S(2)}) collective-permute-start(bf16[4,176,128]{2,1,0:T(8,128)(2,1)S(1)} %pad_maximum_fusion.3), channel_id=1, source_target_pairs={{0,12},{1,13},{2,14},{3,15},{4,0},{5,1},{6,2},{7,3},{8,4},{9,5},{1... | collective-permute-start | bytes 540680 | tf_op jit(solution)/shard_map/ppermute | solution.py:448
  56.6 2.9 %collective-permute-start.2 = (bf16[2,64]{1,0:T(2,128)(2,1)S(1)}, bf16[2,64]{1,0:T(2,128)(2,1)S(1)}, u32[]{:S(2)}, u32[]{:S(2)}) collective-permute-start(bf16[2,64]{1,0:T(2,128)(2,1)S(1)} %max.10), channel_id=1, source_target_pairs={{0,64},{16,80},{32,96},{48,112},{64,0},{80,16},{96,32},{112,48},{1... | collective-permute-start | bytes 776 | tf_op jit(solution)/shard_map/ppermute | solution.py:416
  59.5 11.7 %collective-permute-done.2 = bf16[2,64]{1,0:T(2,128)(2,1)S(1)} collective-permute-done((bf16[2,64]{1,0:T(2,128)(2,1)S(1)}, bf16[2,64]{1,0:T(2,128)(2,1)S(1)}, u32[]{:S(2)}, u32[]{:S(2)}) %collective-permute-start.2) | collective-permute-done | bytes 288 | tf_op jit(solution)/shard_map/ppermute | solution.py:416
  71.3 2.2 %finish.1 = (bf16[2304,128]{1,0:T(8,128)(2,1)}, bf16[512,128]{1,0:T(8,128)(2,1)}) custom-call(s32[2,64]{1,0:T(2,128)S(1)} %bitcast.53, s32[64]{0:T(128)S(1)} %copy-done.2, bf16[2,64]{1,0:T(2,128)(2,1)S(1)} %max.11.peak_ref, bf16[8,704,128]{2,1,0:T(8,128)(2,1)S(1)} %all-to-all-done.1.polar_ref, bf16[4,176,128]{2,1,0:T(8,128)(2,1)S(1)} %pad_maximum_fusion.rest_0_, ...), custom_call_target="tpu_custom_call" | custom-call | flops 10000000 | bytes 4194304 | tf_op jit(solution)/shard_map/finish/pallas_call | solution.py:453
  (23 shorter events, 0.2 us)
Async XLA Ops:
  4.2 11.6 %copy-start.5 = (bf16[1,2,64]{2,1,0:T(2,128)(2,1)S(1)}, bf16[1,2,64]{2,1,0:T(2,128)(2,1)}, u32[]{:S(2)}) copy-start(bf16[1,2,64]{2,1,0:T(2,128)(2,1)} %param.15) | copy-start | bytes 772
  4.2 14.4 %copy-start = (bf16[2,64,2304]{2,1,0:T(8,128)(2,1)S(1)}, bf16[2,64,2304]{2,1,0:T(8,128)(2,1)}, u32[]{:S(2)}) copy-start(bf16[2,64,2304]{2,1,0:T(8,128)(2,1)} %wq_ref.1) | copy-start | bytes 1769476
  4.2 14.4 %copy-start.1 = (bf16[2,64,512]{2,1,0:T(8,128)(2,1)S(1)}, bf16[2,64,512]{2,1,0:T(8,128)(2,1)}, u32[]{:S(2)}) copy-start(bf16[2,64,512]{2,1,0:T(8,128)(2,1)} %wk_ref.1) | copy-start | bytes 393220
  4.2 14.3 %copy-start.2 = (s32[64]{0:T(128)S(1)}, s32[64]{0:T(128)}, u32[]{:S(2)}) copy-start(s32[64]{0:T(128)} %head_ref.1) | copy-start | bytes 772
  4.2 34.3 %copy-start.3 = (s32[64,2,1]{0,2,1:T(1,128)S(1)}, s32[64,2,1]{0,2,1:T(1,128)}, u32[]{:S(2)}) copy-start(s32[64,2,1]{0,2,1:T(1,128)} %param.16) | copy-start | bytes 1540
  4.2 34.3 %copy-start.4 = (f32[2,65536]{1,0:T(2,128)S(1)}, f32[2,65536]{1,0:T(2,128)}, u32[]{:S(2)}) copy-start(f32[2,65536]{1,0:T(2,128)} %param.14) | copy-start | bytes 1572868
  4.2 34.3 %all-to-all-start = ((bf16[128,2,2816]{2,1,0:T(2,128)(2,1)}), bf16[128,2,2816]{2,1,0:T(2,128)(2,1)S(1)}, u32[]{:S(2)}, u32[]{:S(2)}) async-start(bf16[128,2,2816]{2,1,0:T(2,128)(2,1)} %bitcast.55), calls=%async_computation | async-start | bytes 2883584 | tf_op jit(solution)/shard_map/all_to_all | solution.py:396
  15.8 2.0 %collective-permute-start = (bf16[2,64]{1,0:T(2,128)(2,1)S(1)}, bf16[2,64]{1,0:T(2,128)(2,1)S(1)}, u32[]{:S(2)}, u32[]{:S(2)}) collective-permute-start(bf16[2,64]{1,0:T(2,128)(2,1)S(1)} %bitcast.61), channel_id=1, source_target_pairs={{0,16},{16,0},{32,48},{48,32},{64,80},{80,64},{96,112},{112,96},{1... | collective-permute-start | bytes 776 | tf_op jit(solution)/shard_map/ppermute | solution.py:416
  17.7 4.1 %collective-permute-start.1 = (bf16[2,64]{1,0:T(2,128)(2,1)S(1)}, bf16[2,64]{1,0:T(2,128)(2,1)S(1)}, u32[]{:S(2)}, u32[]{:S(2)}) collective-permute-start(bf16[2,64]{1,0:T(2,128)(2,1)S(1)} %bitcast_maximum_fusion), channel_id=1, source_target_pairs={{0,32},{16,48},{32,0},{48,16},{64,96},{80,112},{96,64},{112,80},{1... | collective-permute-start | bytes 776 | tf_op jit(solution)/shard_map/ppermute | solution.py:416
  21.9 25.0 %collective-permute-start.3 = (bf16[4,176,128]{2,1,0:T(8,128)(2,1)S(1)}, bf16[4,176,128]{2,1,0:T(8,128)(2,1)S(1)}, u32[]{:S(2)}, u32[]{:S(2)}) collective-permute-start(bf16[4,176,128]{2,1,0:T(8,128)(2,1)S(1)} %get-tuple-element.30), channel_id=1, source_target_pairs={{0,1},{1,2},{2,3},{3,0},{4,5},{5,6},{6,7},{7,4},{8,9},{9,10},{10,1... | collective-permute-start | bytes 540680 | tf_op jit(solution)/shard_map/ppermute | solution.py:420
  21.9 25.0 %collective-permute-start.4 = (bf16[4,176,128]{2,1,0:T(8,128)(2,1)S(1)}, bf16[4,176,128]{2,1,0:T(8,128)(2,1)S(1)}, u32[]{:S(2)}, u32[]{:S(2)}) collective-permute-start(bf16[4,176,128]{2,1,0:T(8,128)(2,1)S(1)} %get-tuple-element.31), channel_id=1, source_target_pairs={{0,2},{1,3},{2,0},{3,1},{4,6},{5,7},{6,4},{7,5},{8,10},{9,11},{10,... | collective-permute-start | bytes 540680 | tf_op jit(solution)/shard_map/ppermute | solution.py:420
  27.1 19.8 %collective-permute-start.5 = (bf16[4,176,128]{2,1,0:T(8,128)(2,1)S(1)}, bf16[4,176,128]{2,1,0:T(8,128)(2,1)S(1)}, u32[]{:S(2)}, u32[]{:S(2)}) collective-permute-start(bf16[4,176,128]{2,1,0:T(8,128)(2,1)S(1)} %get-tuple-element.32), channel_id=1, source_target_pairs={{0,3},{1,0},{2,1},{3,2},{4,7},{5,4},{6,5},{7,6},{8,11},{9,8},{10,9... | collective-permute-start | bytes 540680 | tf_op jit(solution)/shard_map/ppermute | solution.py:420
  46.9 24.3 %all-to-all-start.1 = ((bf16[8,704,128]{2,1,0:T(8,128)(2,1)}), bf16[8,704,128]{2,1,0:T(8,128)(2,1)S(1)}, u32[]{:S(2)}, u32[]{:S(2)}) async-start(bf16[8,704,128]{2,1,0:T(8,128)(2,1)} %get-tuple-element.33), calls=%async_computation.1 | async-start | bytes 2883584 | tf_op jit(solution)/shard_map/all_to_all | solution.py:449
  51.9 19.3 %collective-permute-start.6 = (bf16[4,176,128]{2,1,0:T(8,128)(2,1)S(1)}, bf16[4,176,128]{2,1,0:T(8,128)(2,1)S(1)}, u32[]{:S(2)}, u32[]{:S(2)}) collective-permute-start(bf16[4,176,128]{2,1,0:T(8,128)(2,1)S(1)} %pad_maximum_fusion.1), channel_id=1, source_target_pairs={{0,4},{1,5},{2,6},{3,7},{4,8},{5,9},{6,10},{7,11},{8,12},{9,13},{1... | collective-permute-start | bytes 540680 | tf_op jit(solution)/shard_map/ppermute | solution.py:448
  52.4 18.9 %collective-permute-start.7 = (bf16[4,176,128]{2,1,0:T(8,128)(2,1)S(1)}, bf16[4,176,128]{2,1,0:T(8,128)(2,1)S(1)}, u32[]{:S(2)}, u32[]{:S(2)}) collective-permute-start(bf16[4,176,128]{2,1,0:T(8,128)(2,1)S(1)} %pad_maximum_fusion.2), channel_id=1, source_target_pairs={{0,8},{1,9},{2,10},{3,11},{4,12},{5,13},{6,14},{7,15},{8,0},{9,1},... | collective-permute-start | bytes 540680 | tf_op jit(solution)/shard_map/ppermute | solution.py:448
  55.4 15.9 %collective-permute-start.8 = (bf16[4,176,128]{2,1,0:T(8,128)(2,1)S(1)}, bf16[4,176,128]{2,1,0:T(8,128)(2,1)S(1)}, u32[]{:S(2)}, u32[]{:S(2)}) collective-permute-start(bf16[4,176,128]{2,1,0:T(8,128)(2,1)S(1)} %pad_maximum_fusion.3), channel_id=1, source_target_pairs={{0,12},{1,13},{2,14},{3,15},{4,0},{5,1},{6,2},{7,3},{8,4},{9,5},{1... | collective-permute-start | bytes 540680 | tf_op jit(solution)/shard_map/ppermute | solution.py:448
  56.6 14.6 %collective-permute-start.2 = (bf16[2,64]{1,0:T(2,128)(2,1)S(1)}, bf16[2,64]{1,0:T(2,128)(2,1)S(1)}, u32[]{:S(2)}, u32[]{:S(2)}) collective-permute-start(bf16[2,64]{1,0:T(2,128)(2,1)S(1)} %max.10), channel_id=1, source_target_pairs={{0,64},{16,80},{32,96},{48,112},{64,0},{80,16},{96,32},{112,48},{1... | collective-permute-start | bytes 776 | tf_op jit(solution)/shard_map/ppermute | solution.py:416

commit v4 on v3

--- a/solution.py
+++ b/solution.py
@@ -43,14 +43,34 @@
 
 
 def pack_grads_kernel(
-    owner_ref, head_ref, gq_far, gk_far, out_far, gq_ref, gk_ref, stage, out_ref, sems, *, ranks, owners, slots
+    owner_far,
+    head_far,
+    gq_far,
+    gk_far,
+    out_far,
+    owner_ref,
+    head_ref,
+    gq_ref,
+    gk_ref,
+    stage,
+    out_ref,
+    sems,
+    sems_send,
+    *,
+    ranks,
+    owners,
+    slots,
 ):
     copies = [
-        pltpu.make_async_copy(gq_far, gq_ref, sems.at[0]),
-        pltpu.make_async_copy(gk_far, gk_ref, sems.at[1]),
+        pltpu.make_async_copy(src, dst, sems.at[j])
+        for j, (src, dst) in enumerate(
+            ((owner_far, owner_ref), (head_far, head_ref), (gq_far, gq_ref), (gk_far, gk_ref))
+        )
     ]
     for copy in copies:
         copy.start()
+    for copy in copies[:2]:
+        copy.wait()
     layers, heads = owner_ref.shape
     devices = ranks * owners
     per_rank = heads // ranks
@@ -76,7 +96,7 @@
         for slot in range(slots):
             chosen = (iota((devices, heads), 0) * slots + slot == target).astype(bf16)
             picks[slot][layer] = dot(chosen, heads_of, ((1,), (1,))).astype(bf16)
-    for copy in copies:
+    for copy in copies[2:]:
         copy.wait()
     for slot in range(slots):
         pick = jnp.concatenate(picks[slot], axis=1)
@@ -87,11 +107,12 @@
                     :, tile * LANE : (tile + 1) * LANE
                 ]
     sends = []
-    count = out_ref.shape[0] // owners
-    for owner in range(owners):
-        at = pl.ds(owner * count, count)
+    parts = sems_send.shape[0]
+    count = out_ref.shape[0] // parts
+    for part in range(parts):
+        at = pl.ds(part * count, count)
         out_ref[at, :] = stage[at, :].astype(bf16)
-        sends.append(pltpu.make_async_copy(out_ref.at[at, :], out_far.at[at, :], sems.at[2 + owner]))
+        sends.append(pltpu.make_async_copy(out_ref.at[at, :], out_far.at[at, :], sems_send.at[part]))
         sends[-1].start()
     for copy in sends:
         copy.wait()
@@ -374,13 +395,16 @@
         functools.partial(pack_grads_kernel, **kw),
         "pack_grads",
         shape((devices * tiles * slots, LANE), bf16),
-        [VMEM, VMEM, HBM, HBM],
+        [HBM] * 4,
         [
+            pltpu.VMEM(owner_2d.shape, jnp.int32),
+            pltpu.VMEM(head_row.shape, jnp.int32),
             pltpu.VMEM((layers * heads, piece_q), bf16),
             pltpu.VMEM((layers * heads, piece_k), bf16),
             pltpu.VMEM((devices * tiles * slots, LANE), f32),
             pltpu.VMEM((devices * tiles * slots, LANE), bf16),
-            pltpu.SemaphoreType.DMA((2 + owners,)),
+            pltpu.SemaphoreType.DMA((4,)),
+            pltpu.SemaphoreType.DMA((4,)),
         ],
         2 * 256 * 128 * 2816,
         3 * 2**20,
@@ -411,16 +435,14 @@
     ]
     along_x = [[(i, (i + t * SIDE) % ranks) for i in range(ranks)] for t in range(SIDE)]
     peaks = logit_peak[0]
-    reach = 1
-    while reach < owners:
+    for reach in (1, 4, 2):
         peaks = jnp.maximum(peaks, lax.ppermute(peaks, "dp", [(i, i ^ reach) for i in range(owners)]))
-        if reach == 2:
+        if reach == 4:
             peaks, by_y = lax.optimization_barrier((peaks, by_y))
-        reach *= 2
     by_y = [by_y[0]] + [lax.ppermute(by_y[s], "mp", along_y[s]) for s in range(1, SIDE)]
     fq = DQ * RQ // LANE
     fk = DN * RK // LANE
-    parts = 4
+    parts = 2
     polar, next_q, next_k = call(
         functools.partial(polar_kernel, **kw),
         "polar",

time: 73.8 us -> 73.1 us (level)
    all_to_all x1, waiting for transfers between devices: 0.01 us -> 1.47 us  [body(): back = lax.all_to_all(polar, 'dp', split_axis=0, concat_axis=0, tiled=True)]
    ppermute x3, waiting for transfers between devices: 15.1 us -> 13.8 us  [body(): lax.ppermute(peaks, 'dp', [(i, i ^ reach) for i in range(owners)])]
  transfers between devices with their start and end apart: 11 -> 11, of which waited for: 4 -> 5; matrix products, arithmetic and copies ran while one was open for 0% -> 0% of each run, Pallas kernels for 12% -> 13%
where the time goes in v4:
time: 73.1 us; the launch traced here: 72.9 us
  starting transfers between devices  32.5 us (44%)
  waiting for transfers between devices  25 us (34%)
  Pallas kernels  14.4 us (20%)
  between operations  0.8 us (1%)
    ppermute x3, waiting for transfers between devices, body(): lax.ppermute(peaks, 'dp', [(i, i ^ reach) for i in range(owners)])  13.8 us
    all_to_all x1, starting transfers between devices, body(): lax.all_to_all(packed, ('dp', 'mp'), split_axis=0, concat_axis=0, tiled=T...  11.5 us
    all_to_all x1, waiting for transfers between devices, body(): lax.all_to_all(packed, ('dp', 'mp'), split_axis=0, concat_axis=0, tiled=T...  9.66 us
    pallas_call x1, Pallas kernels, body(): call(functools.partial(polar_kernel, **kw), 'polar', (shape((owners, slot...  8.5 us
    ppermute x3, starting transfers between devices, body(): lax.ppermute(by_y[s], 'mp', along_y[s])  6.9 us
    ppermute x3, starting transfers between devices, body(): lax.ppermute(peaks, 'dp', [(i, i ^ reach) for i in range(owners)])  5.11 us
    all_to_all x1, starting transfers between devices, body(): back = lax.all_to_all(polar, 'dp', split_axis=0, concat_axis=0, tiled=True)  4.94 us
    ppermute x3, starting transfers between devices, body(): lax.ppermute(by_x[t], 'mp', along_x[t])  4.05 us
  transfers between devices with their start and end apart: 11, of which 5 were waited for; matrix products, arithmetic and copies ran while one was open for 0% of the time, Pallas kernels for 13%

profile of v4, /device:TPU:1, one launch (start us, length us, event | category | flops | bytes accessed | tf_op | source)
XLA Modules:
  0.0 72.9 jit_solution(6867681782721248630)
XLA Ops:
  0.6 2.9 %pack_grads.1 = bf16[5632,128]{1,0:T(8,128)(2,1)} custom-call(s32[2,64]{1,0:T(2,128)} %bitcast.51, s32[1,64]{1,0:T(1,128)} %bitcast.49, bf16[128,2304]{1,0:T(8,128)(2,1)} %bitcast.56, bf16[128,512]{1,0:T(8,128)(2,1)} %bitcast.57), custom_call_target="tpu_custom_call" | custom-call | flops 184549376 | bytes 3145728 | tf_op jit(solution)/shard_map/pack_grads/pallas_call | solution.py:394
  3.5 0.0 copy-start.5
  3.5 0.0 copy-start
  3.5 0.0 copy-start.1
  3.5 0.0 copy-start.2
  3.6 0.0 copy-start.3
  3.6 11.5 %all-to-all-start = ((bf16[128,2,2816]{2,1,0:T(2,128)(2,1)}), bf16[128,2,2816]{2,1,0:T(2,128)(2,1)S(1)}, u32[]{:S(2)}, u32[]{:S(2)}) async-start(bf16[128,2,2816]{2,1,0:T(2,128)(2,1)} %bitcast.55), calls=%async_computation | async-start | bytes 2883584 | tf_op jit(solution)/shard_map/all_to_all | solution.py:420
  15.1 1.1 %collective-permute-start = (bf16[2,64]{1,0:T(2,128)(2,1)S(1)}, bf16[2,64]{1,0:T(2,128)(2,1)S(1)}, u32[]{:S(2)}, u32[]{:S(2)}) collective-permute-start(bf16[2,64]{1,0:T(2,128)(2,1)S(1)} %bitcast.61), channel_id=1, source_target_pairs={{0,16},{16,0},{32,48},{48,32},{64,80},{80,64},{96,112},{112,96},{1... | collective-permute-start | bytes 776 | tf_op jit(solution)/shard_map/ppermute | solution.py:439
  16.3 0.8 %collective-permute-done = bf16[2,64]{1,0:T(2,128)(2,1)S(1)} collective-permute-done((bf16[2,64]{1,0:T(2,128)(2,1)S(1)}, bf16[2,64]{1,0:T(2,128)(2,1)S(1)}, u32[]{:S(2)}, u32[]{:S(2)}) %collective-permute-start) | collective-permute-done | bytes 288 | tf_op jit(solution)/shard_map/ppermute | solution.py:439
  17.1 2.6 %collective-permute-start.1 = (bf16[2,64]{1,0:T(2,128)(2,1)S(1)}, bf16[2,64]{1,0:T(2,128)(2,1)S(1)}, u32[]{:S(2)}, u32[]{:S(2)}) collective-permute-start(bf16[2,64]{1,0:T(2,128)(2,1)S(1)} %bitcast_maximum_fusion), channel_id=1, source_target_pairs={{0,64},{16,80},{32,96},{48,112},{64,0},{80,16},{96,32},{112,48},{1... | collective-permute-start | bytes 776 | tf_op jit(solution)/shard_map/ppermute | solution.py:439
  19.7 0.8 %pack_weights.1 = (bf16[4,176,128]{2,1,0:T(8,128)(2,1)S(1)}, bf16[4,176,128]{2,1,0:T(8,128)(2,1)S(1)}, bf16[4,176,128]{2,1,0:T(8,128)(2,1)S(1)}, bf16[4,176,128]{2,1,0:T(8,128)(2,1)S(1)}) custom-call(s32[1,64]{1,0:T(1,128)S(1)} %bitcast.50, bf16[2,64,2304]{2,1,0:T(8,128)(2,1)S(1)} %copy-done, bf16[2,64,512]{2,1,0:T(8,128)(2,1)S(1)} %copy-done.1), custom_call_target="tpu_custom_call" | custom-call | flops 46137344 | bytes 3145728 | tf_op jit(solution)/shard_map/pack_weights/pallas_call | solution.py:424
  20.4 0.8 %collective-permute-done.1 = bf16[2,64]{1,0:T(2,128)(2,1)S(1)} collective-permute-done((bf16[2,64]{1,0:T(2,128)(2,1)S(1)}, bf16[2,64]{1,0:T(2,128)(2,1)S(1)}, u32[]{:S(2)}, u32[]{:S(2)}) %collective-permute-start.1) | collective-permute-done | bytes 288 | tf_op jit(solution)/shard_map/ppermute | solution.py:439
  21.3 0.9 %collective-permute-start.3 = (bf16[4,176,128]{2,1,0:T(8,128)(2,1)S(1)}, bf16[4,176,128]{2,1,0:T(8,128)(2,1)S(1)}, u32[]{:S(2)}, u32[]{:S(2)}) collective-permute-start(bf16[4,176,128]{2,1,0:T(8,128)(2,1)S(1)} %get-tuple-element.30), channel_id=1, source_target_pairs={{0,1},{1,2},{2,3},{3,0},{4,5},{5,6},{6,7},{7,4},{8,9},{9,10},{10,1... | collective-permute-start | bytes 540680 | tf_op jit(solution)/shard_map/ppermute | solution.py:442
  22.1 6.0 %collective-permute-start.4 = (bf16[4,176,128]{2,1,0:T(8,128)(2,1)S(1)}, bf16[4,176,128]{2,1,0:T(8,128)(2,1)S(1)}, u32[]{:S(2)}, u32[]{:S(2)}) collective-permute-start(bf16[4,176,128]{2,1,0:T(8,128)(2,1)S(1)} %get-tuple-element.31), channel_id=1, source_target_pairs={{0,2},{1,3},{2,0},{3,1},{4,6},{5,7},{6,4},{7,5},{8,10},{9,11},{10,... | collective-permute-start | bytes 540680 | tf_op jit(solution)/shard_map/ppermute | solution.py:442
  28.2 9.7 %all-to-all-done = bf16[128,2,2816]{2,1,0:T(2,128)(2,1)S(1)} async-done(((bf16[128,2,2816]{2,1,0:T(2,128)(2,1)}), bf16[128,2,2816]{2,1,0:T(2,128)(2,1)S(1)}, u32[]{:S(2)}, u32[]{:S(2)}) %all-to-all-start) | async-done | bytes 1441824 | tf_op jit(solution)/shard_map/all_to_all | solution.py:420
  37.8 8.5 %polar.1 = (bf16[8,704,128]{2,1,0:T(8,128)(2,1)}, f32[4608,128]{1,0:T(8,128)}, f32[1024,128]{1,0:T(8,128)}) custom-call(s32[2,64]{1,0:T(2,128)S(1)} %bitcast.52, bf16[5632,128]{1,0:T(8,128)(2,1)S(1)} %bitcast.48, f32[4608,128]{1,0:T(8,128)} %bitcast.58, f32[1024,128]{1,0:T(8,128)S(1)} %bitcast.54), custom_call_target="tpu_custom_call" | custom-call | flops 4000000000 | bytes 8388608 | tf_op jit(solution)/shard_map/polar/pallas_call | solution.py:446
  46.4 4.9 %all-to-all-start.1 = ((bf16[8,704,128]{2,1,0:T(8,128)(2,1)}), bf16[8,704,128]{2,1,0:T(8,128)(2,1)S(1)}, u32[]{:S(2)}, u32[]{:S(2)}) async-start(bf16[8,704,128]{2,1,0:T(8,128)(2,1)} %get-tuple-element.33), calls=%async_computation.1 | async-start | bytes 2883584 | tf_op jit(solution)/shard_map/all_to_all | solution.py:471
  51.4 0.4 collective-permute-start.6
  51.8 2.5 %collective-permute-start.7 = (bf16[4,176,128]{2,1,0:T(8,128)(2,1)S(1)}, bf16[4,176,128]{2,1,0:T(8,128)(2,1)S(1)}, u32[]{:S(2)}, u32[]{:S(2)}) collective-permute-start(bf16[4,176,128]{2,1,0:T(8,128)(2,1)S(1)} %pad_maximum_fusion.2), channel_id=1, source_target_pairs={{0,8},{1,9},{2,10},{3,11},{4,12},{5,13},{6,14},{7,15},{8,0},{9,1},... | collective-permute-start | bytes 540680 | tf_op jit(solution)/shard_map/ppermute | solution.py:470
  54.4 1.1 %collective-permute-start.8 = (bf16[4,176,128]{2,1,0:T(8,128)(2,1)S(1)}, bf16[4,176,128]{2,1,0:T(8,128)(2,1)S(1)}, u32[]{:S(2)}, u32[]{:S(2)}) collective-permute-start(bf16[4,176,128]{2,1,0:T(8,128)(2,1)S(1)} %pad_maximum_fusion.3), channel_id=1, source_target_pairs={{0,12},{1,13},{2,14},{3,15},{4,0},{5,1},{6,2},{7,3},{8,4},{9,5},{1... | collective-permute-start | bytes 540680 | tf_op jit(solution)/shard_map/ppermute | solution.py:470
  55.5 1.4 %collective-permute-start.2 = (bf16[2,64]{1,0:T(2,128)(2,1)S(1)}, bf16[2,64]{1,0:T(2,128)(2,1)S(1)}, u32[]{:S(2)}, u32[]{:S(2)}) collective-permute-start(bf16[2,64]{1,0:T(2,128)(2,1)S(1)} %max.10), channel_id=1, source_target_pairs={{0,32},{16,48},{32,0},{48,16},{64,96},{80,112},{96,64},{112,80},{1... | collective-permute-start | bytes 776 | tf_op jit(solution)/shard_map/ppermute | solution.py:439
  56.9 12.2 %collective-permute-done.2 = bf16[2,64]{1,0:T(2,128)(2,1)S(1)} collective-permute-done((bf16[2,64]{1,0:T(2,128)(2,1)S(1)}, bf16[2,64]{1,0:T(2,128)(2,1)S(1)}, u32[]{:S(2)}, u32[]{:S(2)}) %collective-permute-start.2) | collective-permute-done | bytes 288 | tf_op jit(solution)/shard_map/ppermute | solution.py:439
  69.2 1.5 %all-to-all-done.1.polar_ref = bf16[8,704,128]{2,1,0:T(8,128)(2,1)S(1)} async-done(((bf16[8,704,128]{2,1,0:T(8,128)(2,1)}), bf16[8,704,128]{2,1,0:T(8,128)(2,1)S(1)}, u32[]{:S(2)}, u32[]{:S(2)}) %all-to-all-start.1) | async-done | bytes 1441824 | tf_op jit(solution)/shard_map/all_to_all | solution.py:471
  70.7 2.2 %finish.1 = (bf16[2304,128]{1,0:T(8,128)(2,1)}, bf16[512,128]{1,0:T(8,128)(2,1)}) custom-call(s32[2,64]{1,0:T(2,128)S(1)} %bitcast.53, s32[64]{0:T(128)S(1)} %copy-done.2, bf16[2,64]{1,0:T(2,128)(2,1)S(1)} %max.11.peak_ref, bf16[8,704,128]{2,1,0:T(8,128)(2,1)S(1)} %all-to-all-done.1.polar_ref, bf16[4,176,128]{2,1,0:T(8,128)(2,1)S(1)} %pad_maximum_fusion.rest_0_, ...), custom_call_target="tpu_custom_call" | custom-call | flops 10000000 | bytes 4194304 | tf_op jit(solution)/shard_map/finish/pallas_call | solution.py:475
  (23 shorter events, 0.2 us)
Async XLA Ops:
  3.5 11.6 %copy-start.5 = (bf16[1,2,64]{2,1,0:T(2,128)(2,1)S(1)}, bf16[1,2,64]{2,1,0:T(2,128)(2,1)}, u32[]{:S(2)}) copy-start(bf16[1,2,64]{2,1,0:T(2,128)(2,1)} %param.15) | copy-start | bytes 772
  3.5 16.1 %copy-start = (bf16[2,64,2304]{2,1,0:T(8,128)(2,1)S(1)}, bf16[2,64,2304]{2,1,0:T(8,128)(2,1)}, u32[]{:S(2)}) copy-start(bf16[2,64,2304]{2,1,0:T(8,128)(2,1)} %wq_ref.1) | copy-start | bytes 1769476
  3.5 16.1 %copy-start.1 = (bf16[2,64,512]{2,1,0:T(8,128)(2,1)S(1)}, bf16[2,64,512]{2,1,0:T(8,128)(2,1)}, u32[]{:S(2)}) copy-start(bf16[2,64,512]{2,1,0:T(8,128)(2,1)} %wk_ref.1) | copy-start | bytes 393220
  3.5 16.1 %copy-start.2 = (s32[64]{0:T(128)S(1)}, s32[64]{0:T(128)}, u32[]{:S(2)}) copy-start(s32[64]{0:T(128)} %head_ref.1) | copy-start | bytes 772
  3.6 34.3 %copy-start.3 = (s32[64,2,1]{0,2,1:T(1,128)S(1)}, s32[64,2,1]{0,2,1:T(1,128)}, u32[]{:S(2)}) copy-start(s32[64,2,1]{0,2,1:T(1,128)} %param.16) | copy-start | bytes 1540
  3.6 34.3 %copy-start.4 = (f32[2,65536]{1,0:T(2,128)S(1)}, f32[2,65536]{1,0:T(2,128)}, u32[]{:S(2)}) copy-start(f32[2,65536]{1,0:T(2,128)} %param.14) | copy-start | bytes 1572868
  3.6 34.2 %all-to-all-start = ((bf16[128,2,2816]{2,1,0:T(2,128)(2,1)}), bf16[128,2,2816]{2,1,0:T(2,128)(2,1)S(1)}, u32[]{:S(2)}, u32[]{:S(2)}) async-start(bf16[128,2,2816]{2,1,0:T(2,128)(2,1)} %bitcast.55), calls=%async_computation | async-start | bytes 2883584 | tf_op jit(solution)/shard_map/all_to_all | solution.py:420
  15.1 2.0 %collective-permute-start = (bf16[2,64]{1,0:T(2,128)(2,1)S(1)}, bf16[2,64]{1,0:T(2,128)(2,1)S(1)}, u32[]{:S(2)}, u32[]{:S(2)}) collective-permute-start(bf16[2,64]{1,0:T(2,128)(2,1)S(1)} %bitcast.61), channel_id=1, source_target_pairs={{0,16},{16,0},{32,48},{48,32},{64,80},{80,64},{96,112},{112,96},{1... | collective-permute-start | bytes 776 | tf_op jit(solution)/shard_map/ppermute | solution.py:439
  17.1 4.2 %collective-permute-start.1 = (bf16[2,64]{1,0:T(2,128)(2,1)S(1)}, bf16[2,64]{1,0:T(2,128)(2,1)S(1)}, u32[]{:S(2)}, u32[]{:S(2)}) collective-permute-start(bf16[2,64]{1,0:T(2,128)(2,1)S(1)} %bitcast_maximum_fusion), channel_id=1, source_target_pairs={{0,64},{16,80},{32,96},{48,112},{64,0},{80,16},{96,32},{112,48},{1... | collective-permute-start | bytes 776 | tf_op jit(solution)/shard_map/ppermute | solution.py:439
  21.3 25.1 %collective-permute-start.3 = (bf16[4,176,128]{2,1,0:T(8,128)(2,1)S(1)}, bf16[4,176,128]{2,1,0:T(8,128)(2,1)S(1)}, u32[]{:S(2)}, u32[]{:S(2)}) collective-permute-start(bf16[4,176,128]{2,1,0:T(8,128)(2,1)S(1)} %get-tuple-element.30), channel_id=1, source_target_pairs={{0,1},{1,2},{2,3},{3,0},{4,5},{5,6},{6,7},{7,4},{8,9},{9,10},{10,1... | collective-permute-start | bytes 540680 | tf_op jit(solution)/shard_map/ppermute | solution.py:442
  22.1 24.2 %collective-permute-start.4 = (bf16[4,176,128]{2,1,0:T(8,128)(2,1)S(1)}, bf16[4,176,128]{2,1,0:T(8,128)(2,1)S(1)}, u32[]{:S(2)}, u32[]{:S(2)}) collective-permute-start(bf16[4,176,128]{2,1,0:T(8,128)(2,1)S(1)} %get-tuple-element.31), channel_id=1, source_target_pairs={{0,2},{1,3},{2,0},{3,1},{4,6},{5,7},{6,4},{7,5},{8,10},{9,11},{10,... | collective-permute-start | bytes 540680 | tf_op jit(solution)/shard_map/ppermute | solution.py:442
  28.2 18.2 %collective-permute-start.5 = (bf16[4,176,128]{2,1,0:T(8,128)(2,1)S(1)}, bf16[4,176,128]{2,1,0:T(8,128)(2,1)S(1)}, u32[]{:S(2)}, u32[]{:S(2)}) collective-permute-start(bf16[4,176,128]{2,1,0:T(8,128)(2,1)S(1)} %get-tuple-element.32), channel_id=1, source_target_pairs={{0,3},{1,0},{2,1},{3,2},{4,7},{5,4},{6,5},{7,6},{8,11},{9,8},{10,9... | collective-permute-start | bytes 540680 | tf_op jit(solution)/shard_map/ppermute | solution.py:442
  46.4 24.3 %all-to-all-start.1 = ((bf16[8,704,128]{2,1,0:T(8,128)(2,1)}), bf16[8,704,128]{2,1,0:T(8,128)(2,1)S(1)}, u32[]{:S(2)}, u32[]{:S(2)}) async-start(bf16[8,704,128]{2,1,0:T(8,128)(2,1)} %get-tuple-element.33), calls=%async_computation.1 | async-start | bytes 2883584 | tf_op jit(solution)/shard_map/all_to_all | solution.py:471
  51.4 17.7 %collective-permute-start.6 = (bf16[4,176,128]{2,1,0:T(8,128)(2,1)S(1)}, bf16[4,176,128]{2,1,0:T(8,128)(2,1)S(1)}, u32[]{:S(2)}, u32[]{:S(2)}) collective-permute-start(bf16[4,176,128]{2,1,0:T(8,128)(2,1)S(1)} %pad_maximum_fusion.1), channel_id=1, source_target_pairs={{0,4},{1,5},{2,6},{3,7},{4,8},{5,9},{6,10},{7,11},{8,12},{9,13},{1... | collective-permute-start | bytes 540680 | tf_op jit(solution)/shard_map/ppermute | solution.py:470
  51.8 17.3 %collective-permute-start.7 = (bf16[4,176,128]{2,1,0:T(8,128)(2,1)S(1)}, bf16[4,176,128]{2,1,0:T(8,128)(2,1)S(1)}, u32[]{:S(2)}, u32[]{:S(2)}) collective-permute-start(bf16[4,176,128]{2,1,0:T(8,128)(2,1)S(1)} %pad_maximum_fusion.2), channel_id=1, source_target_pairs={{0,8},{1,9},{2,10},{3,11},{4,12},{5,13},{6,14},{7,15},{8,0},{9,1},... | collective-permute-start | bytes 540680 | tf_op jit(solution)/shard_map/ppermute | solution.py:470
  54.4 14.8 %collective-permute-start.8 = (bf16[4,176,128]{2,1,0:T(8,128)(2,1)S(1)}, bf16[4,176,128]{2,1,0:T(8,128)(2,1)S(1)}, u32[]{:S(2)}, u32[]{:S(2)}) collective-permute-start(bf16[4,176,128]{2,1,0:T(8,128)(2,1)S(1)} %pad_maximum_fusion.3), channel_id=1, source_target_pairs={{0,12},{1,13},{2,14},{3,15},{4,0},{5,1},{6,2},{7,3},{8,4},{9,5},{1... | collective-permute-start | bytes 540680 | tf_op jit(solution)/shard_map/ppermute | solution.py:470
  55.5 13.6 %collective-permute-start.2 = (bf16[2,64]{1,0:T(2,128)(2,1)S(1)}, bf16[2,64]{1,0:T(2,128)(2,1)S(1)}, u32[]{:S(2)}, u32[]{:S(2)}) collective-permute-start(bf16[2,64]{1,0:T(2,128)(2,1)S(1)} %max.10), channel_id=1, source_target_pairs={{0,32},{16,48},{32,0},{48,16},{64,96},{80,112},{96,64},{112,80},{1... | collective-permute-start | bytes 776 | tf_op jit(solution)/shard_map/ppermute | solution.py:439

commit v5 on v4

--- a/solution.py
+++ b/solution.py
@@ -98,13 +98,13 @@
             picks[slot][layer] = dot(chosen, heads_of, ((1,), (1,))).astype(bf16)
     for copy in copies[2:]:
         copy.wait()
-    for slot in range(slots):
-        pick = jnp.concatenate(picks[slot], axis=1)
-        for ref, tiles, base in ((gq_ref, tq, 0), (gk_ref, tk, tq)):
-            value = dot(pick, ref[...])
-            for tile in range(tiles):
+    pick = jnp.concatenate([jnp.concatenate(row, axis=1) for row in picks], axis=0)
+    for ref, tiles, base in ((gk_ref, tk, tq), (gq_ref, tq, 0)):
+        value = dot(pick, ref[...])
+        for tile in range(tiles):
+            for slot in range(slots):
                 stage[pl.ds((base + tile) * slots + slot, devices, stride=rows), :] = value[
-                    :, tile * LANE : (tile + 1) * LANE
+                    slot * devices : (slot + 1) * devices, tile * LANE : (tile + 1) * LANE
                 ]
     sends = []
     parts = sems_send.shape[0]
@@ -159,7 +159,7 @@
     out_ref,
     sems_in,
     sems_out,
-    sems_send,
+    sem_send,
     *,
     ranks,
     owners,
@@ -168,21 +168,22 @@
     devices = ranks * owners
     parts = sems_in.shape[0] // 2
 
-    def piece(ref, part):
-        count = ref.shape[0] // parts
+    def piece(ref, rows, part):
+        count = rows // parts
         return ref.at[pl.ds(part * count, count), :]
 
     def moves(sems, pairs):
         return [
             [
-                pltpu.make_async_copy(piece(src, part), piece(dst, part), sems.at[2 * part + j])
-                for j, (src, dst) in enumerate(pairs)
+                pltpu.make_async_copy(piece(src, rows, part), piece(dst, rows, part), sems.at[2 * part + j])
+                for j, (src, dst, rows) in enumerate(pairs)
             ]
             for part in range(parts)
         ]
 
-    loads = moves(sems_in, ((mq_far, mq_ref), (mk_far, mk_ref)))
-    stores = moves(sems_out, ((mq_ref, mq_next), (mk_ref, mk_next)))
+    nq, nk = mq_far.shape[0], mk_far.shape[0]
+    loads = moves(sems_in, ((mq_far, mq_ref, nq), (mk_far, mk_ref, nk)))
+    stores = moves(sems_out, ((mq_ref, mq_next, nq), (mk_ref, mk_next, nk)))
     for pair in loads:
         for copy in pair:
             copy.start()
@@ -255,7 +256,6 @@
             chains = [x.astype(bf16) for x in chains]
     fq = DQ * RQ // LANE // owners
     fk = DN * RK // LANE // owners
-    sends = []
     for owner in range(owners):
         for slot in range(slots):
             for x, height, width, at in (
@@ -269,10 +269,9 @@
                     out_ref[owner, at + tile * span : at + (tile + 2) * span, :] = jnp.concatenate(
                         both, axis=0
                     ).astype(bf16)
-        sends.append(pltpu.make_async_copy(out_ref.at[owner], out_far.at[owner], sems_send.at[owner]))
-        sends[-1].start()
-    for copy in sends:
-        copy.wait()
+    send = pltpu.make_async_copy(out_ref, out_far, sem_send)
+    send.start()
+    send.wait()
     for pair in stores:
         for copy in pair:
             copy.wait()
@@ -401,7 +400,7 @@
             pltpu.VMEM(head_row.shape, jnp.int32),
             pltpu.VMEM((layers * heads, piece_q), bf16),
             pltpu.VMEM((layers * heads, piece_k), bf16),
-            pltpu.VMEM((devices * tiles * slots, LANE), f32),
+            pltpu.VMEM(((devices + 1) * tiles * slots, LANE), f32),
             pltpu.VMEM((devices * tiles * slots, LANE), bf16),
             pltpu.SemaphoreType.DMA((4,)),
             pltpu.SemaphoreType.DMA((4,)),
@@ -426,7 +425,7 @@
         "pack_weights",
         [shape((SIDE, wrows, LANE), bf16)] * SIDE,
         [VMEM] * 3,
-        [pltpu.VMEM((ranks * wrows, LANE), f32)],
+        [pltpu.VMEM(((ranks + 1) * wrows, LANE), f32)],
         2 * 128 * 64 * 2816,
         3 * 2**20,
     )(head_row, weight_query, weight_key)
@@ -435,7 +434,7 @@
     ]
     along_x = [[(i, (i + t * SIDE) % ranks) for i in range(ranks)] for t in range(SIDE)]
     peaks = logit_peak[0]
-    for reach in (1, 4, 2):
+    for reach in (4, 1, 2):
         peaks = jnp.maximum(peaks, lax.ppermute(peaks, "dp", [(i, i ^ reach) for i in range(owners)]))
         if reach == 4:
             peaks, by_y = lax.optimization_barrier((peaks, by_y))
@@ -453,12 +452,12 @@
         ),
         [VMEM, VMEM, HBM, HBM],
         [
-            pltpu.VMEM((fq * slots, LANE), f32),
-            pltpu.VMEM((fk * slots, LANE), f32),
+            pltpu.VMEM((fq * slots + RQ // LANE * slots, LANE), f32),
+            pltpu.VMEM((fk * slots + RK // LANE * slots, LANE), f32),
             pltpu.VMEM((owners, slots * (fq + fk) // owners, LANE), bf16),
             pltpu.SemaphoreType.DMA((2 * parts,)),
             pltpu.SemaphoreType.DMA((2 * parts,)),
-            pltpu.SemaphoreType.DMA((owners,)),
+            pltpu.SemaphoreType.DMA,
         ],
         4 * 10**9,
         8 * 2**20,
@@ -478,8 +477,8 @@
         (shape((oq, LANE), bf16), shape((ok, LANE), bf16)),
         [SMEM, SMEM, VMEM, VMEM] + [VMEM] * SIDE,
         [
-            pltpu.VMEM((oq, LANE), f32),
-            pltpu.VMEM((ok, LANE), f32),
+            pltpu.VMEM((oq + RQ // LANE * per_rank, LANE), f32),
+            pltpu.VMEM((ok + RK // LANE * per_rank, LANE), f32),
         ],
         10**7,
         4 * 2**20,

time: 73.1 us -> 73.1 us (level)
  starting transfers between devices: 32.5 us -> 35 us
  waiting for transfers between devices: 25 us -> 22.5 us
    ppermute x3, waiting for transfers between devices: 13.8 us -> 11.3 us  [body(): lax.ppermute(peaks, 'dp', [(i, i ^ reach) for i in range(owners)])]
    ppermute x3, starting transfers between devices: 6.9 us -> 8.33 us  [body(): lax.ppermute(by_y[s], 'mp', along_y[s])]
    ppermute x3, starting transfers between devices: 5.11 us -> 6.19 us  [body(): lax.ppermute(peaks, 'dp', [(i, i ^ reach) for i in range(owners)])]
where the time goes in v5:
time: 73.1 us; the launch traced here: 72.9 us
  starting transfers between devices  35 us (48%)
  waiting for transfers between devices  22.5 us (31%)
  Pallas kernels  14.4 us (20%)
  between operations  0.8 us (1%)
    all_to_all x1, starting transfers between devices, body(): lax.all_to_all(packed, ('dp', 'mp'), split_axis=0, concat_axis=0, tiled=T...  11.5 us
    ppermute x3, waiting for transfers between devices, body(): lax.ppermute(peaks, 'dp', [(i, i ^ reach) for i in range(owners)])  11.3 us
    all_to_all x1, waiting for transfers between devices, body(): lax.all_to_all(packed, ('dp', 'mp'), split_axis=0, concat_axis=0, tiled=T...  9.66 us
    pallas_call x1, Pallas kernels, body(): call(functools.partial(polar_kernel, **kw), 'polar', (shape((owners, slot...  8.47 us
    ppermute x3, starting transfers between devices, body(): lax.ppermute(by_y[s], 'mp', along_y[s])  8.33 us
    ppermute x3, starting transfers between devices, body(): lax.ppermute(peaks, 'dp', [(i, i ^ reach) for i in range(owners)])  6.19 us
    all_to_all x1, starting transfers between devices, body(): back = lax.all_to_all(polar, 'dp', split_axis=0, concat_axis=0, tiled=True)  4.94 us
    ppermute x3, starting transfers between devices, body(): lax.ppermute(by_x[t], 'mp', along_x[t])  4.04 us
  transfers between devices with their start and end apart: 11, of which 5 were waited for; matrix products, arithmetic and copies ran while one was open for 0% of the time, Pallas kernels for 13%

profile of v5, /device:TPU:1, one launch (start us, length us, event | category | flops | bytes accessed | tf_op | source)
XLA Modules:
  0.0 72.9 jit_solution(292863780893606650)
XLA Ops:
  0.6 2.9 %pack_grads.1 = bf16[5632,128]{1,0:T(8,128)(2,1)} custom-call(s32[2,64]{1,0:T(2,128)} %bitcast.51, s32[1,64]{1,0:T(1,128)} %bitcast.49, bf16[128,2304]{1,0:T(8,128)(2,1)} %bitcast.56, bf16[128,512]{1,0:T(8,128)(2,1)} %bitcast.57), custom_call_target="tpu_custom_call" | custom-call | flops 184549376 | bytes 3145728 | tf_op jit(solution)/shard_map/pack_grads/pallas_call | solution.py:393
  3.5 0.0 copy-start.5
  3.5 0.0 copy-start
  3.6 0.0 copy-start.1
  3.6 0.0 copy-start.2
  3.6 0.0 copy-start.3
  3.6 11.5 %all-to-all-start = ((bf16[128,2,2816]{2,1,0:T(2,128)(2,1)}), bf16[128,2,2816]{2,1,0:T(2,128)(2,1)S(1)}, u32[]{:S(2)}, u32[]{:S(2)}) async-start(bf16[128,2,2816]{2,1,0:T(2,128)(2,1)} %bitcast.55), calls=%async_computation | async-start | bytes 2883584 | tf_op jit(solution)/shard_map/all_to_all | solution.py:419
  15.1 3.4 %collective-permute-start = (bf16[2,64]{1,0:T(2,128)(2,1)S(1)}, bf16[2,64]{1,0:T(2,128)(2,1)S(1)}, u32[]{:S(2)}, u32[]{:S(2)}) collective-permute-start(bf16[2,64]{1,0:T(2,128)(2,1)S(1)} %bitcast.61), channel_id=1, source_target_pairs={{0,64},{16,80},{32,96},{48,112},{64,0},{80,16},{96,32},{112,48},{1... | collective-permute-start | bytes 776 | tf_op jit(solution)/shard_map/ppermute | solution.py:438
  18.5 0.8 %pack_weights.1 = (bf16[4,176,128]{2,1,0:T(8,128)(2,1)S(1)}, bf16[4,176,128]{2,1,0:T(8,128)(2,1)S(1)}, bf16[4,176,128]{2,1,0:T(8,128)(2,1)S(1)}, bf16[4,176,128]{2,1,0:T(8,128)(2,1)S(1)}) custom-call(s32[1,64]{1,0:T(1,128)S(1)} %bitcast.50, bf16[2,64,2304]{2,1,0:T(8,128)(2,1)S(1)} %copy-done, bf16[2,64,512]{2,1,0:T(8,128)(2,1)S(1)} %copy-done.1), custom_call_target="tpu_custom_call" | custom-call | flops 46137344 | bytes 3145728 | tf_op jit(solution)/shard_map/pack_weights/pallas_call | solution.py:423
  19.3 0.6 collective-permute-done
  19.9 1.8 %collective-permute-start.3 = (bf16[4,176,128]{2,1,0:T(8,128)(2,1)S(1)}, bf16[4,176,128]{2,1,0:T(8,128)(2,1)S(1)}, u32[]{:S(2)}, u32[]{:S(2)}) collective-permute-start(bf16[4,176,128]{2,1,0:T(8,128)(2,1)S(1)} %get-tuple-element.30), channel_id=1, source_target_pairs={{0,1},{1,2},{2,3},{3,0},{4,5},{5,6},{6,7},{7,4},{8,9},{9,10},{10,1... | collective-permute-start | bytes 540680 | tf_op jit(solution)/shard_map/ppermute | solution.py:441
  21.7 6.5 %collective-permute-start.4 = (bf16[4,176,128]{2,1,0:T(8,128)(2,1)S(1)}, bf16[4,176,128]{2,1,0:T(8,128)(2,1)S(1)}, u32[]{:S(2)}, u32[]{:S(2)}) collective-permute-start(bf16[4,176,128]{2,1,0:T(8,128)(2,1)S(1)} %get-tuple-element.31), channel_id=1, source_target_pairs={{0,2},{1,3},{2,0},{3,1},{4,6},{5,7},{6,4},{7,5},{8,10},{9,11},{10,... | collective-permute-start | bytes 540680 | tf_op jit(solution)/shard_map/ppermute | solution.py:441
  28.2 9.7 %all-to-all-done = bf16[128,2,2816]{2,1,0:T(2,128)(2,1)S(1)} async-done(((bf16[128,2,2816]{2,1,0:T(2,128)(2,1)}), bf16[128,2,2816]{2,1,0:T(2,128)(2,1)S(1)}, u32[]{:S(2)}, u32[]{:S(2)}) %all-to-all-start) | async-done | bytes 1441824 | tf_op jit(solution)/shard_map/all_to_all | solution.py:419
  37.9 8.5 %polar.1 = (bf16[8,704,128]{2,1,0:T(8,128)(2,1)}, f32[4608,128]{1,0:T(8,128)}, f32[1024,128]{1,0:T(8,128)}) custom-call(s32[2,64]{1,0:T(2,128)S(1)} %bitcast.52, bf16[5632,128]{1,0:T(8,128)(2,1)S(1)} %bitcast.48, f32[4608,128]{1,0:T(8,128)} %bitcast.58, f32[1024,128]{1,0:T(8,128)S(1)} %bitcast.54), custom_call_target="tpu_custom_call" | custom-call | flops 4000000000 | bytes 8388608 | tf_op jit(solution)/shard_map/polar/pallas_call | solution.py:445
  46.4 4.9 %all-to-all-start.1 = ((bf16[8,704,128]{2,1,0:T(8,128)(2,1)}), bf16[8,704,128]{2,1,0:T(8,128)(2,1)S(1)}, u32[]{:S(2)}, u32[]{:S(2)}) async-start(bf16[8,704,128]{2,1,0:T(8,128)(2,1)} %get-tuple-element.33), calls=%async_computation.1 | async-start | bytes 2883584 | tf_op jit(solution)/shard_map/all_to_all | solution.py:470
  51.4 0.4 collective-permute-start.6
  51.8 2.5 %collective-permute-start.7 = (bf16[4,176,128]{2,1,0:T(8,128)(2,1)S(1)}, bf16[4,176,128]{2,1,0:T(8,128)(2,1)S(1)}, u32[]{:S(2)}, u32[]{:S(2)}) collective-permute-start(bf16[4,176,128]{2,1,0:T(8,128)(2,1)S(1)} %pad_maximum_fusion.2), channel_id=1, source_target_pairs={{0,8},{1,9},{2,10},{3,11},{4,12},{5,13},{6,14},{7,15},{8,0},{9,1},... | collective-permute-start | bytes 540680 | tf_op jit(solution)/shard_map/ppermute | solution.py:469
  54.4 1.1 %collective-permute-start.8 = (bf16[4,176,128]{2,1,0:T(8,128)(2,1)S(1)}, bf16[4,176,128]{2,1,0:T(8,128)(2,1)S(1)}, u32[]{:S(2)}, u32[]{:S(2)}) collective-permute-start(bf16[4,176,128]{2,1,0:T(8,128)(2,1)S(1)} %pad_maximum_fusion.3), channel_id=1, source_target_pairs={{0,12},{1,13},{2,14},{3,15},{4,0},{5,1},{6,2},{7,3},{8,4},{9,5},{1... | collective-permute-start | bytes 540680 | tf_op jit(solution)/shard_map/ppermute | solution.py:469
  55.5 0.8 %collective-permute-start.1 = (bf16[2,64]{1,0:T(2,128)(2,1)S(1)}, bf16[2,64]{1,0:T(2,128)(2,1)S(1)}, u32[]{:S(2)}, u32[]{:S(2)}) collective-permute-start(bf16[2,64]{1,0:T(2,128)(2,1)S(1)} %bitcast_maximum_fusion), channel_id=1, source_target_pairs={{0,16},{16,0},{32,48},{48,32},{64,80},{80,64},{96,112},{112,96},{1... | collective-permute-start | bytes 776 | tf_op jit(solution)/shard_map/ppermute | solution.py:438
  56.4 0.8 %collective-permute-done.1 = bf16[2,64]{1,0:T(2,128)(2,1)S(1)} collective-permute-done((bf16[2,64]{1,0:T(2,128)(2,1)S(1)}, bf16[2,64]{1,0:T(2,128)(2,1)S(1)}, u32[]{:S(2)}, u32[]{:S(2)}) %collective-permute-start.1) | collective-permute-done | bytes 288 | tf_op jit(solution)/shard_map/ppermute | solution.py:438
  57.2 2.0 %collective-permute-start.2 = (bf16[2,64]{1,0:T(2,128)(2,1)S(1)}, bf16[2,64]{1,0:T(2,128)(2,1)S(1)}, u32[]{:S(2)}, u32[]{:S(2)}) collective-permute-start(bf16[2,64]{1,0:T(2,128)(2,1)S(1)} %max.10), channel_id=1, source_target_pairs={{0,32},{16,48},{32,0},{48,16},{64,96},{80,112},{96,64},{112,80},{1... | collective-permute-start | bytes 776 | tf_op jit(solution)/shard_map/ppermute | solution.py:438
  59.2 9.9 %collective-permute-done.2 = bf16[2,64]{1,0:T(2,128)(2,1)S(1)} collective-permute-done((bf16[2,64]{1,0:T(2,128)(2,1)S(1)}, bf16[2,64]{1,0:T(2,128)(2,1)S(1)}, u32[]{:S(2)}, u32[]{:S(2)}) %collective-permute-start.2) | collective-permute-done | bytes 288 | tf_op jit(solution)/shard_map/ppermute | solution.py:438
  69.2 1.5 %all-to-all-done.1.polar_ref = bf16[8,704,128]{2,1,0:T(8,128)(2,1)S(1)} async-done(((bf16[8,704,128]{2,1,0:T(8,128)(2,1)}), bf16[8,704,128]{2,1,0:T(8,128)(2,1)S(1)}, u32[]{:S(2)}, u32[]{:S(2)}) %all-to-all-start.1) | async-done | bytes 1441824 | tf_op jit(solution)/shard_map/all_to_all | solution.py:470
  70.6 2.2 %finish.1 = (bf16[2304,128]{1,0:T(8,128)(2,1)}, bf16[512,128]{1,0:T(8,128)(2,1)}) custom-call(s32[2,64]{1,0:T(2,128)S(1)} %bitcast.53, s32[64]{0:T(128)S(1)} %copy-done.2, bf16[2,64]{1,0:T(2,128)(2,1)S(1)} %max.11.peak_ref, bf16[8,704,128]{2,1,0:T(8,128)(2,1)S(1)} %all-to-all-done.1.polar_ref, bf16[4,176,128]{2,1,0:T(8,128)(2,1)S(1)} %pad_maximum_fusion.rest_0_, ...), custom_call_target="tpu_custom_call" | custom-call | flops 10000000 | bytes 4194304 | tf_op jit(solution)/shard_map/finish/pallas_call | solution.py:474
  (23 shorter events, 0.2 us)
Async XLA Ops:
  3.5 11.6 %copy-start.5 = (bf16[1,2,64]{2,1,0:T(2,128)(2,1)S(1)}, bf16[1,2,64]{2,1,0:T(2,128)(2,1)}, u32[]{:S(2)}) copy-start(bf16[1,2,64]{2,1,0:T(2,128)(2,1)} %param.15) | copy-start | bytes 772
  3.5 14.9 %copy-start = (bf16[2,64,2304]{2,1,0:T(8,128)(2,1)S(1)}, bf16[2,64,2304]{2,1,0:T(8,128)(2,1)}, u32[]{:S(2)}) copy-start(bf16[2,64,2304]{2,1,0:T(8,128)(2,1)} %wq_ref.1) | copy-start | bytes 1769476
  3.6 14.9 %copy-start.1 = (bf16[2,64,512]{2,1,0:T(8,128)(2,1)S(1)}, bf16[2,64,512]{2,1,0:T(8,128)(2,1)}, u32[]{:S(2)}) copy-start(bf16[2,64,512]{2,1,0:T(8,128)(2,1)} %wk_ref.1) | copy-start | bytes 393220
  3.6 14.9 %copy-start.2 = (s32[64]{0:T(128)S(1)}, s32[64]{0:T(128)}, u32[]{:S(2)}) copy-start(s32[64]{0:T(128)} %head_ref.1) | copy-start | bytes 772
  3.6 34.3 %copy-start.3 = (s32[64,2,1]{0,2,1:T(1,128)S(1)}, s32[64,2,1]{0,2,1:T(1,128)}, u32[]{:S(2)}) copy-start(s32[64,2,1]{0,2,1:T(1,128)} %param.16) | copy-start | bytes 1540
  3.6 34.3 %copy-start.4 = (f32[2,65536]{1,0:T(2,128)S(1)}, f32[2,65536]{1,0:T(2,128)}, u32[]{:S(2)}) copy-start(f32[2,65536]{1,0:T(2,128)} %param.14) | copy-start | bytes 1572868
  3.6 34.2 %all-to-all-start = ((bf16[128,2,2816]{2,1,0:T(2,128)(2,1)}), bf16[128,2,2816]{2,1,0:T(2,128)(2,1)S(1)}, u32[]{:S(2)}, u32[]{:S(2)}) async-start(bf16[128,2,2816]{2,1,0:T(2,128)(2,1)} %bitcast.55), calls=%async_computation | async-start | bytes 2883584 | tf_op jit(solution)/shard_map/all_to_all | solution.py:419
  15.1 4.7 %collective-permute-start = (bf16[2,64]{1,0:T(2,128)(2,1)S(1)}, bf16[2,64]{1,0:T(2,128)(2,1)S(1)}, u32[]{:S(2)}, u32[]{:S(2)}) collective-permute-start(bf16[2,64]{1,0:T(2,128)(2,1)S(1)} %bitcast.61), channel_id=1, source_target_pairs={{0,64},{16,80},{32,96},{48,112},{64,0},{80,16},{96,32},{112,48},{1... | collective-permute-start | bytes 776 | tf_op jit(solution)/shard_map/ppermute | solution.py:438
  19.9 26.5 %collective-permute-start.3 = (bf16[4,176,128]{2,1,0:T(8,128)(2,1)S(1)}, bf16[4,176,128]{2,1,0:T(8,128)(2,1)S(1)}, u32[]{:S(2)}, u32[]{:S(2)}) collective-permute-start(bf16[4,176,128]{2,1,0:T(8,128)(2,1)S(1)} %get-tuple-element.30), channel_id=1, source_target_pairs={{0,1},{1,2},{2,3},{3,0},{4,5},{5,6},{6,7},{7,4},{8,9},{9,10},{10,1... | collective-permute-start | bytes 540680 | tf_op jit(solution)/shard_map/ppermute | solution.py:441
  21.7 24.7 %collective-permute-start.4 = (bf16[4,176,128]{2,1,0:T(8,128)(2,1)S(1)}, bf16[4,176,128]{2,1,0:T(8,128)(2,1)S(1)}, u32[]{:S(2)}, u32[]{:S(2)}) collective-permute-start(bf16[4,176,128]{2,1,0:T(8,128)(2,1)S(1)} %get-tuple-element.31), channel_id=1, source_target_pairs={{0,2},{1,3},{2,0},{3,1},{4,6},{5,7},{6,4},{7,5},{8,10},{9,11},{10,... | collective-permute-start | bytes 540680 | tf_op jit(solution)/shard_map/ppermute | solution.py:441
  28.2 18.2 %collective-permute-start.5 = (bf16[4,176,128]{2,1,0:T(8,128)(2,1)S(1)}, bf16[4,176,128]{2,1,0:T(8,128)(2,1)S(1)}, u32[]{:S(2)}, u32[]{:S(2)}) collective-permute-start(bf16[4,176,128]{2,1,0:T(8,128)(2,1)S(1)} %get-tuple-element.32), channel_id=1, source_target_pairs={{0,3},{1,0},{2,1},{3,2},{4,7},{5,4},{6,5},{7,6},{8,11},{9,8},{10,9... | collective-permute-start | bytes 540680 | tf_op jit(solution)/shard_map/ppermute | solution.py:441
  46.4 24.3 %all-to-all-start.1 = ((bf16[8,704,128]{2,1,0:T(8,128)(2,1)}), bf16[8,704,128]{2,1,0:T(8,128)(2,1)S(1)}, u32[]{:S(2)}, u32[]{:S(2)}) async-start(bf16[8,704,128]{2,1,0:T(8,128)(2,1)} %get-tuple-element.33), calls=%async_computation.1 | async-start | bytes 2883584 | tf_op jit(solution)/shard_map/all_to_all | solution.py:470
  51.4 17.7 %collective-permute-start.6 = (bf16[4,176,128]{2,1,0:T(8,128)(2,1)S(1)}, bf16[4,176,128]{2,1,0:T(8,128)(2,1)S(1)}, u32[]{:S(2)}, u32[]{:S(2)}) collective-permute-start(bf16[4,176,128]{2,1,0:T(8,128)(2,1)S(1)} %pad_maximum_fusion.1), channel_id=1, source_target_pairs={{0,4},{1,5},{2,6},{3,7},{4,8},{5,9},{6,10},{7,11},{8,12},{9,13},{1... | collective-permute-start | bytes 540680 | tf_op jit(solution)/shard_map/ppermute | solution.py:469
  51.8 17.3 %collective-permute-start.7 = (bf16[4,176,128]{2,1,0:T(8,128)(2,1)S(1)}, bf16[4,176,128]{2,1,0:T(8,128)(2,1)S(1)}, u32[]{:S(2)}, u32[]{:S(2)}) collective-permute-start(bf16[4,176,128]{2,1,0:T(8,128)(2,1)S(1)} %pad_maximum_fusion.2), channel_id=1, source_target_pairs={{0,8},{1,9},{2,10},{3,11},{4,12},{5,13},{6,14},{7,15},{8,0},{9,1},... | collective-permute-start | bytes 540680 | tf_op jit(solution)/shard_map/ppermute | solution.py:469
  54.4 14.8 %collective-permute-start.8 = (bf16[4,176,128]{2,1,0:T(8,128)(2,1)S(1)}, bf16[4,176,128]{2,1,0:T(8,128)(2,1)S(1)}, u32[]{:S(2)}, u32[]{:S(2)}) collective-permute-start(bf16[4,176,128]{2,1,0:T(8,128)(2,1)S(1)} %pad_maximum_fusion.3), channel_id=1, source_target_pairs={{0,12},{1,13},{2,14},{3,15},{4,0},{5,1},{6,2},{7,3},{8,4},{9,5},{1... | collective-permute-start | bytes 540680 | tf_op jit(solution)/shard_map/ppermute | solution.py:469
  55.5 1.7 %collective-permute-start.1 = (bf16[2,64]{1,0:T(2,128)(2,1)S(1)}, bf16[2,64]{1,0:T(2,128)(2,1)S(1)}, u32[]{:S(2)}, u32[]{:S(2)}) collective-permute-start(bf16[2,64]{1,0:T(2,128)(2,1)S(1)} %bitcast_maximum_fusion), channel_id=1, source_target_pairs={{0,16},{16,0},{32,48},{48,32},{64,80},{80,64},{96,112},{112,96},{1... | collective-permute-start | bytes 776 | tf_op jit(solution)/shard_map/ppermute | solution.py:438
  57.2 11.9 %collective-permute-start.2 = (bf16[2,64]{1,0:T(2,128)(2,1)S(1)}, bf16[2,64]{1,0:T(2,128)(2,1)S(1)}, u32[]{:S(2)}, u32[]{:S(2)}) collective-permute-start(bf16[2,64]{1,0:T(2,128)(2,1)S(1)} %max.10), channel_id=1, source_target_pairs={{0,32},{16,48},{32,0},{48,16},{64,96},{80,112},{96,64},{112,80},{1... | collective-permute-start | bytes 776 | tf_op jit(solution)/shard_map/ppermute | solution.py:438

commit v6 on v5

--- a/solution.py
+++ b/solution.py
@@ -156,6 +156,8 @@
     mk_next,
     mq_ref,
     mk_ref,
+    gq_ref,
+    gk_ref,
     out_ref,
     sems_in,
     sems_out,
@@ -204,28 +206,39 @@
     def tile_of(value, index):
         return value[index * 8 : (index + 1) * 8, :]
 
-    def step(quad, totals):
-        totals = list(totals)
+    @pl.loop(0, devices // 4)
+    def _(quad):
         block = recv_ref[pl.ds(pl.multiple_of(quad * 4 * rows, 16), 4 * rows), :].astype(f32)
         for pair in range(2):
             g = [tile_of(block, pair * 11 + j) for j in range(11)]
             query = g[0:4] + [jnp.where(low, g[4], g[5])] + g[6:10]
             key = [pltpu.roll(jnp.where(low, g[5], g[4]), 4, 0), g[10]]
-            for which, (grads, ref, count) in enumerate(((query, mq_ref, 9), (key, mk_ref, 2))):
-                base = pl.multiple_of((quad * 2 + pair) * count * 8, 8)
-                for j in range(count):
-                    at = pl.ds(pl.multiple_of(base + j * 8, 8), 8)
-                    new = ref[at, :] * decay + grads[j]
-                    ref[at, :] = new
-                    totals[which] += new * new
-        return tuple(totals)
-
-    totals = (jnp.zeros((8, LANE), f32), jnp.zeros((8, LANE), f32))
-    turns = devices // 4 // parts
+            for grads, ref in ((query, gq_ref), (key, gk_ref)):
+                base = pl.multiple_of((quad * 2 + pair) * len(grads) * 8, 8)
+                for j, value in enumerate(grads):
+                    ref[pl.ds(pl.multiple_of(base + j * 8, 8), 8), :] = value
+
+    def update(ref, grad_ref, first, count, total):
+        span = 128
+
+        def step(index, total):
+            at = pl.ds(pl.multiple_of(first + index * span, span), span)
+            old, grad = ref[at, :], grad_ref[at, :]
+            news = [tile_of(old, j) * decay + tile_of(grad, j) for j in range(span // 8)]
+            ref[at, :] = jnp.concatenate(news, axis=0)
+            for new in news:
+                total = total + new * new
+            return total
+
+        return lax.fori_loop(0, count // span, step, total)
+
+    totals = [jnp.zeros((8, LANE), f32)] * 2
     for part in range(parts):
         for copy in loads[part]:
             copy.wait()
-        totals = lax.fori_loop(part * turns, (part + 1) * turns, step, totals)
+        for which, (ref, grad_ref) in enumerate(((mq_ref, gq_ref), (mk_ref, gk_ref))):
+            count = grad_ref.shape[0] // parts
+            totals[which] = update(ref, grad_ref, part * count, count, totals[which])
         for copy in stores[part]:
             copy.start()
 
@@ -441,7 +454,7 @@
     by_y = [by_y[0]] + [lax.ppermute(by_y[s], "mp", along_y[s]) for s in range(1, SIDE)]
     fq = DQ * RQ // LANE
     fk = DN * RK // LANE
-    parts = 2
+    parts = 4
     polar, next_q, next_k = call(
         functools.partial(polar_kernel, **kw),
         "polar",
@@ -454,6 +467,8 @@
         [
             pltpu.VMEM((fq * slots + RQ // LANE * slots, LANE), f32),
             pltpu.VMEM((fk * slots + RK // LANE * slots, LANE), f32),
+            pltpu.VMEM((fq * slots, LANE), f32),
+            pltpu.VMEM((fk * slots, LANE), f32),
             pltpu.VMEM((owners, slots * (fq + fk) // owners, LANE), bf16),
             pltpu.SemaphoreType.DMA((2 * parts,)),
             pltpu.SemaphoreType.DMA((2 * parts,)),

time: 73.1 us -> 73.1 us (level)
  no operation moved by 1% of the time
where the time goes in v6:
time: 73.1 us; the launch traced here: 72.9 us
  starting transfers between devices  35 us (48%)
  waiting for transfers between devices  22.5 us (31%)
  Pallas kernels  14.4 us (20%)
  between operations  0.8 us (1%)
    all_to_all x1, starting transfers between devices, body(): lax.all_to_all(packed, ('dp', 'mp'), split_axis=0, concat_axis=0, tiled=T...  11.5 us
    ppermute x3, waiting for transfers between devices, body(): lax.ppermute(peaks, 'dp', [(i, i ^ reach) for i in range(owners)])  11.3 us
    all_to_all x1, waiting for transfers between devices, body(): lax.all_to_all(packed, ('dp', 'mp'), split_axis=0, concat_axis=0, tiled=T...  9.66 us
    pallas_call x1, Pallas kernels, body(): call(functools.partial(polar_kernel, **kw), 'polar', (shape((owners, slot...  8.46 us
    ppermute x3, starting transfers between devices, body(): lax.ppermute(by_y[s], 'mp', along_y[s])  8.33 us
    ppermute x3, starting transfers between devices, body(): lax.ppermute(peaks, 'dp', [(i, i ^ reach) for i in range(owners)])  6.19 us
    all_to_all x1, starting transfers between devices, body(): back = lax.all_to_all(polar, 'dp', split_axis=0, concat_axis=0, tiled=True)  4.94 us
    ppermute x3, starting transfers between devices, body(): lax.ppermute(by_x[t], 'mp', along_x[t])  4.06 us
  transfers between devices with their start and end apart: 11, of which 5 were waited for; matrix products, arithmetic and copies ran while one was open for 0% of the time, Pallas kernels for 13%

profile of v6, /device:TPU:1, one launch (start us, length us, event | category | flops | bytes accessed | tf_op | source)
XLA Modules:
  0.0 72.9 jit_solution(4840998194473643724)
XLA Ops:
  0.6 2.9 %pack_grads.1 = bf16[5632,128]{1,0:T(8,128)(2,1)} custom-call(s32[2,64]{1,0:T(2,128)} %bitcast.51, s32[1,64]{1,0:T(1,128)} %bitcast.49, bf16[128,2304]{1,0:T(8,128)(2,1)} %bitcast.56, bf16[128,512]{1,0:T(8,128)(2,1)} %bitcast.57), custom_call_target="tpu_custom_call" | custom-call | flops 184549376 | bytes 3145728 | tf_op jit(solution)/shard_map/pack_grads/pallas_call | solution.py:406
  3.5 0.0 copy-start.5
  3.5 0.0 copy-start
  3.6 0.0 copy-start.1
  3.6 0.0 copy-start.3
  3.6 0.0 copy-start.4
  3.6 11.5 %all-to-all-start = ((bf16[128,2,2816]{2,1,0:T(2,128)(2,1)}), bf16[128,2,2816]{2,1,0:T(2,128)(2,1)S(1)}, u32[]{:S(2)}, u32[]{:S(2)}) async-start(bf16[128,2,2816]{2,1,0:T(2,128)(2,1)} %bitcast.55), calls=%async_computation | async-start | bytes 2883584 | tf_op jit(solution)/shard_map/all_to_all | solution.py:432
  15.1 3.4 %collective-permute-start = (bf16[2,64]{1,0:T(2,128)(2,1)S(1)}, bf16[2,64]{1,0:T(2,128)(2,1)S(1)}, u32[]{:S(2)}, u32[]{:S(2)}) collective-permute-start(bf16[2,64]{1,0:T(2,128)(2,1)S(1)} %bitcast.61), channel_id=1, source_target_pairs={{0,64},{16,80},{32,96},{48,112},{64,0},{80,16},{96,32},{112,48},{1... | collective-permute-start | bytes 776 | tf_op jit(solution)/shard_map/ppermute | solution.py:451
  18.5 0.8 %pack_weights.1 = (bf16[4,176,128]{2,1,0:T(8,128)(2,1)S(1)}, bf16[4,176,128]{2,1,0:T(8,128)(2,1)S(1)}, bf16[4,176,128]{2,1,0:T(8,128)(2,1)S(1)}, bf16[4,176,128]{2,1,0:T(8,128)(2,1)S(1)}) custom-call(s32[1,64]{1,0:T(1,128)S(1)} %bitcast.50, bf16[2,64,2304]{2,1,0:T(8,128)(2,1)S(1)} %copy-done, bf16[2,64,512]{2,1,0:T(8,128)(2,1)S(1)} %copy-done.1), custom_call_target="tpu_custom_call" | custom-call | flops 46137344 | bytes 3145728 | tf_op jit(solution)/shard_map/pack_weights/pallas_call | solution.py:436
  19.3 0.6 collective-permute-done
  19.9 1.8 %collective-permute-start.3 = (bf16[4,176,128]{2,1,0:T(8,128)(2,1)S(1)}, bf16[4,176,128]{2,1,0:T(8,128)(2,1)S(1)}, u32[]{:S(2)}, u32[]{:S(2)}) collective-permute-start(bf16[4,176,128]{2,1,0:T(8,128)(2,1)S(1)} %get-tuple-element.30), channel_id=1, source_target_pairs={{0,1},{1,2},{2,3},{3,0},{4,5},{5,6},{6,7},{7,4},{8,9},{9,10},{10,1... | collective-permute-start | bytes 540680 | tf_op jit(solution)/shard_map/ppermute | solution.py:454
  21.7 6.5 %collective-permute-start.4 = (bf16[4,176,128]{2,1,0:T(8,128)(2,1)S(1)}, bf16[4,176,128]{2,1,0:T(8,128)(2,1)S(1)}, u32[]{:S(2)}, u32[]{:S(2)}) collective-permute-start(bf16[4,176,128]{2,1,0:T(8,128)(2,1)S(1)} %get-tuple-element.31), channel_id=1, source_target_pairs={{0,2},{1,3},{2,0},{3,1},{4,6},{5,7},{6,4},{7,5},{8,10},{9,11},{10,... | collective-permute-start | bytes 540680 | tf_op jit(solution)/shard_map/ppermute | solution.py:454
  28.2 9.7 %all-to-all-done = bf16[128,2,2816]{2,1,0:T(2,128)(2,1)S(1)} async-done(((bf16[128,2,2816]{2,1,0:T(2,128)(2,1)}), bf16[128,2,2816]{2,1,0:T(2,128)(2,1)S(1)}, u32[]{:S(2)}, u32[]{:S(2)}) %all-to-all-start) | async-done | bytes 1441824 | tf_op jit(solution)/shard_map/all_to_all | solution.py:432
  37.9 8.5 %polar.1 = (bf16[8,704,128]{2,1,0:T(8,128)(2,1)}, f32[4608,128]{1,0:T(8,128)}, f32[1024,128]{1,0:T(8,128)}) custom-call(s32[2,64]{1,0:T(2,128)S(1)} %bitcast.52, bf16[5632,128]{1,0:T(8,128)(2,1)S(1)} %bitcast.48, f32[4608,128]{1,0:T(8,128)} %bitcast.58, f32[1024,128]{1,0:T(8,128)S(1)} %bitcast.54), custom_call_target="tpu_custom_call" | custom-call | flops 4000000000 | bytes 8388608 | tf_op jit(solution)/shard_map/polar/pallas_call | solution.py:458
  46.4 4.9 %all-to-all-start.1 = ((bf16[8,704,128]{2,1,0:T(8,128)(2,1)}), bf16[8,704,128]{2,1,0:T(8,128)(2,1)S(1)}, u32[]{:S(2)}, u32[]{:S(2)}) async-start(bf16[8,704,128]{2,1,0:T(8,128)(2,1)} %get-tuple-element.33), calls=%async_computation.1 | async-start | bytes 2883584 | tf_op jit(solution)/shard_map/all_to_all | solution.py:485
  51.4 0.4 collective-permute-start.6
  51.8 2.5 %collective-permute-start.7 = (bf16[4,176,128]{2,1,0:T(8,128)(2,1)S(1)}, bf16[4,176,128]{2,1,0:T(8,128)(2,1)S(1)}, u32[]{:S(2)}, u32[]{:S(2)}) collective-permute-start(bf16[4,176,128]{2,1,0:T(8,128)(2,1)S(1)} %pad_maximum_fusion.2), channel_id=1, source_target_pairs={{0,8},{1,9},{2,10},{3,11},{4,12},{5,13},{6,14},{7,15},{8,0},{9,1},... | collective-permute-start | bytes 540680 | tf_op jit(solution)/shard_map/ppermute | solution.py:484
  54.4 1.1 %collective-permute-start.8 = (bf16[4,176,128]{2,1,0:T(8,128)(2,1)S(1)}, bf16[4,176,128]{2,1,0:T(8,128)(2,1)S(1)}, u32[]{:S(2)}, u32[]{:S(2)}) collective-permute-start(bf16[4,176,128]{2,1,0:T(8,128)(2,1)S(1)} %pad_maximum_fusion.3), channel_id=1, source_target_pairs={{0,12},{1,13},{2,14},{3,15},{4,0},{5,1},{6,2},{7,3},{8,4},{9,5},{1... | collective-permute-start | bytes 540680 | tf_op jit(solution)/shard_map/ppermute | solution.py:484
  55.5 0.8 %collective-permute-start.1 = (bf16[2,64]{1,0:T(2,128)(2,1)S(1)}, bf16[2,64]{1,0:T(2,128)(2,1)S(1)}, u32[]{:S(2)}, u32[]{:S(2)}) collective-permute-start(bf16[2,64]{1,0:T(2,128)(2,1)S(1)} %bitcast_maximum_fusion), channel_id=1, source_target_pairs={{0,16},{16,0},{32,48},{48,32},{64,80},{80,64},{96,112},{112,96},{1... | collective-permute-start | bytes 776 | tf_op jit(solution)/shard_map/ppermute | solution.py:451
  56.4 0.8 %collective-permute-done.1 = bf16[2,64]{1,0:T(2,128)(2,1)S(1)} collective-permute-done((bf16[2,64]{1,0:T(2,128)(2,1)S(1)}, bf16[2,64]{1,0:T(2,128)(2,1)S(1)}, u32[]{:S(2)}, u32[]{:S(2)}) %collective-permute-start.1) | collective-permute-done | bytes 288 | tf_op jit(solution)/shard_map/ppermute | solution.py:451
  57.2 2.0 %collective-permute-start.2 = (bf16[2,64]{1,0:T(2,128)(2,1)S(1)}, bf16[2,64]{1,0:T(2,128)(2,1)S(1)}, u32[]{:S(2)}, u32[]{:S(2)}) collective-permute-start(bf16[2,64]{1,0:T(2,128)(2,1)S(1)} %max.10), channel_id=1, source_target_pairs={{0,32},{16,48},{32,0},{48,16},{64,96},{80,112},{96,64},{112,80},{1... | collective-permute-start | bytes 776 | tf_op jit(solution)/shard_map/ppermute | solution.py:451
  59.2 9.9 %collective-permute-done.2 = bf16[2,64]{1,0:T(2,128)(2,1)S(1)} collective-permute-done((bf16[2,64]{1,0:T(2,128)(2,1)S(1)}, bf16[2,64]{1,0:T(2,128)(2,1)S(1)}, u32[]{:S(2)}, u32[]{:S(2)}) %collective-permute-start.2) | collective-permute-done | bytes 288 | tf_op jit(solution)/shard_map/ppermute | solution.py:451
  69.2 1.5 %all-to-all-done.1.polar_ref = bf16[8,704,128]{2,1,0:T(8,128)(2,1)S(1)} async-done(((bf16[8,704,128]{2,1,0:T(8,128)(2,1)}), bf16[8,704,128]{2,1,0:T(8,128)(2,1)S(1)}, u32[]{:S(2)}, u32[]{:S(2)}) %all-to-all-start.1) | async-done | bytes 1441824 | tf_op jit(solution)/shard_map/all_to_all | solution.py:485
  70.6 2.2 %finish.1 = (bf16[2304,128]{1,0:T(8,128)(2,1)}, bf16[512,128]{1,0:T(8,128)(2,1)}) custom-call(s32[2,64]{1,0:T(2,128)S(1)} %bitcast.53, s32[64]{0:T(128)S(1)} %copy-done.2, bf16[2,64]{1,0:T(2,128)(2,1)S(1)} %max.11.peak_ref, bf16[8,704,128]{2,1,0:T(8,128)(2,1)S(1)} %all-to-all-done.1.polar_ref, bf16[4,176,128]{2,1,0:T(8,128)(2,1)S(1)} %pad_maximum_fusion.rest_0_, ...), custom_call_target="tpu_custom_call" | custom-call | flops 10000000 | bytes 4194304 | tf_op jit(solution)/shard_map/finish/pallas_call | solution.py:489
  (23 shorter events, 0.2 us)
Async XLA Ops:
  3.5 11.6 %copy-start.5 = (bf16[1,2,64]{2,1,0:T(2,128)(2,1)S(1)}, bf16[1,2,64]{2,1,0:T(2,128)(2,1)}, u32[]{:S(2)}) copy-start(bf16[1,2,64]{2,1,0:T(2,128)(2,1)} %param.15) | copy-start | bytes 772
  3.5 14.9 %copy-start = (bf16[2,64,2304]{2,1,0:T(8,128)(2,1)S(1)}, bf16[2,64,2304]{2,1,0:T(8,128)(2,1)}, u32[]{:S(2)}) copy-start(bf16[2,64,2304]{2,1,0:T(8,128)(2,1)} %wq_ref.1) | copy-start | bytes 1769476
  3.6 14.9 %copy-start.1 = (bf16[2,64,512]{2,1,0:T(8,128)(2,1)S(1)}, bf16[2,64,512]{2,1,0:T(8,128)(2,1)}, u32[]{:S(2)}) copy-start(bf16[2,64,512]{2,1,0:T(8,128)(2,1)} %wk_ref.1) | copy-start | bytes 393220
  3.6 14.9 %copy-start.2 = (s32[64]{0:T(128)S(1)}, s32[64]{0:T(128)}, u32[]{:S(2)}) copy-start(s32[64]{0:T(128)} %head_ref.1) | copy-start | bytes 772
  3.6 34.3 %copy-start.3 = (s32[64,2,1]{0,2,1:T(1,128)S(1)}, s32[64,2,1]{0,2,1:T(1,128)}, u32[]{:S(2)}) copy-start(s32[64,2,1]{0,2,1:T(1,128)} %param.16) | copy-start | bytes 1540
  3.6 34.3 %copy-start.4 = (f32[2,65536]{1,0:T(2,128)S(1)}, f32[2,65536]{1,0:T(2,128)}, u32[]{:S(2)}) copy-start(f32[2,65536]{1,0:T(2,128)} %param.14) | copy-start | bytes 1572868
  3.6 34.2 %all-to-all-start = ((bf16[128,2,2816]{2,1,0:T(2,128)(2,1)}), bf16[128,2,2816]{2,1,0:T(2,128)(2,1)S(1)}, u32[]{:S(2)}, u32[]{:S(2)}) async-start(bf16[128,2,2816]{2,1,0:T(2,128)(2,1)} %bitcast.55), calls=%async_computation | async-start | bytes 2883584 | tf_op jit(solution)/shard_map/all_to_all | solution.py:432
  15.1 4.7 %collective-permute-start = (bf16[2,64]{1,0:T(2,128)(2,1)S(1)}, bf16[2,64]{1,0:T(2,128)(2,1)S(1)}, u32[]{:S(2)}, u32[]{:S(2)}) collective-permute-start(bf16[2,64]{1,0:T(2,128)(2,1)S(1)} %bitcast.61), channel_id=1, source_target_pairs={{0,64},{16,80},{32,96},{48,112},{64,0},{80,16},{96,32},{112,48},{1... | collective-permute-start | bytes 776 | tf_op jit(solution)/shard_map/ppermute | solution.py:451
  19.9 26.5 %collective-permute-start.3 = (bf16[4,176,128]{2,1,0:T(8,128)(2,1)S(1)}, bf16[4,176,128]{2,1,0:T(8,128)(2,1)S(1)}, u32[]{:S(2)}, u32[]{:S(2)}) collective-permute-start(bf16[4,176,128]{2,1,0:T(8,128)(2,1)S(1)} %get-tuple-element.30), channel_id=1, source_target_pairs={{0,1},{1,2},{2,3},{3,0},{4,5},{5,6},{6,7},{7,4},{8,9},{9,10},{10,1... | collective-permute-start | bytes 540680 | tf_op jit(solution)/shard_map/ppermute | solution.py:454
  21.7 24.7 %collective-permute-start.4 = (bf16[4,176,128]{2,1,0:T(8,128)(2,1)S(1)}, bf16[4,176,128]{2,1,0:T(8,128)(2,1)S(1)}, u32[]{:S(2)}, u32[]{:S(2)}) collective-permute-start(bf16[4,176,128]{2,1,0:T(8,128)(2,1)S(1)} %get-tuple-element.31), channel_id=1, source_target_pairs={{0,2},{1,3},{2,0},{3,1},{4,6},{5,7},{6,4},{7,5},{8,10},{9,11},{10,... | collective-permute-start | bytes 540680 | tf_op jit(solution)/shard_map/ppermute | solution.py:454
  28.2 18.2 %collective-permute-start.5 = (bf16[4,176,128]{2,1,0:T(8,128)(2,1)S(1)}, bf16[4,176,128]{2,1,0:T(8,128)(2,1)S(1)}, u32[]{:S(2)}, u32[]{:S(2)}) collective-permute-start(bf16[4,176,128]{2,1,0:T(8,128)(2,1)S(1)} %get-tuple-element.32), channel_id=1, source_target_pairs={{0,3},{1,0},{2,1},{3,2},{4,7},{5,4},{6,5},{7,6},{8,11},{9,8},{10,9... | collective-permute-start | bytes 540680 | tf_op jit(solution)/shard_map/ppermute | solution.py:454
  46.4 24.3 %all-to-all-start.1 = ((bf16[8,704,128]{2,1,0:T(8,128)(2,1)}), bf16[8,704,128]{2,1,0:T(8,128)(2,1)S(1)}, u32[]{:S(2)}, u32[]{:S(2)}) async-start(bf16[8,704,128]{2,1,0:T(8,128)(2,1)} %get-tuple-element.33), calls=%async_computation.1 | async-start | bytes 2883584 | tf_op jit(solution)/shard_map/all_to_all | solution.py:485
  51.4 17.7 %collective-permute-start.6 = (bf16[4,176,128]{2,1,0:T(8,128)(2,1)S(1)}, bf16[4,176,128]{2,1,0:T(8,128)(2,1)S(1)}, u32[]{:S(2)}, u32[]{:S(2)}) collective-permute-start(bf16[4,176,128]{2,1,0:T(8,128)(2,1)S(1)} %pad_maximum_fusion.1), channel_id=1, source_target_pairs={{0,4},{1,5},{2,6},{3,7},{4,8},{5,9},{6,10},{7,11},{8,12},{9,13},{1... | collective-permute-start | bytes 540680 | tf_op jit(solution)/shard_map/ppermute | solution.py:484
  51.8 17.3 %collective-permute-start.7 = (bf16[4,176,128]{2,1,0:T(8,128)(2,1)S(1)}, bf16[4,176,128]{2,1,0:T(8,128)(2,1)S(1)}, u32[]{:S(2)}, u32[]{:S(2)}) collective-permute-start(bf16[4,176,128]{2,1,0:T(8,128)(2,1)S(1)} %pad_maximum_fusion.2), channel_id=1, source_target_pairs={{0,8},{1,9},{2,10},{3,11},{4,12},{5,13},{6,14},{7,15},{8,0},{9,1},... | collective-permute-start | bytes 540680 | tf_op jit(solution)/shard_map/ppermute | solution.py:484
  54.4 14.8 %collective-permute-start.8 = (bf16[4,176,128]{2,1,0:T(8,128)(2,1)S(1)}, bf16[4,176,128]{2,1,0:T(8,128)(2,1)S(1)}, u32[]{:S(2)}, u32[]{:S(2)}) collective-permute-start(bf16[4,176,128]{2,1,0:T(8,128)(2,1)S(1)} %pad_maximum_fusion.3), channel_id=1, source_target_pairs={{0,12},{1,13},{2,14},{3,15},{4,0},{5,1},{6,2},{7,3},{8,4},{9,5},{1... | collective-permute-start | bytes 540680 | tf_op jit(solution)/shard_map/ppermute | solution.py:484
  55.5 1.7 %collective-permute-start.1 = (bf16[2,64]{1,0:T(2,128)(2,1)S(1)}, bf16[2,64]{1,0:T(2,128)(2,1)S(1)}, u32[]{:S(2)}, u32[]{:S(2)}) collective-permute-start(bf16[2,64]{1,0:T(2,128)(2,1)S(1)} %bitcast_maximum_fusion), channel_id=1, source_target_pairs={{0,16},{16,0},{32,48},{48,32},{64,80},{80,64},{96,112},{112,96},{1... | collective-permute-start | bytes 776 | tf_op jit(solution)/shard_map/ppermute | solution.py:451
  57.2 11.9 %collective-permute-start.2 = (bf16[2,64]{1,0:T(2,128)(2,1)S(1)}, bf16[2,64]{1,0:T(2,128)(2,1)S(1)}, u32[]{:S(2)}, u32[]{:S(2)}) collective-permute-start(bf16[2,64]{1,0:T(2,128)(2,1)S(1)} %max.10), channel_id=1, source_target_pairs={{0,32},{16,48},{32,0},{48,16},{64,96},{80,112},{96,64},{112,80},{1... | collective-permute-start | bytes 776 | tf_op jit(solution)/shard_map/ppermute | solution.py:451
